TPU v7x, 768 devices: a whole 4x8x12 slice. The times are simulated.
768 devices in a mesh: port: 24 (over x, z_hi, core), tm: 32 (over y, z_lo).
Axes of the slice: x: 4, y: 8, z: 12 (z_hi: 3, z_lo: 4; z = z_hi * 4 + z_lo), core: 2. Of those that a mesh axis runs over, the one named last changes fastest.
Arguments:
- query_rows: bfloat16 [1536, 64, 256], P('port', 'tm'), may hold values from -8 to 8
- key_rows: bfloat16 [1536, 64, 256], P('port', 'tm'), may hold values from -8 to 8
- value_rows: bfloat16 [1536, 64, 256], P('port', 'tm'), may hold values from -6 to 6
- out_grad: bfloat16 [1536, 64, 512], P('port', 'tm'), may hold values from -12 to 12
- out_weight: bfloat16 [256, 512], replicated, may hold values from -0.375 to 0.375
- adjacency: int32 [48, 48], P('port'), may hold values from 0 to 1, as said below
Outputs:
- query_grad: bfloat16 [1536, 64, 256], P('port', 'tm')
- key_grad: bfloat16 [1536, 64, 256], P('port', 'tm')
- value_grad: bfloat16 [1536, 64, 256], P('port', 'tm')
- weight_grad: float32 [256, 512], replicated
Inputs may be any that keep to these rules, and one draw needn't show every extreme that they name: `adjacency`: symmetric, with ones on the diagonal.
All inputs are finite; a program needn't handle non-finite values.
Results may differ from a plain program's by a relative error of at most 0.015.
Values may be sent and summed in bfloat16 or wider, within the bound.
No kernel may reach another device: no remote copies, remote signals or barrier semaphores. Data moves between devices by JAX's collectives and lax.ppermute only.
A program may use at most 64 MiB of HBM per device.

v0:
```python
import jax
import jax.numpy as jnp
from jax import lax
from jax.sharding import PartitionSpec as P

HEAD_DIM = 64
BLK = 32


score_scale = 0.125


def head_softmax(query_head, key_head, allowed):
    scores = (
        jnp.einsum("ihc,jhc->hij", query_head, key_head, preferred_element_type=jnp.float32)
        * score_scale
    )
    masked = jnp.where(allowed, scores, -1e30)
    row_max = jnp.max(masked, axis=2, keepdims=True)
    row_total = jnp.sum(jnp.where(allowed, jnp.exp(masked - row_max), 0.0), axis=2, keepdims=True)
    log_total = row_max + jnp.log(row_total)
    prob_rows = jnp.where(allowed, jnp.exp(masked - log_total), 0.0)
    return (prob_rows, log_total)


def per_device(query_rows, key_rows, value_rows, out_grad, out_weight, adjacency):
    port_dev, hour_dev, attn_width = query_rows.shape
    head_count = attn_width // HEAD_DIM
    hour_count = hour_dev * lax.axis_size("tm")
    allowed_rows = jnp.repeat(jnp.repeat(adjacency, BLK, axis=0), BLK, axis=1) == 1
    allowed = allowed_rows[None]
    out_delta = jnp.einsum(
        "ihm,am->iha", out_grad, out_weight, preferred_element_type=jnp.float32
    ).astype(jnp.bfloat16)
    key_all, value_all = (
        lax.all_gather(key_rows, "port", axis=0, tiled=True),
        lax.all_gather(value_rows, "port", axis=0, tiled=True),
    )
    prob_kept = []
    grad_kept = []
    attended_parts = []
    total_parts = []
    term_parts = []
    query_parts = []
    for head_index in range(head_count):
        begin_col = head_index * HEAD_DIM
        end_col = begin_col + HEAD_DIM
        delta_head = out_delta[:, :, begin_col:end_col]
        value_head = value_all[:, :, begin_col:end_col]
        key_head = key_all[:, :, begin_col:end_col]
        prob_rows, log_total = head_softmax(query_rows[:, :, begin_col:end_col], key_head, allowed)
        prob_low = prob_rows.astype(jnp.bfloat16)
        attended = jnp.einsum(
            "hij,jhc->ihc", prob_low, value_head, preferred_element_type=jnp.float32
        ).astype(jnp.bfloat16)
        row_term = jnp.sum(delta_head.astype(jnp.float32) * attended.astype(jnp.float32), axis=2)
        prob_grad = jnp.einsum(
            "ihc,jhc->hij", delta_head, value_head, preferred_element_type=jnp.float32
        )
        score_grad = (prob_rows * (prob_grad - row_term.T[:, :, None])).astype(jnp.bfloat16)
        query_parts.append(
            jnp.einsum("hij,jhc->ihc", score_grad, key_head, preferred_element_type=jnp.float32)
            * score_scale
        )
        attended_parts.append(attended)
        total_parts.append(log_total[:, :, 0].T)
        term_parts.append(row_term)
        prob_kept.append(prob_low)
        grad_kept.append(score_grad)
    attended_all = jnp.concatenate(attended_parts, axis=2)
    weight_term = jnp.einsum(
        "iha,ihm->am", attended_all, out_grad, preferred_element_type=jnp.float32
    )
    weight_grad = lax.psum(weight_term, ("port", "tm")) / hour_count
    query_grad = jnp.concatenate(query_parts, axis=2).astype(jnp.bfloat16)
    key_parts = []
    value_parts = []
    for head_index in range(head_count):
        begin_col = head_index * HEAD_DIM
        end_col = begin_col + HEAD_DIM
        grad_cols = grad_kept[head_index]
        prob_cols = prob_kept[head_index]
        key_parts.append(
            jnp.einsum(
                "hij,ihc->jhc",
                grad_cols,
                query_rows[:, :, begin_col:end_col],
                preferred_element_type=jnp.float32,
            )
            * score_scale
        )
        value_parts.append(
            jnp.einsum(
                "hij,ihc->jhc",
                prob_cols,
                out_delta[:, :, begin_col:end_col],
                preferred_element_type=jnp.float32,
            )
        )
    summed = lax.psum_scatter(
        jnp.concatenate(key_parts + value_parts, axis=2), "port", scatter_dimension=0, tiled=True
    )
    key_grad = summed[:, :, :attn_width].astype(jnp.bfloat16)
    value_grad = summed[:, :, attn_width:].astype(jnp.bfloat16)
    return (query_grad, key_grad, value_grad, weight_grad)


def solution(mesh):
    return jax.shard_map(
        per_device,
        mesh=mesh,
        in_specs=(
            P("port", "tm", None),
            P("port", "tm", None),
            P("port", "tm", None),
            P("port", "tm", None),
            P(),
            P("port", None),
        ),
        out_specs=(P("port", "tm", None), P("port", "tm", None), P("port", "tm", None), P()),
        check_vma=False,
    )
```

profile of v0, /device:TPU:1, one launch (start us, length us, event | category | flops | bytes accessed | tf_op | source)
XLA Modules:
  0.0 1002.9 jit_solution(15586612200681819311)
XLA Ops:
  7.2 0.0 copy-start
  7.2 0.0 all-gather.5.cloned.1.call-start
  7.2 0.7 all-gather.5.cloned.1.call-update
  7.9 0.0 all-gather.3.cloned.1.call-start
  8.0 0.7 all-gather.3.cloned.1.call-update
  8.7 0.0 all-reduce.4.cloned.1.call-start
  8.7 0.7 broadcast_compare_fusion
  9.4 0.1 copy.71
  9.5 0.1 broadcast_in_dim.78
  9.6 0.3 copy.72
  9.9 1.3 dynamic-slice
  11.8 1.6 fusion.86
  13.4 1.8 convolution_convert_fusion
  15.2 80.1 %all-gather.5.cloned.1.call-done = bf16[1536,2,256]{2,1,0:T(2,128)(2,1)} async-done(((bf16[64,2,256]{2,1,0:T(2,128)(2,1)}), bf16[1536,2,256]{2,1,0:T(2,128)(2,1)}) %all-gather.5.cloned.1.call-update) | async-done | bytes 1572880 | tf_op jit(solution)/shard_map/all_gather | solution.py:37
  95.2 5.1 fusion.83
  100.3 1.7 copy.116
  101.9 68.0 %all-gather.3.cloned.1.call-done = bf16[1536,2,256]{2,1,0:T(2,128)(2,1)} async-done(((bf16[64,2,256]{2,1,0:T(2,128)(2,1)}), bf16[1536,2,256]{2,1,0:T(2,128)(2,1)}) %all-gather.3.cloned.1.call-update) | async-done | bytes 1572880 | tf_op jit(solution)/shard_map/all_gather | solution.py:36
  169.9 5.0 fusion.84
  174.9 0.6 copy.115
  175.5 1.7 copy.110
  177.2 2.2 copy.109
  179.4 2.4 copy.106
  181.8 1.7 copy.112
  183.5 0.3 fusion.90
  183.8 1.1 fusion.88
  184.9 1.1 fusion.87
  186.0 1.4 fusion.89
  187.4 1.3 select_reduce_fusion.3
  188.7 2.9 copy.113
  191.6 2.9 copy.107
  194.5 0.0 copy-start.9
  194.6 0.8 log_add_fusion.3
  195.3 1.3 fusion.29
  196.7 0.7 log_add_fusion
  197.4 1.4 fusion.30
  198.8 1.4 fusion.31
  200.2 0.0 copy-start.15
  200.2 2.0 multiply_reduce_fusion.3
  202.3 1.1 fusion.20
  203.4 0.8 fusion.35
  204.2 1.2 fusion.9
  205.4 0.4 fusion.23
  205.8 0.9 fusion.32
  206.7 0.3 fusion.22
  207.0 0.9 fusion.33
  207.9 0.4 fusion.21
  208.3 0.9 fusion.34
  209.2 1.2 fusion.11
  210.4 1.2 fusion.13
  211.5 1.2 fusion.15
  212.8 1.3 fusion.19
  214.1 1.3 fusion.18
  215.4 1.3 fusion.17
  216.6 1.3 fusion.16
  217.9 10.2 %copy.94 = f32[1536,2,512]{2,1,0:T(2,128)} copy(f32[1536,2,512]{0,2,1:T(8,128)} %fusion.16) | data formatting | bytes 12582912 | tf_op jit(solution)/shard_map/concatenate | solution.py:101
  228.2 296.6 %all-reduce.5 = bf16[1536,2,512]{2,1,0:T(2,128)(2,1)S(1)} all-reduce(f32[1536,2,512]{2,1,0:T(2,128)} %copy.94), channel_id=2, replica_groups=mesh['port'=24,'tm'=32] {'port'}, use_global_device_ids=true, to_apply=%region_12.13.clone | all-reduce | flops 1572864 | bytes 9437184
  524.8 1.9 convolution_bitcast_fusion.4
  526.7 0.0 all-reduce.4.cloned.1.call-update
  526.7 0.1 dynamic-slice_convert_fusion
  526.8 0.9 pad_maximum_fusion
  527.8 0.7 copy.96
  528.5 0.7 fusion.85
  529.2 465.3 %all-reduce.4.cloned.1.call-done = f32[256,512]{1,0:T(8,128)} async-done(((f32[256,512]{1,0:T(8,128)}), f32[256,512]{1,0:T(8,128)}) %all-reduce.4.cloned.1.call-update) | async-done | bytes 524304 | tf_op jit(solution)/shard_map/psum | solution.py:74
  994.5 1.9 broadcast_multiply_fusion
  (39 shorter events, 0.1 us)
Async XLA Ops:
  7.2 6.2 copy-start
  7.2 88.0 %all-gather.5.cloned.1.call-start = ((), (), s32[]{:S(2)}) async-start(), calls=%async_computation.1 | async-start | bytes 1638400 | tf_op jit(solution)/shard_map/all_gather | solution.py:37
  7.9 162.0 %all-gather.3.cloned.1.call-start = ((), (), s32[]{:S(2)}) async-start(), calls=%async_computation | async-start | bytes 1638400 | tf_op jit(solution)/shard_map/all_gather | solution.py:36
  8.7 985.8 %all-reduce.4.cloned.1.call-start = ((), (), s32[]{:S(2)}) async-start(), calls=%async_computation.2 | async-start | bytes 1048576 | tf_op jit(solution)/shard_map/psum | solution.py:74
  175.5 8.3 copy-start.3
  179.4 6.6 copy-start.1
  181.8 4.3 copy-start.6
  194.5 7.7 copy-start.12
  194.5 8.8 copy-start.7
  194.5 9.7 copy-start.16
  194.5 10.9 %copy-start.8 = (bf16[64,2,256]{2,0,1:T(8,128)(2,1)S(1)}, bf16[64,2,256]{2,0,1:T(8,128)(2,1)}, u32[]{:S(2)}) copy-start(bf16[64,2,256]{2,0,1:T(8,128)(2,1)} %convolution_convert_fusion) | copy-start | bytes 196612
  194.5 10.9 %copy-start.9 = (bf16[1536,2,64]{0,2,1:T(8,128)(2,1)S(1)}, bf16[1536,2,64]{0,2,1:T(8,128)(2,1)}, u32[]{:S(2)}) copy-start(bf16[1536,2,64]{0,2,1:T(8,128)(2,1)} %copy.116) | copy-start | bytes 1179652
  194.6 11.3 %copy-start.4 = (bf16[1536,2,64]{0,2,1:T(8,128)(2,1)S(1)}, bf16[1536,2,64]{0,2,1:T(8,128)(2,1)}, u32[]{:S(2)}) copy-start(bf16[1536,2,64]{0,2,1:T(8,128)(2,1)} %copy-done.3) | copy-start | bytes 1179652
  194.6 12.1 %copy-start.11 = (bf16[1536,2,64]{0,2,1:T(8,128)(2,1)S(1)}, bf16[1536,2,64]{0,2,1:T(8,128)(2,1)}, u32[]{:S(2)}) copy-start(bf16[1536,2,64]{0,2,1:T(8,128)(2,1)} %copy.113) | copy-start | bytes 1179652
  196.7 3.5 copy-start.17
  197.4 9.6 copy-start.5
  198.8 3.5 copy-start.18
  198.8 9.1 copy-start.10
  200.2 2.1 copy-start.19
  200.2 8.1 copy-start.2
  200.2 9.0 copy-start.15
  202.2 8.1 copy-start.14
  228.2 296.6 %copy-start.13 = (bf16[64,2,512]{2,1,0:T(2,128)(2,1)S(1)}, bf16[64,2,512]{2,1,0:T(2,128)(2,1)}, u32[]{:S(2)}) copy-start(bf16[64,2,512]{2,1,0:T(2,128)(2,1)} %param.9) | copy-start | bytes 393220
Sparse Core Ops, SparseCore 0:
  12.0 83.1 all-gather.4
  99.2 70.6 all-gather.2
  526.9 467.5 all-reduce.3
where the time goes:
time: 1000 us
  waiting for transfers between devices  615 us (62%)
  blocking collectives  297 us (30%)
  local copies, waits for them, and re-layouts  41.2 us (4%)
  matrix products  29.2 us (3%)
  between operations  14.7 us (1%)
    psum x1, waiting for transfers between devices, per_device(): weight_grad = lax.psum(weight_term, ('port', 'tm')) / hour_count  465 us
    unnamed x1, blocking collectives  297 us
    all_gather x1, waiting for transfers between devices, per_device(): lax.all_gather(value_rows, 'port', axis=0, tiled=True)  80.1 us
    all_gather x1, waiting for transfers between devices, per_device(): lax.all_gather(key_rows, 'port', axis=0, tiled=True)  68 us
  transfers between devices with their start and end apart: 3, of which 3 were waited for; matrix products, arithmetic and copies ran while one was open for 1% of the time, Pallas kernels for 0%

commit v1 on v0

v1 whole, which is shorter than its diff:
```python
import functools

import jax
import jax.numpy as jnp
from jax import lax
from jax.experimental import pallas as pl
from jax.experimental.pallas import tpu as pltpu
from jax.sharding import Mesh, PartitionSpec as P

HEAD_DIM = 64
BLK = 32
LOG2E = 1.4426950408889634
BIG = 1e30
F32, BF16 = jnp.float32, jnp.bfloat16

PORT_AXES = ("x", "zh", "c")
TM_AXES = ("y", "zl")
NT = (((1,), (1,)), ((), ()))
NN = (((1,), (0,)), ((), ()))
TN = (((0,), (0,)), ((), ()))


def dot(a, b, dims):
    return lax.dot_general(a, b, dims, preferred_element_type=F32)


def low_half(rows):
    return lax.broadcasted_iota(jnp.int32, (rows, 128), 1) < HEAD_DIM


def swap(a):
    return jnp.concatenate([a[:, HEAD_DIM:], a[:, :HEAD_DIM]], axis=1)


def pack_kernel(parts, q_ref, k_ref, v_ref, g_ref, w_ref, adj_ref, out_ref):
    hours, ports, width = q_ref.shape
    bias = (adj_ref[...].astype(F32) - 1.0) * BIG
    low = low_half(ports)
    for h in range(hours):
        d = dot(g_ref[h], w_ref[...], NT)
        for t in range(width // 128):
            cols = slice(t * 128, (t + 1) * 128)
            q, k, v = (r[h, :, cols].astype(F32) for r in (q_ref, k_ref, v_ref))
            dd = d[:, cols]
            qs, ks, vs, ds = swap(q), swap(k), swap(v), swap(dd)
            for odd in range(2):
                n = 2 * t + odd
                top = jnp.where(low, qs, v) if odd else jnp.where(low, q, vs)
                bot = jnp.where(low, ks, dd) if odd else jnp.where(low, k, ds)
                for z in range(parts):
                    out_ref[n, z, h, :ports, :] = top.astype(BF16)
                    out_ref[n, z, h, ports : 2 * ports, :] = bot.astype(BF16)
                    out_ref[n, z, h, 2 * ports :, :] = bias.astype(BF16)


def attend_kernel(parts, rows, z_ref, r_ref, out_ref, qx, kx, dx, x1, x2, x1t, x2t, dkt, dvt):
    sources = r_ref.shape[0]
    ports = 64
    total = sources * ports
    own = total // parts
    pair = 2 * ports
    heads = own // pair
    zh = z_ref[0]
    lane = lax.broadcasted_iota(jnp.int32, (pair, 128), 1)
    row = lax.broadcasted_iota(jnp.int32, (pair, 128), 0)
    low = lane < HEAD_DIM
    for r in range(parts):
        z = lax.rem(zh + r, parts)
        for x in range(heads):
            at = r * own + x * pair
            group = x * parts + z
            src = r_ref.at[pl.ds(group * 2, 2)]
            a1 = src[:, :ports, :].reshape(pair, 128)
            a2 = src[:, ports : 2 * ports, :].reshape(pair, 128)
            m = src[:, 2 * ports : 2 * ports + 8, :].astype(F32)
            bias = jnp.concatenate(
                [jnp.broadcast_to(m[s, e : e + 1, :], (BLK, 128)) for s in range(2) for e in range(2)], axis=0
            )
            block = group * (pair // BLK) + lax.shift_right_logical(row, 5)
            hot = jnp.where(lane - HEAD_DIM == block, 1.0, 0.0)
            f1, f2 = a1.astype(F32), a2.astype(F32)
            sl = slice(at, at + pair)
            x1[sl, :] = a1
            x2[sl, :] = a2
            qx[sl, :] = jnp.where(low, f1, bias).astype(BF16)
            kx[sl, :] = jnp.where(low, f2, hot).astype(BF16)
            dx[sl, :] = jnp.where(low, 0.0, f2).astype(BF16)
            x1t[:, sl] = f1.T.astype(BF16)
            x2t[:, sl] = f2.T.astype(BF16)
    dkt[...] = jnp.zeros_like(dkt)
    dvt[...] = jnp.zeros_like(dvt)
    scale2 = 0.125 * LOG2E

    def step(at, is_own):
        s = dot(qx[pl.ds(at, rows), :], kx[...], NT)
        top = jnp.max(s, axis=1, keepdims=True)
        e = jnp.exp2((s - top) * scale2)
        inv = 1.0 / jnp.sum(e, axis=1, keepdims=True)
        p = e * inv
        p_low = p.astype(BF16)
        att = dot(p_low, x1[...], NN)
        d_rows = dx[pl.ds(at, rows), :]
        term = jnp.sum(d_rows.astype(F32) * att.astype(BF16).astype(F32), axis=1, keepdims=True)
        cols = total if is_own else own
        dp = dot(d_rows, x1[:cols, :], NT)
        ds = (p[:, :cols] * (dp - term)).astype(BF16)
        dkt[...] += dot(x1t[:, pl.ds(at, rows)], ds[:, :own], NN)
        dvt[...] += dot(x2t[:, pl.ds(at, rows)], p_low[:, :own], NN)
        if is_own:
            dq = dot(ds, x2[...], NN) * 0.125
            both = jnp.where(low_half(rows), dq, att).astype(BF16)
            for b in range(rows // ports):
                out_ref[at // ports + b, :ports, :] = both[b * ports : (b + 1) * ports, :]

    for b in range(own // rows):
        step(b * rows, True)

    def rest(b, carry):
        step(pl.multiple_of(own + b * rows, rows), False)
        return carry

    lax.fori_loop(0, (total - own) // rows, rest, 0)
    both = jnp.where(low_half(own), dkt[...].T * 0.125, dvt[...].T).astype(BF16)
    for b in range(own // ports):
        out_ref[b, ports : 2 * ports, :] = both[b * ports : (b + 1) * ports, :]


def unpack_kernel(t_ref, g_ref, q_ref, k_ref, v_ref, w_ref):
    hours, ports, width = q_ref.shape
    low = low_half(ports)
    att = []
    for h in range(hours):
        cols = []
        for t in range(width // 128):
            a = t_ref[2 * t, h, :ports, :].astype(F32)
            b = t_ref[2 * t + 1, h, :ports, :].astype(F32)
            c = t_ref[2 * t, h, ports:, :].astype(F32)
            d = t_ref[2 * t + 1, h, ports:, :].astype(F32)
            sl = slice(t * 128, (t + 1) * 128)
            q_ref[h, :, sl] = jnp.where(low, a, swap(b)).astype(BF16)
            k_ref[h, :, sl] = jnp.where(low, c, swap(d)).astype(BF16)
            v_ref[h, :, sl] = jnp.where(low, swap(c), d).astype(BF16)
            cols.append(jnp.where(low, swap(a), b))
        att.append(jnp.concatenate(cols, axis=1))
    whole = jnp.concatenate(att, axis=0).astype(BF16)
    g = g_ref[...].reshape(hours * ports, g_ref.shape[2])
    w_ref[...] = dot(whole, g, TN).astype(BF16)


def params():
    return pltpu.CompilerParams(vmem_limit_bytes=40 * 1024 * 1024)


def per_device(query_rows, key_rows, value_rows, out_grad, out_weight, adjacency):
    parts = lax.axis_size("zh")
    heads, hours = lax.axis_size("x"), lax.axis_size("c")
    port_count = lax.axis_size(PORT_AXES)
    tm_count = lax.axis_size(TM_AXES)
    ports, _, width = query_rows.shape
    q, k, v, g = (a.transpose(1, 0, 2) for a in (query_rows, key_rows, value_rows, out_grad))
    adj = jnp.pad(adjacency, ((0, 6), (HEAD_DIM, 128 - HEAD_DIM - adjacency.shape[1])))
    chunk = 2 * ports + 8
    send = pl.pallas_call(
        functools.partial(pack_kernel, parts),
        out_shape=jax.ShapeDtypeStruct((heads, parts, hours, chunk, 128), BF16),
        compiler_params=params(),
        name="pack",
    )(q, k, v, g, out_weight, adj)
    got = lax.all_to_all(send.reshape(port_count, chunk, 128), PORT_AXES, 0, 0, tiled=True)
    total = port_count * ports
    own = total // parts
    zh = lax.axis_index("zh").reshape(1)
    vec = pltpu.VMEM((total, 128), BF16)
    wide = pltpu.VMEM((128, total), BF16)
    acc = pltpu.VMEM((128, own), F32)
    back = pl.pallas_call(
        functools.partial(attend_kernel, parts, 256),
        out_shape=jax.ShapeDtypeStruct((heads * hours, 2 * ports, 128), BF16),
        in_specs=[pl.BlockSpec(memory_space=pltpu.SMEM), pl.BlockSpec(memory_space=pltpu.VMEM)],
        out_specs=pl.BlockSpec(memory_space=pltpu.VMEM),
        scratch_shapes=[vec] * 5 + [wide] * 2 + [acc] * 2,
        compiler_params=params(),
        name="attend",
    )(zh, got)
    mine = lax.all_to_all(back, ("x", "c"), 0, 0, tiled=True)
    grads = jax.ShapeDtypeStruct((hours, ports, width), BF16)
    dq, dk, dv, dw = pl.pallas_call(
        unpack_kernel,
        out_shape=(grads, grads, grads, jax.ShapeDtypeStruct((width, out_grad.shape[2]), BF16)),
        compiler_params=params(),
        name="unpack",
    )(mine.reshape(heads, hours, 2 * ports, 128), g)
    dq, dk, dv = (a.transpose(1, 0, 2) for a in (dq, dk, dv))
    rows = width // tm_count
    dw = dw.reshape(tm_count, rows, -1)
    dw = lax.all_to_all(dw, TM_AXES, 0, 0, tiled=True)
    dw = jnp.sum(dw.astype(F32), axis=0).astype(BF16)
    dw = lax.all_to_all(jnp.broadcast_to(dw, (port_count, *dw.shape)), PORT_AXES, 0, 0, tiled=True)
    dw = (jnp.sum(dw.astype(F32), axis=0) * (1.0 / (hours * tm_count))).astype(BF16)
    dw = lax.all_to_all(jnp.broadcast_to(dw, (tm_count, *dw.shape)), TM_AXES, 0, 0, tiled=True)
    return dq, dk, dv, dw.reshape(width, -1).astype(F32)


def solution(mesh):
    fine = Mesh(mesh.devices.reshape(4, 3, 2, 8, 4), PORT_AXES + TM_AXES)
    rows = P(PORT_AXES, TM_AXES, None)
    return jax.shard_map(
        per_device,
        mesh=fine,
        in_specs=(rows, rows, rows, rows, P(), P(PORT_AXES, None)),
        out_specs=(rows, rows, rows, P()),
        check_vma=False,
    )
```

time: 1000 us -> 132 us (0.13)
  waiting for transfers between devices: 615 us -> 38.2 us
  blocking collectives: 297 us -> 55 us
  local copies, waits for them, and re-layouts: 41.2 us -> 4.7 us
  matrix products: 29.2 us -> 0 us
  starting transfers between devices: 0.11 us -> 21.8 us
  between operations: 14.7 us -> 0.76 us
    psum x1 -> x0, waiting for transfers between devices: 465 us -> none  [per_device(): weight_grad = lax.psum(weight_term, ('port', 'tm')) / hour_count]
    unnamed x1 -> x0, blocking collectives: 297 us -> none
    all_gather x2 -> x0, waiting for transfers between devices: 148 us -> none  [the longest x1 80.1 us: per_device(): lax.all_gather(value_rows, 'port', axis=0, tiled=True)]
    all_to_all x0 -> x3, blocking collectives: none -> 55 us  [the longest x1 21.4 us: per_device(): dw = lax.all_to_all(dw, TM_AXES, 0, 0, tiled=True)]
    all_to_all x0 -> x2, waiting for transfers between devices: none -> 38.2 us  [the longest x1 28.9 us: per_device(): lax.all_to_all(send.reshape(port_count, chunk, 128), PORT_AXES, 0, 0, til...]
    dot_general x26 -> x0, matrix products: 29.2 us -> none  [the longest x4 6.1 us: per_device(): jnp.einsum('hij,jhc->ihc', prob_low, value_head, preferred_element_type=j...]
    all_to_all x0 -> x2, starting transfers between devices: none -> 21.8 us  [the longest x1 18 us: per_device(): lax.all_to_all(send.reshape(port_count, chunk, 128), PORT_AXES, 0, 0, til...]
    unnamed x50 -> x15, local copies, waits for them, and re-layouts: 18 us -> 3.88 us
  transfers between devices with their start and end apart: 3 -> 2, of which waited for: 3 -> 2; matrix products, arithmetic and copies ran while one was open for 1% -> 2% of each run, Pallas kernels for 0% -> 0%
where the time goes in v1:
time: 132 us; the launch traced here: 131 us
  blocking collectives  55 us (42%)
  waiting for transfers between devices  38.2 us (29%)
  starting transfers between devices  21.8 us (17%)
  Pallas kernels  9.94 us (8%)
  local copies, waits for them, and re-layouts  4.7 us (4%)
    all_to_all x1, waiting for transfers between devices, per_device(): lax.all_to_all(send.reshape(port_count, chunk, 128), PORT_AXES, 0, 0, til...  28.9 us
    all_to_all x1, blocking collectives, per_device(): dw = lax.all_to_all(dw, TM_AXES, 0, 0, tiled=True)  21.4 us
    all_to_all x1, blocking collectives, per_device(): lax.all_to_all(jnp.broadcast_to(dw, (port_count, *dw.shape)), PORT_AXES,...  21.4 us
    all_to_all x1, starting transfers between devices, per_device(): lax.all_to_all(send.reshape(port_count, chunk, 128), PORT_AXES, 0, 0, til...  18 us
    all_to_all x1, blocking collectives, per_device(): mine = lax.all_to_all(back, ('x', 'c'), 0, 0, tiled=True)  12.2 us
    all_to_all x1, waiting for transfers between devices, per_device(): lax.all_to_all(jnp.broadcast_to(dw, (tm_count, *dw.shape)), TM_AXES, 0, 0...  9.3 us
    pallas_call x1, Pallas kernels, per_device(): pl.pallas_call(functools.partial(attend_kernel, parts, 256), out_shape=ja...  8.35 us
    unnamed x15, local copies, waits for them, and re-layouts  3.88 us
  transfers between devices with their start and end apart: 2, of which 2 were waited for; matrix products, arithmetic and copies ran while one was open for 2% of the time, Pallas kernels for 0%

profile of v1, /device:TPU:1, one launch (start us, length us, event | category | flops | bytes accessed | tf_op | source)
XLA Modules:
  0.0 131.4 jit_solution(15796617702710717977)
XLA Ops:
  0.6 0.0 copy-start.1
  0.6 0.0 copy-start.2
  0.7 0.0 copy-start.3
  0.7 1.0 copy.28
  1.6 0.0 copy-done.1
  1.6 0.0 copy-start
  1.7 0.0 copy-done.2
  1.7 0.0 copy-done.3
  1.7 0.0 copy-start.4
  1.7 0.7 copy-done.4
  2.4 0.1 pad.4.adj_ref
  2.5 0.1 copy-done
  2.6 1.3 pack.1
  3.9 18.0 %all-to-all-start = ((bf16[24,136,128]{2,1,0:T(8,128)(2,1)}), bf16[24,136,128]{2,1,0:T(8,128)(2,1)S(1)}, u32[]{:S(2)}, u32[]{:S(2)}) async-start(bf16[24,136,128]{2,1,0:T(8,128)(2,1)} %bitcast.5), calls=%async_computation | async-start | bytes 1671168 | tf_op jit(solution)/shard_map/all_to_all | solution.py:169
  21.8 28.9 %all-to-all-done.r_ref = bf16[24,136,128]{2,1,0:T(8,128)(2,1)S(1)} async-done(((bf16[24,136,128]{2,1,0:T(8,128)(2,1)}), bf16[24,136,128]{2,1,0:T(8,128)(2,1)S(1)}, u32[]{:S(2)}, u32[]{:S(2)}) %all-to-all-start) | async-done | bytes 835616 | tf_op jit(solution)/shard_map/all_to_all | solution.py:169
  50.8 8.4 %attend.1 = bf16[8,128,128]{2,1,0:T(8,128)(2,1)S(1)} custom-call(s32[1]{0:T(128)} %bitcast.z_ref, bf16[24,136,128]{2,1,0:T(8,128)(2,1)S(1)} %all-to-all-done.r_ref), custom_call_target="tpu_custom_call" | custom-call | tf_op jit(solution)/shard_map/attend/pallas_call | solution.py:176
  59.1 12.2 %all_to_all.25 = bf16[8,128,128]{2,1,0:T(8,128)(2,1)S(1)} all-to-all(bf16[8,128,128]{2,1,0:T(8,128)(2,1)S(1)} %attend.1), channel_id=1, replica_groups=mesh['x'=4,'zh'=3,'c'=2,'y'=8,'zl'=4] {'x','c'}, dimensions={0} | all-to-all | bytes 524288 | tf_op jit(solution)/shard_map/all_to_all | solution.py:185
  71.4 0.3 unpack.1
  71.7 21.4 %all_to_all.26 = bf16[32,8,512]{2,1,0:T(8,128)(2,1)S(1)} all-to-all(bf16[32,8,512]{2,1,0:T(8,128)(2,1)S(1)} %bitcast.24), channel_id=1, replica_groups=mesh['x'=4,'zh'=3,'c'=2,'y'=8,'zl'=4] {'y','zl'}, dimensions={0} | all-to-all | bytes 524288 | tf_op jit(solution)/shard_map/all_to_all | solution.py:196
  93.1 0.1 reduce_sum.21
  93.2 21.4 %all_to_all.27 = bf16[24,8,512]{2,1,0:T(8,128)(2,1)S(1)} all-to-all(bf16[24,8,512]{2,1,0:T(8,128)(2,1)S(1)} %broadcast_in_dim.6), channel_id=1, replica_groups=mesh['x'=4,'zh'=3,'c'=2,'y'=8,'zl'=4] {'x','zh','c'}, dimensions={0} | all-to-all | bytes 393216 | tf_op jit(solution)/shard_map/all_to_all | solution.py:198
  114.6 0.7 broadcast_in_dim.7
  115.3 3.9 %all-to-all-start.4 = ((bf16[32,8,512]{2,1,0:T(8,128)(2,1)}), bf16[32,8,512]{2,1,0:T(8,128)(2,1)S(1)}, u32[]{:S(2)}, u32[]{:S(2)}) async-start(bf16[32,8,512]{2,1,0:T(8,128)(2,1)} %broadcast_in_dim.7), calls=%async_computation.4 | async-start | bytes 524288 | tf_op jit(solution)/shard_map/all_to_all | solution.py:200
  119.2 0.7 copy.21
  119.9 0.7 copy.22
  120.6 0.7 copy.23
  121.3 9.3 %all-to-all-done.4 = bf16[32,8,512]{2,1,0:T(8,128)(2,1)S(1)} async-done(((bf16[32,8,512]{2,1,0:T(8,128)(2,1)}), bf16[32,8,512]{2,1,0:T(8,128)(2,1)S(1)}, u32[]{:S(2)}, u32[]{:S(2)}) %all-to-all-start.4) | async-done | bytes 262176 | tf_op jit(solution)/shard_map/all_to_all | solution.py:200
  130.6 0.9 bitcast_convert_fusion
  (5 shorter events, 0.1 us)
Async XLA Ops:
  0.6 1.0 copy-start.1
  0.6 1.0 copy-start.2
  0.7 1.0 copy-start.3
  1.6 1.0 copy-start
  1.7 0.7 copy-start.4
  3.9 46.9 %all-to-all-start = ((bf16[24,136,128]{2,1,0:T(8,128)(2,1)}), bf16[24,136,128]{2,1,0:T(8,128)(2,1)S(1)}, u32[]{:S(2)}, u32[]{:S(2)}) async-start(bf16[24,136,128]{2,1,0:T(8,128)(2,1)} %bitcast.5), calls=%async_computation | async-start | bytes 1671168 | tf_op jit(solution)/shard_map/all_to_all | solution.py:169
  115.3 15.3 %all-to-all-start.4 = ((bf16[32,8,512]{2,1,0:T(8,128)(2,1)}), bf16[32,8,512]{2,1,0:T(8,128)(2,1)S(1)}, u32[]{:S(2)}, u32[]{:S(2)}) async-start(bf16[32,8,512]{2,1,0:T(8,128)(2,1)} %broadcast_in_dim.7), calls=%async_computation.4 | async-start | bytes 524288 | tf_op jit(solution)/shard_map/all_to_all | solution.py:200

commit v2 on v1

--- a/solution.py
+++ b/solution.py
@@ -8,6 +8,7 @@
 from jax.sharding import Mesh, PartitionSpec as P
 
 HEAD_DIM = 64
+HALF = HEAD_DIM // 2
 BLK = 32
 LOG2E = 1.4426950408889634
 BIG = 1e30
@@ -108,18 +109,19 @@
         dvt[...] += dot(x2t[:, pl.ds(at, rows)], p_low[:, :own], NN)
         if is_own:
             dq = dot(ds, x2[...], NN) * 0.125
-            both = jnp.where(low_half(rows), dq, att).astype(BF16)
-            for b in range(rows // ports):
-                out_ref[at // ports + b, :ports, :] = both[b * ports : (b + 1) * ports, :]
+            for b in range(0, rows, pair):
+                one, two = att[b : b + ports], att[b + ports : b + pair]
+                for c in range(2):
+                    sl = slice(HEAD_DIM + c * HALF, HEAD_DIM + (c + 1) * HALF)
+                    first = dq[b + c * ports : b + (c + 1) * ports, :HEAD_DIM]
+                    both = jnp.concatenate([first, one[:, sl], two[:, sl]], axis=1)
+                    out_ref[(at + b) // ports + c, :ports, :] = both.astype(BF16)
 
     for b in range(own // rows):
         step(b * rows, True)
 
-    def rest(b, carry):
-        step(pl.multiple_of(own + b * rows, rows), False)
-        return carry
-
-    lax.fori_loop(0, (total - own) // rows, rest, 0)
+    for b in range((total - own) // rows):
+        step(own + b * rows, False)
     both = jnp.where(low_half(own), dkt[...].T * 0.125, dvt[...].T).astype(BF16)
     for b in range(own // ports):
         out_ref[b, ports : 2 * ports, :] = both[b * ports : (b + 1) * ports, :]
@@ -127,10 +129,10 @@
 
 def unpack_kernel(t_ref, g_ref, q_ref, k_ref, v_ref, w_ref):
     hours, ports, width = q_ref.shape
+    cores, model = g_ref.shape[0], g_ref.shape[3]
+    heads = t_ref.shape[0]
     low = low_half(ports)
-    att = []
     for h in range(hours):
-        cols = []
         for t in range(width // 128):
             a = t_ref[2 * t, h, :ports, :].astype(F32)
             b = t_ref[2 * t + 1, h, :ports, :].astype(F32)
@@ -140,11 +142,27 @@
             q_ref[h, :, sl] = jnp.where(low, a, swap(b)).astype(BF16)
             k_ref[h, :, sl] = jnp.where(low, c, swap(d)).astype(BF16)
             v_ref[h, :, sl] = jnp.where(low, swap(c), d).astype(BF16)
-            cols.append(jnp.where(low, swap(a), b))
-        att.append(jnp.concatenate(cols, axis=1))
-    whole = jnp.concatenate(att, axis=0).astype(BF16)
-    g = g_ref[...].reshape(hours * ports, g_ref.shape[2])
-    w_ref[...] = dot(whole, g, TN).astype(BF16)
+    dw = None
+    for core in range(cores):
+        sl = slice(HEAD_DIM + core * HALF, HEAD_DIM + (core + 1) * HALF)
+        att = jnp.concatenate(
+            [
+                jnp.concatenate([t_ref[n, h, :ports, :].astype(F32)[:, sl] for n in range(heads)], axis=1)
+                for h in range(hours)
+            ],
+            axis=0,
+        ).astype(BF16)
+        part = dot(att, g_ref[core].reshape(hours * ports, model), TN)
+        dw = part if dw is None else dw + part
+    dw = dw.astype(BF16)
+    wide = model // 128
+    for r in range(dw.shape[0] // 8):
+        for c in range(wide):
+            w_ref[r * wide + c] = dw[r * 8 : (r + 1) * 8, c * 128 : (c + 1) * 128]
+
+
+def exchange(a, axes):
+    return lax.all_to_all(a, axes, 0, 0, tiled=True)
 
 
 def params():
@@ -166,7 +184,7 @@
         compiler_params=params(),
         name="pack",
     )(q, k, v, g, out_weight, adj)
-    got = lax.all_to_all(send.reshape(port_count, chunk, 128), PORT_AXES, 0, 0, tiled=True)
+    got = exchange(send.reshape(port_count, chunk, 128), PORT_AXES)
     total = port_count * ports
     own = total // parts
     zh = lax.axis_index("zh").reshape(1)
@@ -182,23 +200,26 @@
         compiler_params=params(),
         name="attend",
     )(zh, got)
-    mine = lax.all_to_all(back, ("x", "c"), 0, 0, tiled=True)
+    mine = exchange(back, ("x", "c"))
     grads = jax.ShapeDtypeStruct((hours, ports, width), BF16)
+    half = heads * HALF
+    wide = out_grad.shape[2] // 128
+    tiles = half // 8 * wide
     dq, dk, dv, dw = pl.pallas_call(
         unpack_kernel,
-        out_shape=(grads, grads, grads, jax.ShapeDtypeStruct((width, out_grad.shape[2]), BF16)),
+        out_shape=(grads, grads, grads, jax.ShapeDtypeStruct((tiles, 8, 128), BF16)),
         compiler_params=params(),
         name="unpack",
-    )(mine.reshape(heads, hours, 2 * ports, 128), g)
+    )(mine.reshape(heads, hours, 2 * ports, 128), lax.all_gather(g, "c"))
     dq, dk, dv = (a.transpose(1, 0, 2) for a in (dq, dk, dv))
-    rows = width // tm_count
-    dw = dw.reshape(tm_count, rows, -1)
-    dw = lax.all_to_all(dw, TM_AXES, 0, 0, tiled=True)
+    dw = exchange(dw, TM_AXES).reshape(tm_count, -1, 8, 128)
     dw = jnp.sum(dw.astype(F32), axis=0).astype(BF16)
-    dw = lax.all_to_all(jnp.broadcast_to(dw, (port_count, *dw.shape)), PORT_AXES, 0, 0, tiled=True)
+    dw = exchange(jnp.broadcast_to(dw, (heads * parts, *dw.shape)), ("x", "zh"))
     dw = (jnp.sum(dw.astype(F32), axis=0) * (1.0 / (hours * tm_count))).astype(BF16)
-    dw = lax.all_to_all(jnp.broadcast_to(dw, (tm_count, *dw.shape)), TM_AXES, 0, 0, tiled=True)
-    return dq, dk, dv, dw.reshape(width, -1).astype(F32)
+    dw = exchange(jnp.broadcast_to(dw, (tm_count, *dw.shape)), TM_AXES)
+    dw = lax.all_gather(dw, "c").reshape(2, heads, HALF // 8, wide, 8, 128)
+    dw = dw.transpose(1, 0, 2, 4, 3, 5).reshape(width, -1).astype(F32)
+    return dq, dk, dv, dw
 
 
 def solution(mesh):

time: 132 us -> 129 us (0.977)
  blocking collectives: 55 us -> 42.2 us
  starting transfers between devices: 21.8 us -> 28.3 us
  waiting for transfers between devices: 38.2 us -> 41.3 us
    all_to_all x3 -> x2, blocking collectives: 55 us -> 33.7 us  [exchange(): return lax.all_to_all(a, axes, 0, 0, tiled=True)]
    all_gather x0 -> x2, blocking collectives: none -> 8.57 us  [the longest x1 6.59 us: per_device(): dw = lax.all_gather(dw, 'c').reshape(2, heads, HALF // 8, wide, 8, 128)]
    all_to_all x2 -> x3, starting transfers between devices: 21.8 us -> 28.3 us  [exchange(): return lax.all_to_all(a, axes, 0, 0, tiled=True)]
    all_to_all x2 -> x3, waiting for transfers between devices: 38.2 us -> 41.3 us  [exchange(): return lax.all_to_all(a, axes, 0, 0, tiled=True)]
  transfers between devices with their start and end apart: 2 -> 3, of which waited for: 2 -> 3; matrix products, arithmetic and copies ran while one was open for 2% -> 2% of each run, Pallas kernels for 0% -> 0%
where the time goes in v2:
time: 129 us; the launch traced here: 128 us
  blocking collectives  42.2 us (33%)
  waiting for transfers between devices  41.3 us (32%)
  starting transfers between devices  28.3 us (22%)
  Pallas kernels  10.1 us (8%)
  local copies, waits for them, and re-layouts  5.49 us (4%)
    all_to_all x3, waiting for transfers between devices, exchange(): return lax.all_to_all(a, axes, 0, 0, tiled=True)  41.3 us
    all_to_all x2, blocking collectives, exchange(): return lax.all_to_all(a, axes, 0, 0, tiled=True)  33.7 us
    all_to_all x3, starting transfers between devices, exchange(): return lax.all_to_all(a, axes, 0, 0, tiled=True)  28.3 us
    pallas_call x1, Pallas kernels, per_device(): pl.pallas_call(functools.partial(attend_kernel, parts, 256), out_shape=ja...  8.47 us
    all_gather x1, blocking collectives, per_device(): dw = lax.all_gather(dw, 'c').reshape(2, heads, HALF // 8, wide, 8, 128)  6.59 us
    unnamed x15, local copies, waits for them, and re-layouts  3.88 us
  transfers between devices with their start and end apart: 3, of which 3 were waited for; matrix products, arithmetic and copies ran while one was open for 2% of the time, Pallas kernels for 0%

profile of v2, /device:TPU:1, one launch (start us, length us, event | category | flops | bytes accessed | tf_op | source)
XLA Modules:
  0.0 128.3 jit_solution(2169707837603137823)
XLA Ops:
  0.6 0.0 copy-start.1
  0.6 0.0 copy-start.2
  0.7 0.0 copy-start.3
  0.7 1.0 copy.52
  1.6 0.0 copy-done.1
  1.6 0.0 copy-start
  1.7 0.0 copy-done.2
  1.7 0.0 copy-done.3
  1.7 0.0 copy-start.4
  1.7 0.7 copy-done.4
  2.4 0.1 pad.4.adj_ref
  2.5 0.1 copy-done
  2.6 1.3 pack.1
  3.8 18.0 %all-to-all-start = ((bf16[24,136,128]{2,1,0:T(8,128)(2,1)}), bf16[24,136,128]{2,1,0:T(8,128)(2,1)S(1)}, u32[]{:S(2)}, u32[]{:S(2)}) async-start(bf16[24,136,128]{2,1,0:T(8,128)(2,1)} %bitcast.5), calls=%async_computation | async-start | bytes 1671168 | tf_op jit(solution)/shard_map/all_to_all | solution.py:165
  21.8 28.9 %all-to-all-done.r_ref = bf16[24,136,128]{2,1,0:T(8,128)(2,1)S(1)} async-done(((bf16[24,136,128]{2,1,0:T(8,128)(2,1)}), bf16[24,136,128]{2,1,0:T(8,128)(2,1)S(1)}, u32[]{:S(2)}, u32[]{:S(2)}) %all-to-all-start) | async-done | bytes 835616 | tf_op jit(solution)/shard_map/all_to_all | solution.py:165
  50.8 8.5 %attend.1 = bf16[8,128,128]{2,1,0:T(8,128)(2,1)} custom-call(s32[1]{0:T(128)} %bitcast.z_ref, bf16[24,136,128]{2,1,0:T(8,128)(2,1)S(1)} %all-to-all-done.r_ref), custom_call_target="tpu_custom_call" | custom-call | tf_op jit(solution)/shard_map/attend/pallas_call | solution.py:194
  59.2 6.5 %all-to-all-start.1 = ((bf16[8,128,128]{2,1,0:T(8,128)(2,1)}), bf16[8,128,128]{2,1,0:T(8,128)(2,1)S(1)}, u32[]{:S(2)}, u32[]{:S(2)}) async-start(bf16[8,128,128]{2,1,0:T(8,128)(2,1)} %attend.1), calls=%async_computation.1 | async-start | bytes 524288 | tf_op jit(solution)/shard_map/all_to_all | solution.py:165
  65.7 2.0 %all-gather = bf16[4,64,512]{2,1,0:T(8,128)(2,1)S(1)} all-gather(bf16[2,64,512]{2,1,0:T(8,128)(2,1)S(1)} %bitcast.24), channel_id=2, replica_groups=mesh['x'=4,'zh'=3,'c'=2,'y'=8,'zl'=4] {'c'}, dimensions={0}, use_global_device_ids=true | all-gather | bytes 393216 | tf_op jit(solution)/shard_map/all_gather | solution.py:213
  67.7 4.5 %all-to-all-done.1 = bf16[8,128,128]{2,1,0:T(8,128)(2,1)S(1)} async-done(((bf16[8,128,128]{2,1,0:T(8,128)(2,1)}), bf16[8,128,128]{2,1,0:T(8,128)(2,1)S(1)}, u32[]{:S(2)}, u32[]{:S(2)}) %all-to-all-start.1) | async-done | bytes 262176 | tf_op jit(solution)/shard_map/all_to_all | solution.py:165
  72.2 0.3 unpack.1
  72.6 20.5 %all_to_all.25 = bf16[64,8,128]{2,1,0:T(8,128)(2,1)S(1)} all-to-all(bf16[64,8,128]{2,1,0:T(8,128)(2,1)S(1)} %get-tuple-element.11), channel_id=1, replica_groups=mesh['x'=4,'zh'=3,'c'=2,'y'=8,'zl'=4] {'y','zl'}, dimensions={0} | all-to-all | bytes 262144 | tf_op jit(solution)/shard_map/all_to_all | solution.py:165
  93.1 13.2 %all_to_all.26 = bf16[12,2,8,128]{3,2,1,0:T(8,128)(2,1)S(1)} all-to-all(bf16[12,2,8,128]{3,2,1,0:T(8,128)(2,1)S(1)} %broadcast_in_dim.6), channel_id=1, replica_groups=mesh['x'=4,'zh'=3,'c'=2,'y'=8,'zl'=4] {'x','zh'}, dimensions={0} | all-to-all | bytes 98304 | tf_op jit(solution)/shard_map/all_to_all | solution.py:165
  106.3 0.7 broadcast_in_dim.7
  107.0 3.9 %all-to-all-start.4 = ((bf16[32,2,8,128]{3,2,1,0:T(8,128)(2,1)}), bf16[32,2,8,128]{3,2,1,0:T(8,128)(2,1)S(1)}, u32[]{:S(2)}, u32[]{:S(2)}) async-start(bf16[32,2,8,128]{3,2,1,0:T(8,128)(2,1)} %broadcast_in_dim.7), calls=%async_computation.4 | async-start | bytes 262144 | tf_op jit(solution)/shard_map/all_to_all | solution.py:165
  110.9 0.7 copy.45
  111.6 0.7 copy.46
  112.3 0.7 copy.47
  113.0 7.8 %all-to-all-done.4 = bf16[32,2,8,128]{3,2,1,0:T(8,128)(2,1)S(1)} async-done(((bf16[32,2,8,128]{3,2,1,0:T(8,128)(2,1)}), bf16[32,2,8,128]{3,2,1,0:T(8,128)(2,1)S(1)}, u32[]{:S(2)}, u32[]{:S(2)}) %all-to-all-start.4) | async-done | bytes 131104 | tf_op jit(solution)/shard_map/all_to_all | solution.py:165
  120.8 6.6 %all-gather.1 = bf16[64,2,8,128]{3,2,1,0:T(8,128)(2,1)S(1)} all-gather(bf16[32,2,8,128]{3,2,1,0:T(8,128)(2,1)S(1)} %all-to-all-done.4), channel_id=3, replica_groups=mesh['x'=4,'zh'=3,'c'=2,'y'=8,'zl'=4] {'c'}, dimensions={0}, use_global_device_ids=true | all-gather | bytes 393216 | tf_op jit(solution)/shard_map/all_gather | solution.py:220
  127.4 0.8 copy.44
  (7 shorter events, 0.1 us)
Async XLA Ops:
  0.6 1.0 copy-start.1
  0.6 1.0 copy-start.2
  0.7 1.0 copy-start.3
  1.6 1.0 copy-start
  1.7 0.7 copy-start.4
  3.8 46.9 %all-to-all-start = ((bf16[24,136,128]{2,1,0:T(8,128)(2,1)}), bf16[24,136,128]{2,1,0:T(8,128)(2,1)S(1)}, u32[]{:S(2)}, u32[]{:S(2)}) async-start(bf16[24,136,128]{2,1,0:T(8,128)(2,1)} %bitcast.5), calls=%async_computation | async-start | bytes 1671168 | tf_op jit(solution)/shard_map/all_to_all | solution.py:165
  59.2 13.0 %all-to-all-start.1 = ((bf16[8,128,128]{2,1,0:T(8,128)(2,1)}), bf16[8,128,128]{2,1,0:T(8,128)(2,1)S(1)}, u32[]{:S(2)}, u32[]{:S(2)}) async-start(bf16[8,128,128]{2,1,0:T(8,128)(2,1)} %attend.1), calls=%async_computation.1 | async-start | bytes 524288 | tf_op jit(solution)/shard_map/all_to_all | solution.py:165
  107.0 13.8 %all-to-all-start.4 = ((bf16[32,2,8,128]{3,2,1,0:T(8,128)(2,1)}), bf16[32,2,8,128]{3,2,1,0:T(8,128)(2,1)S(1)}, u32[]{:S(2)}, u32[]{:S(2)}) async-start(bf16[32,2,8,128]{3,2,1,0:T(8,128)(2,1)} %broadcast_in_dim.7), calls=%async_computation.4 | async-start | bytes 262144 | tf_op jit(solution)/shard_map/all_to_all | solution.py:165

commit v3 on v1

v3 whole, which is shorter than its diff:
```python
import functools

import jax
import jax.numpy as jnp
from jax import lax
from jax.experimental import pallas as pl
from jax.experimental.pallas import tpu as pltpu
from jax.sharding import Mesh, PartitionSpec as P

HEAD_DIM = 64
BLK = 32
LANES = 128
LOG2E = 1.4426950408889634
BIG = 1e30
F32, BF16 = jnp.float32, jnp.bfloat16

PORT_AXES = ("x", "zh", "c")
TM_AXES = ("y", "zl")
NT = (((1,), (1,)), ((), ()))
NN = (((1,), (0,)), ((), ()))
TN = (((0,), (0,)), ((), ()))


def dot(a, b, dims):
    return lax.dot_general(a, b, dims, preferred_element_type=F32)


def low_half(rows):
    return lax.broadcasted_iota(jnp.int32, (rows, LANES), 1) < HEAD_DIM


def swap(a):
    return jnp.concatenate([a[:, HEAD_DIM:], a[:, :HEAD_DIM]], axis=1)


def pack_kv_kernel(k_ref, v_ref, out_ref):
    hours, ports, width = k_ref.shape
    low = low_half(ports)
    for h in range(hours):
        for t in range(width // LANES):
            cols = slice(t * LANES, (t + 1) * LANES)
            k, v = k_ref[h, :, cols].astype(F32), v_ref[h, :, cols].astype(F32)
            out_ref[2 * t, h] = jnp.where(low, k, swap(v)).astype(BF16)
            out_ref[2 * t + 1, h] = jnp.where(low, swap(k), v).astype(BF16)


def pack_qg_kernel(q_ref, g_ref, adj_ref, out_ref):
    hours, ports, width = q_ref.shape
    low = low_half(ports)
    bias = (adj_ref[...].astype(F32) - 1.0) * BIG
    bias = jnp.concatenate(
        [jnp.broadcast_to(bias[b : b + 1, :], (BLK, LANES)) for b in range(ports // BLK)], axis=0
    )
    for h in range(hours):
        for t in range(width // LANES):
            q = q_ref[h, :, t * LANES : (t + 1) * LANES].astype(F32)
            out_ref[2 * t, h, :, :LANES] = jnp.where(low, q, bias).astype(BF16)
            out_ref[2 * t + 1, h, :, :LANES] = jnp.where(low, swap(q), bias).astype(BF16)
        for n in range(out_ref.shape[0]):
            out_ref[n, h, :, LANES:] = g_ref[h]


def attend_kernel(
    rows, z_ref, kv0_ref, kv1_ref, kv2_ref, qg_ref, w_ref, d0_ref, d1_ref, d2_ref, dq_ref, dw_ref, kx, kv, dkt, dvt
):
    group, ports, _ = kv0_ref.shape
    own = group * ports
    total = 3 * own
    lane = lax.broadcasted_iota(jnp.int32, (own, LANES), 1)
    row = lax.broadcasted_iota(jnp.int32, (own, LANES), 0)
    for r, ref in enumerate((kv0_ref, kv1_ref, kv2_ref)):
        z = lax.rem(z_ref[0] + r, 3)
        part = ref[...].reshape(own, LANES)
        pair = lax.shift_right_logical(row, 7)
        block = (pair * 3 + z) * 4 + lax.bitwise_and(lax.shift_right_logical(row, 5), 3)
        hot = jnp.where(lane - HEAD_DIM == block, 1.0, 0.0)
        sl = slice(r * own, (r + 1) * own)
        kv[sl, :] = part
        kx[sl, :] = jnp.where(lane < HEAD_DIM, part.astype(F32), hot).astype(BF16)
    w_n = jnp.concatenate([jnp.zeros_like(w_ref), w_ref[...]], axis=0)
    scale2 = 0.125 * LOG2E
    low = low_half(rows)
    per = rows // ports
    dw = None
    for b in range(own // rows):
        mine = qg_ref[b * per : (b + 1) * per]
        qx = mine[:, :, :LANES].reshape(rows, LANES)
        g = mine[:, :, LANES:].reshape(rows, -1)
        d = dot(g, w_n, NT).astype(BF16)
        s = dot(qx, kx[...], NT)
        top = jnp.max(s, axis=1, keepdims=True)
        e = jnp.exp2((s - top) * scale2)
        p = e * (1.0 / jnp.sum(e, axis=1, keepdims=True))
        p_low = p.astype(BF16)
        att = dot(p_low, kv[...], NN).astype(BF16)
        part = dot(att, g, TN)
        dw = part if dw is None else dw + part
        d32 = d.astype(F32)
        term = jnp.sum(d32 * att.astype(F32), axis=1, keepdims=True)
        dp = dot(d, kv[...], NT)
        ds = (p * (dp - term)).astype(BF16)
        dq = dot(ds, kv[...], NN) * 0.125
        qdt = jnp.where(low, qx.astype(F32), d32).T.astype(BF16)
        dk_part = dot(qdt[:HEAD_DIM], ds, NN)
        dv_part = dot(qdt[HEAD_DIM:], p_low, NN)
        if b:
            dkt[...] += dk_part
            dvt[...] += dv_part
        else:
            dkt[...] = dk_part
            dvt[...] = dv_part
        half = ports // 2
        for i in range(per):
            a, c = dq[i * ports : i * ports + half], dq[i * ports + half : (i + 1) * ports]
            dq_ref[b * per + i] = jnp.where(low_half(half), a, swap(c)).astype(BF16)
    dw = dw[HEAD_DIM:].astype(BF16)
    wide = dw.shape[1] // LANES
    for r in range(HEAD_DIM // 8):
        for c in range(wide):
            dw_ref[r * wide + c] = dw[r * 8 : (r + 1) * 8, c * LANES : (c + 1) * LANES]
    for r, ref in enumerate((d0_ref, d1_ref, d2_ref)):
        sl = slice(r * own, (r + 1) * own)
        both = jnp.concatenate([dkt[:, sl] * 0.125, dvt[:, sl]], axis=0).T
        ref[...] = both.astype(ref.dtype).reshape(ref.shape)


def merge_kernel(d0_ref, d1_ref, d2_ref, dq_ref, out_ref):
    ports = d0_ref.shape[1]
    summed = d0_ref[...] + d1_ref[...].astype(F32) + d2_ref[...].astype(F32)
    out_ref[:, :ports, :] = summed.astype(BF16)
    out_ref[:, ports:, :] = dq_ref[...]


def unpack_kernel(t_ref, q_ref, k_ref, v_ref):
    hours, ports, width = q_ref.shape
    low = low_half(ports)
    half = ports // 2
    lh = low_half(half)
    for h in range(hours):
        for t in range(width // LANES):
            sl = slice(t * LANES, (t + 1) * LANES)
            c, d = (t_ref[n, h, :ports].astype(F32) for n in (2 * t, 2 * t + 1))
            k_ref[h, :, sl] = jnp.where(low, c, swap(d)).astype(BF16)
            v_ref[h, :, sl] = jnp.where(low, swap(c), d).astype(BF16)
            a, b = (t_ref[n, h, ports:].astype(F32) for n in (2 * t, 2 * t + 1))
            q_ref[h, :half, sl] = jnp.where(lh, a, swap(b)).astype(BF16)
            q_ref[h, half:, sl] = jnp.where(lh, swap(a), b).astype(BF16)


def call(kernel, outs, *args, scratch=(), name):
    return pl.pallas_call(
        kernel,
        out_shape=outs,
        scratch_shapes=scratch,
        compiler_params=pltpu.CompilerParams(vmem_limit_bytes=40 * 1024 * 1024),
        name=name,
    )(*args)


def shape(*dims):
    return jax.ShapeDtypeStruct(dims, BF16)


def exchange(a, axes):
    return lax.all_to_all(a, axes, 0, 0, tiled=True)


def shift(a, by):
    return lax.ppermute(a, "zh", [((i + by) % 3, i) for i in range(3)])


def per_device(query_rows, key_rows, value_rows, out_grad, out_weight, adjacency):
    parts = lax.axis_size("zh")
    heads, hours = lax.axis_size("x"), lax.axis_size("c")
    port_count = lax.axis_size(PORT_AXES)
    tm_count = lax.axis_size(TM_AXES)
    ports, _, width = query_rows.shape
    model = out_grad.shape[2]
    group = heads * hours
    total = port_count * ports
    q, k, v, g = (a.transpose(1, 0, 2) for a in (query_rows, key_rows, value_rows, out_grad))
    kv_send = call(pack_kv_kernel, shape(heads, hours, ports, LANES), k, v, name="pack_kv")
    kv0 = exchange(kv_send.reshape(group, ports, LANES), ("x", "c"))
    adj = jnp.pad(adjacency, ((0, 0), (HEAD_DIM, LANES - HEAD_DIM - adjacency.shape[1])))
    qg_send = call(pack_qg_kernel, shape(heads, hours, ports, LANES + model), q, g, adj, name="pack_qg")
    kv0, qg_send = lax.optimization_barrier((kv0, qg_send))
    kv1, kv2 = shift(kv0, 1), shift(kv0, 2)
    qg_got = exchange(qg_send.reshape(group, ports, LANES + model), ("x", "c"))
    w_n = lax.dynamic_slice_in_dim(out_weight, lax.axis_index("x") * HEAD_DIM, HEAD_DIM, 0)
    tiles = HEAD_DIM * model // (8 * LANES)
    vec, acc = pltpu.VMEM((total, LANES), BF16), pltpu.VMEM((HEAD_DIM, total), F32)
    block = shape(group, ports, LANES)
    vmem = pl.BlockSpec(memory_space=pltpu.VMEM)
    d0, d1, d2, dq, dw = pl.pallas_call(
        functools.partial(attend_kernel, 256),
        out_shape=(
            jax.ShapeDtypeStruct(block.shape, F32),
            block,
            block,
            shape(group, ports // 2, LANES),
            shape(tiles, 8, LANES),
        ),
        in_specs=[pl.BlockSpec(memory_space=pltpu.SMEM)] + [vmem] * 5,
        out_specs=(vmem,) * 5,
        scratch_shapes=[vec, vec, acc, acc],
        compiler_params=pltpu.CompilerParams(vmem_limit_bytes=40 * 1024 * 1024),
        name="attend",
    )(lax.axis_index("zh").reshape(1), kv0, kv1, kv2, qg_got, w_n)
    d1, d2 = shift(d1, 2), shift(d2, 1)
    dw = exchange(dw, TM_AXES)
    dw = jnp.sum(dw.reshape(tm_count, -1, 8, LANES).astype(F32), axis=0).astype(BF16)
    dw = exchange(jnp.broadcast_to(dw, (port_count, *dw.shape)), PORT_AXES)
    back = call(merge_kernel, shape(group, ports + ports // 2, LANES), d0, d1, d2, dq, name="merge")
    back = exchange(back, ("x", "c"))
    dw = dw.reshape(heads, parts, hours, -1, 8, LANES).astype(F32)
    dw = (jnp.sum(dw, axis=(1, 2)) * (1.0 / (hours * tm_count))).astype(BF16)
    dw = exchange(jnp.broadcast_to(dw, (tm_count, *dw.shape)), TM_AXES)
    dw = dw.transpose(1, 0, 2, 3, 4).reshape(heads, HEAD_DIM // 8, model // LANES, 8, LANES)
    dw = dw.transpose(0, 1, 3, 2, 4).reshape(width, model).astype(F32)
    grads = shape(hours, ports, width)
    grads = call(
        unpack_kernel, (grads,) * 3, back.reshape(heads, hours, ports + ports // 2, LANES), name="unpack"
    )
    return *(a.transpose(1, 0, 2) for a in grads), dw


def solution(mesh):
    fine = Mesh(mesh.devices.reshape(4, 3, 2, 8, 4), PORT_AXES + TM_AXES)
    rows = P(PORT_AXES, TM_AXES, None)
    return jax.shard_map(
        per_device,
        mesh=fine,
        in_specs=(rows, rows, rows, rows, P(), P(PORT_AXES, None)),
        out_specs=(rows, rows, rows, P()),
        check_vma=False,
    )
```

time: 132 us -> 137 us (1.038)
  blocking collectives: 55 us -> 20.9 us
  starting transfers between devices: 21.8 us -> 55 us
  waiting for transfers between devices: 38.2 us -> 46.2 us
  Pallas kernels: 9.94 us -> 6.36 us
  local copies, waits for them, and re-layouts: 4.7 us -> 6.92 us
    all_to_all x3 -> x1, blocking collectives: 55 us -> 20.9 us  [exchange(): return lax.all_to_all(a, axes, 0, 0, tiled=True)]
    ppermute x0 -> x4, waiting for transfers between devices: none -> 28.7 us  [shift(): return lax.ppermute(a, 'zh', [((i + by) % 3, i) for i in range(3)])]
    all_to_all x2 -> x5, waiting for transfers between devices: 38.2 us -> 17.5 us  [exchange(): return lax.all_to_all(a, axes, 0, 0, tiled=True)]
    ppermute x0 -> x4, starting transfers between devices: none -> 18.4 us  [shift(): return lax.ppermute(a, 'zh', [((i + by) % 3, i) for i in range(3)])]
    all_to_all x2 -> x5, starting transfers between devices: 21.8 us -> 36.7 us  [exchange(): return lax.all_to_all(a, axes, 0, 0, tiled=True)]
    pallas_call x3 -> x5, Pallas kernels: 9.94 us -> 6.36 us  [the longest x1 3.83 us: per_device(): pl.pallas_call(functools.partial(attend_kernel, 256), out_shape=(jax.Shap...]
    unnamed x15 -> x13, local copies, waits for them, and re-layouts: 3.88 us -> 3.68 us
  transfers between devices with their start and end apart: 2 -> 9, of which waited for: 2 -> 7; matrix products, arithmetic and copies ran while one was open for 2% -> 2% of each run, Pallas kernels for 0% -> 1%
where the time goes in v3:
time: 137 us; the launch traced here: 136 us
  starting transfers between devices  55 us (40%)
  waiting for transfers between devices  46.2 us (34%)
  blocking collectives  20.9 us (15%)
  local copies, waits for them, and re-layouts  6.92 us (5%)
  Pallas kernels  6.36 us (5%)
    all_to_all x5, starting transfers between devices, exchange(): return lax.all_to_all(a, axes, 0, 0, tiled=True)  36.7 us
    ppermute x4, waiting for transfers between devices, shift(): return lax.ppermute(a, 'zh', [((i + by) % 3, i) for i in range(3)])  28.7 us
    all_to_all x1, blocking collectives, exchange(): return lax.all_to_all(a, axes, 0, 0, tiled=True)  20.9 us
    ppermute x4, starting transfers between devices, shift(): return lax.ppermute(a, 'zh', [((i + by) % 3, i) for i in range(3)])  18.4 us
    all_to_all x5, waiting for transfers between devices, exchange(): return lax.all_to_all(a, axes, 0, 0, tiled=True)  17.5 us
    pallas_call x1, Pallas kernels, per_device(): pl.pallas_call(functools.partial(attend_kernel, 256), out_shape=(jax.Shap...  3.83 us
    unnamed x13, local copies, waits for them, and re-layouts  3.68 us
  transfers between devices with their start and end apart: 9, of which 7 were waited for; matrix products, arithmetic and copies ran while one was open for 2% of the time, Pallas kernels for 1%

profile of v3, /device:TPU:1, one launch (start us, length us, event | category | flops | bytes accessed | tf_op | source)
XLA Modules:
  0.0 136.3 jit_solution(2795174345072300112)
XLA Ops:
  0.6 0.0 copy-start
  0.6 0.9 copy_bitcast_fusion.2
  1.6 0.8 pack_kv.1
  2.3 0.0 copy-start.2
  2.3 13.9 %all-to-all-start = ((bf16[8,64,128]{2,1,0:T(8,128)(2,1)}), bf16[8,64,128]{2,1,0:T(8,128)(2,1)S(1)}, u32[]{:S(2)}, u32[]{:S(2)}) async-start(bf16[8,64,128]{2,1,0:T(8,128)(2,1)} %bitcast.3), calls=%async_computation | async-start | bytes 262144 | tf_op jit(solution)/shard_map/all_to_all | solution.py:165
  16.3 0.0 copy-done.2
  16.3 0.0 copy-start.1
  16.3 0.9 copy-done.1
  17.2 0.0 copy-start.3
  17.2 0.7 copy-done.3
  17.9 0.1 pad.4.adj_ref
  17.9 0.9 pack_qg.1
  18.9 2.7 %all-to-all-done.kv0_ref = bf16[8,64,128]{2,1,0:T(8,128)(2,1)S(1)} async-done(((bf16[8,64,128]{2,1,0:T(8,128)(2,1)}), bf16[8,64,128]{2,1,0:T(8,128)(2,1)S(1)}, u32[]{:S(2)}, u32[]{:S(2)}) %all-to-all-start) | async-done | bytes 131104 | tf_op jit(solution)/shard_map/all_to_all | solution.py:165
  21.6 4.3 %all-to-all-start.1 = ((bf16[8,64,640]{2,1,0:T(8,128)(2,1)}), bf16[8,64,640]{2,1,0:T(8,128)(2,1)S(1)}, u32[]{:S(2)}, u32[]{:S(2)}) async-start(bf16[8,64,640]{2,1,0:T(8,128)(2,1)} %bitcast.6), calls=%async_computation.1 | async-start | bytes 1310720 | tf_op jit(solution)/shard_map/all_to_all | solution.py:165
  25.9 2.6 %collective-permute-start.1 = (bf16[8,64,128]{2,1,0:T(8,128)(2,1)S(1)}, bf16[8,64,128]{2,1,0:T(8,128)(2,1)S(1)}, u32[]{:S(2)}, u32[]{:S(2)}) collective-permute-start(bf16[8,64,128]{2,1,0:T(8,128)(2,1)S(1)} %all-to-all-done.kv0_ref), channel_id=1, source_target_pairs={{128,0},{0,64},{64,128},{129,1},{1,65},{65,129},{130,2},{2,66},{66... | collective-permute-start | bytes 393224 | tf_op jit(solution)/shard_map/ppermute | solution.py:169
  28.5 6.6 %collective-permute-start = (bf16[8,64,128]{2,1,0:T(8,128)(2,1)S(1)}, bf16[8,64,128]{2,1,0:T(8,128)(2,1)S(1)}, u32[]{:S(2)}, u32[]{:S(2)}) collective-permute-start(bf16[8,64,128]{2,1,0:T(8,128)(2,1)S(1)} %all-to-all-done.kv0_ref), channel_id=1, source_target_pairs={{64,0},{128,64},{0,128},{65,1},{129,65},{1,129},{66,2},{130,66},{2... | collective-permute-start | bytes 393224 | tf_op jit(solution)/shard_map/ppermute | solution.py:169
  35.1 0.0 copy-done
  35.1 1.6 %collective-permute-done.1.kv2_ref = bf16[8,64,128]{2,1,0:T(8,128)(2,1)S(1)} collective-permute-done((bf16[8,64,128]{2,1,0:T(8,128)(2,1)S(1)}, bf16[8,64,128]{2,1,0:T(8,128)(2,1)S(1)}, u32[]{:S(2)}, u32[]{:S(2)}) %collective-permute-start.1) | collective-permute-done | bytes 131104 | tf_op jit(solution)/shard_map/ppermute | solution.py:169
  36.7 9.8 %collective-permute-done.kv1_ref = bf16[8,64,128]{2,1,0:T(8,128)(2,1)S(1)} collective-permute-done((bf16[8,64,128]{2,1,0:T(8,128)(2,1)S(1)}, bf16[8,64,128]{2,1,0:T(8,128)(2,1)S(1)}, u32[]{:S(2)}, u32[]{:S(2)}) %collective-permute-start) | collective-permute-done | bytes 131104 | tf_op jit(solution)/shard_map/ppermute | solution.py:169
  46.5 0.0 all-to-all-done.1.qg_ref
  46.5 3.8 %attend.1 = (f32[8,64,128]{2,1,0:T(8,128)S(1)}, bf16[8,64,128]{2,1,0:T(8,128)(2,1)S(1)}, bf16[8,64,128]{2,1,0:T(8,128)(2,1)S(1)}, bf16[8,32,128]{2,1,0:T(8,128)(2,1)S(1)}, bf16[32,8,128]{2,1,0:T(8,128)(2,1)S(1)}) custom-call(s32[1]{0:T(128)} %bitcast.z_ref, bf16[8,64,128]{2,1,0:T(8,128)(2,1)S(1)} %all-to-all-done.kv0_ref, ...), custom_call_target="tpu_custom_call" | custom-call | tf_op jit(solution)/shard_map/attend/pallas_call | solution.py:194
  50.3 20.9 %all_to_all.30 = bf16[32,8,128]{2,1,0:T(8,128)(2,1)S(1)} all-to-all(bf16[32,8,128]{2,1,0:T(8,128)(2,1)S(1)} %get-tuple-element.23), channel_id=1, replica_groups=mesh['x'=4,'zh'=3,'c'=2,'y'=8,'zl'=4] {'y','zl'}, dimensions={0} | all-to-all | bytes 131072 | tf_op jit(solution)/shard_map/all_to_all | solution.py:165
  71.2 0.6 broadcast_in_dim.6
  71.8 9.8 %all-to-all-start.4 = ((bf16[24,1,8,128]{3,2,1,0:T(8,128)(2,1)}), bf16[24,1,8,128]{3,2,1,0:T(8,128)(2,1)S(1)}, u32[]{:S(2)}, u32[]{:S(2)}) async-start(bf16[24,1,8,128]{3,2,1,0:T(8,128)(2,1)} %broadcast_in_dim.6), calls=%async_computation.4 | async-start | bytes 98304 | tf_op jit(solution)/shard_map/all_to_all | solution.py:165
  81.7 7.2 %collective-permute-start.2 = (bf16[8,64,128]{2,1,0:T(8,128)(2,1)S(1)}, bf16[8,64,128]{2,1,0:T(8,128)(2,1)S(1)}, u32[]{:S(2)}, u32[]{:S(2)}) collective-permute-start(bf16[8,64,128]{2,1,0:T(8,128)(2,1)S(1)} %get-tuple-element.17), channel_id=1, source_target_pairs={{128,0},{0,64},{64,128},{129,1},{1,65},{65,129},{130,2},{2,66},{66... | collective-permute-start | bytes 393224 | tf_op jit(solution)/shard_map/ppermute | solution.py:169
  88.9 2.0 %collective-permute-start.3 = (bf16[8,64,128]{2,1,0:T(8,128)(2,1)S(1)}, bf16[8,64,128]{2,1,0:T(8,128)(2,1)S(1)}, u32[]{:S(2)}, u32[]{:S(2)}) collective-permute-start(bf16[8,64,128]{2,1,0:T(8,128)(2,1)S(1)} %get-tuple-element.18), channel_id=1, source_target_pairs={{64,0},{128,64},{0,128},{65,1},{129,65},{1,129},{66,2},{130,66},{2... | collective-permute-start | bytes 393224 | tf_op jit(solution)/shard_map/ppermute | solution.py:169
  90.9 1.7 %collective-permute-done.2.d1_ref = bf16[8,64,128]{2,1,0:T(8,128)(2,1)S(1)} collective-permute-done((bf16[8,64,128]{2,1,0:T(8,128)(2,1)S(1)}, bf16[8,64,128]{2,1,0:T(8,128)(2,1)S(1)}, u32[]{:S(2)}, u32[]{:S(2)}) %collective-permute-start.2) | collective-permute-done | bytes 131104 | tf_op jit(solution)/shard_map/ppermute | solution.py:169
  92.6 15.6 %collective-permute-done.3.d2_ref = bf16[8,64,128]{2,1,0:T(8,128)(2,1)S(1)} collective-permute-done((bf16[8,64,128]{2,1,0:T(8,128)(2,1)S(1)}, bf16[8,64,128]{2,1,0:T(8,128)(2,1)S(1)}, u32[]{:S(2)}, u32[]{:S(2)}) %collective-permute-start.3) | collective-permute-done | bytes 131104 | tf_op jit(solution)/shard_map/ppermute | solution.py:169
  108.2 0.7 merge.1
  108.9 0.0 all-to-all-done.4
  108.9 4.7 %all-to-all-start.2 = ((bf16[8,96,128]{2,1,0:T(8,128)(2,1)}), bf16[8,96,128]{2,1,0:T(8,128)(2,1)S(1)}, u32[]{:S(2)}, u32[]{:S(2)}) async-start(bf16[8,96,128]{2,1,0:T(8,128)(2,1)} %merge.1), calls=%async_computation.2 | async-start | bytes 393216 | tf_op jit(solution)/shard_map/all_to_all | solution.py:165
  113.7 5.9 %all-to-all-done.2 = bf16[8,96,128]{2,1,0:T(8,128)(2,1)S(1)} async-done(((bf16[8,96,128]{2,1,0:T(8,128)(2,1)}), bf16[8,96,128]{2,1,0:T(8,128)(2,1)S(1)}, u32[]{:S(2)}, u32[]{:S(2)}) %all-to-all-start.2) | async-done | bytes 196640 | tf_op jit(solution)/shard_map/all_to_all | solution.py:165
  119.5 0.7 broadcast_in_dim.7
  120.3 3.9 %all-to-all-start.5 = ((bf16[32,4,1,8,128]{4,3,1,2,0:T(8,128)(2,1)}), bf16[32,4,1,8,128]{4,3,1,2,0:T(8,128)(2,1)S(1)}, u32[]{:S(2)}, u32[]{:S(2)}) async-start(bf16[32,4,1,8,128]{4,3,1,2,0:T(8,128)(2,1)} %broadcast_in_dim.7), calls=%async_computation.5 | async-start | bytes 524288 | tf_op jit(solution)/shard_map/all_to_all | solution.py:165
  124.2 0.1 unpack.1
  124.3 0.7 copy.38
  125.0 0.7 copy.39
  125.7 0.7 copy.40
  126.4 9.0 %all-to-all-done.5 = bf16[32,4,1,8,128]{4,3,1,2,0:T(8,128)(2,1)S(1)} async-done(((bf16[32,4,1,8,128]{4,3,1,2,0:T(8,128)(2,1)}), bf16[32,4,1,8,128]{4,3,1,2,0:T(8,128)(2,1)S(1)}, u32[]{:S(2)}, u32[]{:S(2)}) %all-to-all-start.5) | async-done | bytes 262176 | tf_op jit(solution)/shard_map/all_to_all | solution.py:165
  135.4 0.9 copy.37
  (7 shorter events, 0.1 us)
Async XLA Ops:
  0.6 34.4 %copy-start = (bf16[256,512]{1,0:T(8,128)(2,1)S(1)}, bf16[256,512]{1,0:T(8,128)(2,1)}, u32[]{:S(2)}) copy-start(bf16[256,512]{1,0:T(8,128)(2,1)} %param.10) | copy-start | bytes 786436
  2.3 13.9 %copy-start.2 = (bf16[64,2,256]{2,1,0:T(2,128)(2,1)S(1)}, bf16[64,2,256]{2,1,0:T(2,128)(2,1)}, u32[]{:S(2)}) copy-start(bf16[64,2,256]{2,1,0:T(2,128)(2,1)} %param.6) | copy-start | bytes 196612
  2.3 19.2 %all-to-all-start = ((bf16[8,64,128]{2,1,0:T(8,128)(2,1)}), bf16[8,64,128]{2,1,0:T(8,128)(2,1)S(1)}, u32[]{:S(2)}, u32[]{:S(2)}) async-start(bf16[8,64,128]{2,1,0:T(8,128)(2,1)} %bitcast.3), calls=%async_computation | async-start | bytes 262144 | tf_op jit(solution)/shard_map/all_to_all | solution.py:165
  16.3 0.9 copy-start.1
  17.2 0.7 copy-start.3
  21.6 24.9 %all-to-all-start.1 = ((bf16[8,64,640]{2,1,0:T(8,128)(2,1)}), bf16[8,64,640]{2,1,0:T(8,128)(2,1)S(1)}, u32[]{:S(2)}, u32[]{:S(2)}) async-start(bf16[8,64,640]{2,1,0:T(8,128)(2,1)} %bitcast.6), calls=%async_computation.1 | async-start | bytes 1310720 | tf_op jit(solution)/shard_map/all_to_all | solution.py:165
  25.9 10.8 %collective-permute-start.1 = (bf16[8,64,128]{2,1,0:T(8,128)(2,1)S(1)}, bf16[8,64,128]{2,1,0:T(8,128)(2,1)S(1)}, u32[]{:S(2)}, u32[]{:S(2)}) collective-permute-start(bf16[8,64,128]{2,1,0:T(8,128)(2,1)S(1)} %all-to-all-done.kv0_ref), channel_id=1, source_target_pairs={{128,0},{0,64},{64,128},{129,1},{1,65},{65,129},{130,2},{2,66},{66... | collective-permute-start | bytes 393224 | tf_op jit(solution)/shard_map/ppermute | solution.py:169
  28.5 18.0 %collective-permute-start = (bf16[8,64,128]{2,1,0:T(8,128)(2,1)S(1)}, bf16[8,64,128]{2,1,0:T(8,128)(2,1)S(1)}, u32[]{:S(2)}, u32[]{:S(2)}) collective-permute-start(bf16[8,64,128]{2,1,0:T(8,128)(2,1)S(1)} %all-to-all-done.kv0_ref), channel_id=1, source_target_pairs={{64,0},{128,64},{0,128},{65,1},{129,65},{1,129},{66,2},{130,66},{2... | collective-permute-start | bytes 393224 | tf_op jit(solution)/shard_map/ppermute | solution.py:169
  71.8 37.1 %all-to-all-start.4 = ((bf16[24,1,8,128]{3,2,1,0:T(8,128)(2,1)}), bf16[24,1,8,128]{3,2,1,0:T(8,128)(2,1)S(1)}, u32[]{:S(2)}, u32[]{:S(2)}) async-start(bf16[24,1,8,128]{3,2,1,0:T(8,128)(2,1)} %broadcast_in_dim.6), calls=%async_computation.4 | async-start | bytes 98304 | tf_op jit(solution)/shard_map/all_to_all | solution.py:165
  81.7 10.9 %collective-permute-start.2 = (bf16[8,64,128]{2,1,0:T(8,128)(2,1)S(1)}, bf16[8,64,128]{2,1,0:T(8,128)(2,1)S(1)}, u32[]{:S(2)}, u32[]{:S(2)}) collective-permute-start(bf16[8,64,128]{2,1,0:T(8,128)(2,1)S(1)} %get-tuple-element.17), channel_id=1, source_target_pairs={{128,0},{0,64},{64,128},{129,1},{1,65},{65,129},{130,2},{2,66},{66... | collective-permute-start | bytes 393224 | tf_op jit(solution)/shard_map/ppermute | solution.py:169
  88.9 19.3 %collective-permute-start.3 = (bf16[8,64,128]{2,1,0:T(8,128)(2,1)S(1)}, bf16[8,64,128]{2,1,0:T(8,128)(2,1)S(1)}, u32[]{:S(2)}, u32[]{:S(2)}) collective-permute-start(bf16[8,64,128]{2,1,0:T(8,128)(2,1)S(1)} %get-tuple-element.18), channel_id=1, source_target_pairs={{64,0},{128,64},{0,128},{65,1},{129,65},{1,129},{66,2},{130,66},{2... | collective-permute-start | bytes 393224 | tf_op jit(solution)/shard_map/ppermute | solution.py:169
  108.9 10.6 %all-to-all-start.2 = ((bf16[8,96,128]{2,1,0:T(8,128)(2,1)}), bf16[8,96,128]{2,1,0:T(8,128)(2,1)S(1)}, u32[]{:S(2)}, u32[]{:S(2)}) async-start(bf16[8,96,128]{2,1,0:T(8,128)(2,1)} %merge.1), calls=%async_computation.2 | async-start | bytes 393216 | tf_op jit(solution)/shard_map/all_to_all | solution.py:165
  120.3 15.1 %all-to-all-start.5 = ((bf16[32,4,1,8,128]{4,3,1,2,0:T(8,128)(2,1)}), bf16[32,4,1,8,128]{4,3,1,2,0:T(8,128)(2,1)S(1)}, u32[]{:S(2)}, u32[]{:S(2)}) async-start(bf16[32,4,1,8,128]{4,3,1,2,0:T(8,128)(2,1)} %broadcast_in_dim.7), calls=%async_computation.5 | async-start | bytes 524288 | tf_op jit(solution)/shard_map/all_to_all | solution.py:165

commit v4 on v3

--- a/solution.py
+++ b/solution.py
@@ -208,6 +208,7 @@
     )(lax.axis_index("zh").reshape(1), kv0, kv1, kv2, qg_got, w_n)
     d1, d2 = shift(d1, 2), shift(d2, 1)
     dw = exchange(dw, TM_AXES)
+    dw, d1, d2 = lax.optimization_barrier((dw, d1, d2))
     dw = jnp.sum(dw.reshape(tm_count, -1, 8, LANES).astype(F32), axis=0).astype(BF16)
     dw = exchange(jnp.broadcast_to(dw, (port_count, *dw.shape)), PORT_AXES)
     back = call(merge_kernel, shape(group, ports + ports // 2, LANES), d0, d1, d2, dq, name="merge")

time: 137 us -> 137 us (level)
  starting transfers between devices: 55 us -> 75.9 us
  blocking collectives: 20.9 us -> 0 us
    all_to_all x5 -> x6, starting transfers between devices: 36.7 us -> 57.6 us  [exchange(): return lax.all_to_all(a, axes, 0, 0, tiled=True)]
    all_to_all x1 -> x0, blocking collectives: 20.9 us -> none  [exchange(): return lax.all_to_all(a, axes, 0, 0, tiled=True)]
    ppermute x4, waiting for transfers between devices: 28.7 us -> 19 us  [shift(): return lax.ppermute(a, 'zh', [((i + by) % 3, i) for i in range(3)])]
    all_to_all x5 -> x6, waiting for transfers between devices: 17.5 us -> 26.4 us  [exchange(): return lax.all_to_all(a, axes, 0, 0, tiled=True)]
  transfers between devices with their start and end apart: 9 -> 10, of which waited for: 7 -> 8; matrix products, arithmetic and copies ran while one was open for 2% -> 2% of each run, Pallas kernels for 1% -> 1%
where the time goes in v4:
time: 137 us; the launch traced here: 136 us
  starting transfers between devices  75.9 us (55%)
  waiting for transfers between devices  45.4 us (33%)
  local copies, waits for them, and re-layouts  6.92 us (5%)
  Pallas kernels  6.8 us (5%)
    all_to_all x6, starting transfers between devices, exchange(): return lax.all_to_all(a, axes, 0, 0, tiled=True)  57.6 us
    all_to_all x6, waiting for transfers between devices, exchange(): return lax.all_to_all(a, axes, 0, 0, tiled=True)  26.4 us
    ppermute x4, waiting for transfers between devices, shift(): return lax.ppermute(a, 'zh', [((i + by) % 3, i) for i in range(3)])  19 us
    ppermute x4, starting transfers between devices, shift(): return lax.ppermute(a, 'zh', [((i + by) % 3, i) for i in range(3)])  18.4 us
    pallas_call x1, Pallas kernels, per_device(): pl.pallas_call(functools.partial(attend_kernel, 256), out_shape=(jax.Shap...  4.26 us
    unnamed x13, local copies, waits for them, and re-layouts  3.68 us
  transfers between devices with their start and end apart: 10, of which 8 were waited for; matrix products, arithmetic and copies ran while one was open for 2% of the time, Pallas kernels for 1%

profile of v4, /device:TPU:1, one launch (start us, length us, event | category | flops | bytes accessed | tf_op | source)
XLA Modules:
  0.0 135.9 jit_solution(5402425902852495574)
XLA Ops:
  0.6 0.0 copy-start
  0.6 0.9 copy_bitcast_fusion.2
  1.6 0.8 pack_kv.1
  2.3 0.0 copy-start.2
  2.3 13.9 %all-to-all-start = ((bf16[8,64,128]{2,1,0:T(8,128)(2,1)}), bf16[8,64,128]{2,1,0:T(8,128)(2,1)S(1)}, u32[]{:S(2)}, u32[]{:S(2)}) async-start(bf16[8,64,128]{2,1,0:T(8,128)(2,1)} %bitcast.3), calls=%async_computation | async-start | bytes 262144 | tf_op jit(solution)/shard_map/all_to_all | solution.py:165
  16.3 0.0 copy-done.2
  16.3 0.0 copy-start.1
  16.3 0.9 copy-done.1
  17.2 0.0 copy-start.3
  17.2 0.7 copy-done.3
  17.9 0.1 pad.4.adj_ref
  17.9 0.9 pack_qg.1
  18.9 2.7 %all-to-all-done.kv0_ref = bf16[8,64,128]{2,1,0:T(8,128)(2,1)S(1)} async-done(((bf16[8,64,128]{2,1,0:T(8,128)(2,1)}), bf16[8,64,128]{2,1,0:T(8,128)(2,1)S(1)}, u32[]{:S(2)}, u32[]{:S(2)}) %all-to-all-start) | async-done | bytes 131104 | tf_op jit(solution)/shard_map/all_to_all | solution.py:165
  21.6 4.3 %all-to-all-start.1 = ((bf16[8,64,640]{2,1,0:T(8,128)(2,1)}), bf16[8,64,640]{2,1,0:T(8,128)(2,1)S(1)}, u32[]{:S(2)}, u32[]{:S(2)}) async-start(bf16[8,64,640]{2,1,0:T(8,128)(2,1)} %bitcast.6), calls=%async_computation.1 | async-start | bytes 1310720 | tf_op jit(solution)/shard_map/all_to_all | solution.py:165
  25.9 2.6 %collective-permute-start.1 = (bf16[8,64,128]{2,1,0:T(8,128)(2,1)S(1)}, bf16[8,64,128]{2,1,0:T(8,128)(2,1)S(1)}, u32[]{:S(2)}, u32[]{:S(2)}) collective-permute-start(bf16[8,64,128]{2,1,0:T(8,128)(2,1)S(1)} %all-to-all-done.kv0_ref), channel_id=1, source_target_pairs={{128,0},{0,64},{64,128},{129,1},{1,65},{65,129},{130,2},{2,66},{66... | collective-permute-start | bytes 393224 | tf_op jit(solution)/shard_map/ppermute | solution.py:169
  28.5 6.6 %collective-permute-start = (bf16[8,64,128]{2,1,0:T(8,128)(2,1)S(1)}, bf16[8,64,128]{2,1,0:T(8,128)(2,1)S(1)}, u32[]{:S(2)}, u32[]{:S(2)}) collective-permute-start(bf16[8,64,128]{2,1,0:T(8,128)(2,1)S(1)} %all-to-all-done.kv0_ref), channel_id=1, source_target_pairs={{64,0},{128,64},{0,128},{65,1},{129,65},{1,129},{66,2},{130,66},{2... | collective-permute-start | bytes 393224 | tf_op jit(solution)/shard_map/ppermute | solution.py:169
  35.1 0.0 copy-done
  35.1 1.6 %collective-permute-done.1.kv2_ref = bf16[8,64,128]{2,1,0:T(8,128)(2,1)S(1)} collective-permute-done((bf16[8,64,128]{2,1,0:T(8,128)(2,1)S(1)}, bf16[8,64,128]{2,1,0:T(8,128)(2,1)S(1)}, u32[]{:S(2)}, u32[]{:S(2)}) %collective-permute-start.1) | collective-permute-done | bytes 131104 | tf_op jit(solution)/shard_map/ppermute | solution.py:169
  36.7 9.8 %collective-permute-done.kv1_ref = bf16[8,64,128]{2,1,0:T(8,128)(2,1)S(1)} collective-permute-done((bf16[8,64,128]{2,1,0:T(8,128)(2,1)S(1)}, bf16[8,64,128]{2,1,0:T(8,128)(2,1)S(1)}, u32[]{:S(2)}, u32[]{:S(2)}) %collective-permute-start) | collective-permute-done | bytes 131104 | tf_op jit(solution)/shard_map/ppermute | solution.py:169
  46.5 0.0 all-to-all-done.1.qg_ref
  46.5 4.3 %attend.1 = (f32[8,64,128]{2,1,0:T(8,128)S(1)}, bf16[8,64,128]{2,1,0:T(8,128)(2,1)S(1)}, bf16[8,64,128]{2,1,0:T(8,128)(2,1)S(1)}, bf16[8,32,128]{2,1,0:T(8,128)(2,1)S(1)}, bf16[32,8,128]{2,1,0:T(8,128)(2,1)}) custom-call(s32[1]{0:T(128)} %bitcast.z_ref, bf16[8,64,128]{2,1,0:T(8,128)(2,1)S(1)} %all-to-all-done.kv0_ref, ...), custom_call_target="tpu_custom_call" | custom-call | tf_op jit(solution)/shard_map/attend/pallas_call | solution.py:194
  50.7 11.7 %all-to-all-start.2 = ((bf16[32,8,128]{2,1,0:T(8,128)(2,1)}), bf16[32,8,128]{2,1,0:T(8,128)(2,1)S(1)}, u32[]{:S(2)}, u32[]{:S(2)}) async-start(bf16[32,8,128]{2,1,0:T(8,128)(2,1)} %get-tuple-element.20), calls=%async_computation.2 | async-start | bytes 131072 | tf_op jit(solution)/shard_map/all_to_all | solution.py:165
  62.4 5.3 %collective-permute-start.2 = (bf16[8,64,128]{2,1,0:T(8,128)(2,1)S(1)}, bf16[8,64,128]{2,1,0:T(8,128)(2,1)S(1)}, u32[]{:S(2)}, u32[]{:S(2)}) collective-permute-start(bf16[8,64,128]{2,1,0:T(8,128)(2,1)S(1)} %get-tuple-element.21), channel_id=1, source_target_pairs={{128,0},{0,64},{64,128},{129,1},{1,65},{65,129},{130,2},{2,66},{66... | collective-permute-start | bytes 393224 | tf_op jit(solution)/shard_map/ppermute | solution.py:169
  67.8 3.9 %collective-permute-start.3 = (bf16[8,64,128]{2,1,0:T(8,128)(2,1)S(1)}, bf16[8,64,128]{2,1,0:T(8,128)(2,1)S(1)}, u32[]{:S(2)}, u32[]{:S(2)}) collective-permute-start(bf16[8,64,128]{2,1,0:T(8,128)(2,1)S(1)} %get-tuple-element.22), channel_id=1, source_target_pairs={{64,0},{128,64},{0,128},{65,1},{129,65},{1,129},{66,2},{130,66},{2... | collective-permute-start | bytes 393224 | tf_op jit(solution)/shard_map/ppermute | solution.py:169
  71.6 0.7 collective-permute-done.2.d1_ref
  72.3 6.9 %collective-permute-done.3.d2_ref = bf16[8,64,128]{2,1,0:T(8,128)(2,1)S(1)} collective-permute-done((bf16[8,64,128]{2,1,0:T(8,128)(2,1)S(1)}, bf16[8,64,128]{2,1,0:T(8,128)(2,1)S(1)}, u32[]{:S(2)}, u32[]{:S(2)}) %collective-permute-start.3) | collective-permute-done | bytes 131104 | tf_op jit(solution)/shard_map/ppermute | solution.py:169
  79.3 0.0 all-to-all-done.2
  79.3 0.6 broadcast_in_dim.6
  80.0 10.6 %all-to-all-start.4 = ((bf16[24,1,8,128]{3,2,1,0:T(8,128)(2,1)}), bf16[24,1,8,128]{3,2,1,0:T(8,128)(2,1)S(1)}, u32[]{:S(2)}, u32[]{:S(2)}) async-start(bf16[24,1,8,128]{3,2,1,0:T(8,128)(2,1)} %broadcast_in_dim.6), calls=%async_computation.4 | async-start | bytes 98304 | tf_op jit(solution)/shard_map/all_to_all | solution.py:165
  90.6 0.7 merge.1
  91.3 9.0 %all-to-all-done.4 = bf16[24,1,8,128]{3,2,1,0:T(8,128)(2,1)S(1)} async-done(((bf16[24,1,8,128]{3,2,1,0:T(8,128)(2,1)}), bf16[24,1,8,128]{3,2,1,0:T(8,128)(2,1)S(1)}, u32[]{:S(2)}, u32[]{:S(2)}) %all-to-all-start.4) | async-done | bytes 49184 | tf_op jit(solution)/shard_map/all_to_all | solution.py:165
  100.3 3.8 %all-to-all-start.3 = ((bf16[8,96,128]{2,1,0:T(8,128)(2,1)}), bf16[8,96,128]{2,1,0:T(8,128)(2,1)S(1)}, u32[]{:S(2)}, u32[]{:S(2)}) async-start(bf16[8,96,128]{2,1,0:T(8,128)(2,1)} %merge.1), calls=%async_computation.3 | async-start | bytes 393216 | tf_op jit(solution)/shard_map/all_to_all | solution.py:165
  104.1 5.9 %all-to-all-done.3 = bf16[8,96,128]{2,1,0:T(8,128)(2,1)S(1)} async-done(((bf16[8,96,128]{2,1,0:T(8,128)(2,1)}), bf16[8,96,128]{2,1,0:T(8,128)(2,1)S(1)}, u32[]{:S(2)}, u32[]{:S(2)}) %all-to-all-start.3) | async-done | bytes 196640 | tf_op jit(solution)/shard_map/all_to_all | solution.py:165
  110.0 0.7 broadcast_in_dim.7
  110.7 13.3 %all-to-all-start.5 = ((bf16[32,4,1,8,128]{4,3,1,2,0:T(8,128)(2,1)}), bf16[32,4,1,8,128]{4,3,1,2,0:T(8,128)(2,1)S(1)}, u32[]{:S(2)}, u32[]{:S(2)}) async-start(bf16[32,4,1,8,128]{4,3,1,2,0:T(8,128)(2,1)} %broadcast_in_dim.7), calls=%async_computation.5 | async-start | bytes 524288 | tf_op jit(solution)/shard_map/all_to_all | solution.py:165
  124.0 0.1 unpack.1
  124.1 0.7 copy.38
  124.8 0.7 copy.39
  125.5 0.7 copy.40
  126.2 8.7 %all-to-all-done.5 = bf16[32,4,1,8,128]{4,3,1,2,0:T(8,128)(2,1)S(1)} async-done(((bf16[32,4,1,8,128]{4,3,1,2,0:T(8,128)(2,1)}), bf16[32,4,1,8,128]{4,3,1,2,0:T(8,128)(2,1)S(1)}, u32[]{:S(2)}, u32[]{:S(2)}) %all-to-all-start.5) | async-done | bytes 262176 | tf_op jit(solution)/shard_map/all_to_all | solution.py:165
  135.0 0.9 copy.37
  (7 shorter events, 0.1 us)
Async XLA Ops:
  0.6 34.4 %copy-start = (bf16[256,512]{1,0:T(8,128)(2,1)S(1)}, bf16[256,512]{1,0:T(8,128)(2,1)}, u32[]{:S(2)}) copy-start(bf16[256,512]{1,0:T(8,128)(2,1)} %param.10) | copy-start | bytes 786436
  2.3 13.9 %copy-start.2 = (bf16[64,2,256]{2,1,0:T(2,128)(2,1)S(1)}, bf16[64,2,256]{2,1,0:T(2,128)(2,1)}, u32[]{:S(2)}) copy-start(bf16[64,2,256]{2,1,0:T(2,128)(2,1)} %param.6) | copy-start | bytes 196612
  2.3 19.2 %all-to-all-start = ((bf16[8,64,128]{2,1,0:T(8,128)(2,1)}), bf16[8,64,128]{2,1,0:T(8,128)(2,1)S(1)}, u32[]{:S(2)}, u32[]{:S(2)}) async-start(bf16[8,64,128]{2,1,0:T(8,128)(2,1)} %bitcast.3), calls=%async_computation | async-start | bytes 262144 | tf_op jit(solution)/shard_map/all_to_all | solution.py:165
  16.3 0.9 copy-start.1
  17.2 0.7 copy-start.3
  21.6 24.9 %all-to-all-start.1 = ((bf16[8,64,640]{2,1,0:T(8,128)(2,1)}), bf16[8,64,640]{2,1,0:T(8,128)(2,1)S(1)}, u32[]{:S(2)}, u32[]{:S(2)}) async-start(bf16[8,64,640]{2,1,0:T(8,128)(2,1)} %bitcast.6), calls=%async_computation.1 | async-start | bytes 1310720 | tf_op jit(solution)/shard_map/all_to_all | solution.py:165
  25.9 10.8 %collective-permute-start.1 = (bf16[8,64,128]{2,1,0:T(8,128)(2,1)S(1)}, bf16[8,64,128]{2,1,0:T(8,128)(2,1)S(1)}, u32[]{:S(2)}, u32[]{:S(2)}) collective-permute-start(bf16[8,64,128]{2,1,0:T(8,128)(2,1)S(1)} %all-to-all-done.kv0_ref), channel_id=1, source_target_pairs={{128,0},{0,64},{64,128},{129,1},{1,65},{65,129},{130,2},{2,66},{66... | collective-permute-start | bytes 393224 | tf_op jit(solution)/shard_map/ppermute | solution.py:169
  28.5 18.0 %collective-permute-start = (bf16[8,64,128]{2,1,0:T(8,128)(2,1)S(1)}, bf16[8,64,128]{2,1,0:T(8,128)(2,1)S(1)}, u32[]{:S(2)}, u32[]{:S(2)}) collective-permute-start(bf16[8,64,128]{2,1,0:T(8,128)(2,1)S(1)} %all-to-all-done.kv0_ref), channel_id=1, source_target_pairs={{64,0},{128,64},{0,128},{65,1},{129,65},{1,129},{66,2},{130,66},{2... | collective-permute-start | bytes 393224 | tf_op jit(solution)/shard_map/ppermute | solution.py:169
  50.7 28.6 %all-to-all-start.2 = ((bf16[32,8,128]{2,1,0:T(8,128)(2,1)}), bf16[32,8,128]{2,1,0:T(8,128)(2,1)S(1)}, u32[]{:S(2)}, u32[]{:S(2)}) async-start(bf16[32,8,128]{2,1,0:T(8,128)(2,1)} %get-tuple-element.20), calls=%async_computation.2 | async-start | bytes 131072 | tf_op jit(solution)/shard_map/all_to_all | solution.py:165
  62.4 9.9 %collective-permute-start.2 = (bf16[8,64,128]{2,1,0:T(8,128)(2,1)S(1)}, bf16[8,64,128]{2,1,0:T(8,128)(2,1)S(1)}, u32[]{:S(2)}, u32[]{:S(2)}) collective-permute-start(bf16[8,64,128]{2,1,0:T(8,128)(2,1)S(1)} %get-tuple-element.21), channel_id=1, source_target_pairs={{128,0},{0,64},{64,128},{129,1},{1,65},{65,129},{130,2},{2,66},{66... | collective-permute-start | bytes 393224 | tf_op jit(solution)/shard_map/ppermute | solution.py:169
  67.8 11.5 %collective-permute-start.3 = (bf16[8,64,128]{2,1,0:T(8,128)(2,1)S(1)}, bf16[8,64,128]{2,1,0:T(8,128)(2,1)S(1)}, u32[]{:S(2)}, u32[]{:S(2)}) collective-permute-start(bf16[8,64,128]{2,1,0:T(8,128)(2,1)S(1)} %get-tuple-element.22), channel_id=1, source_target_pairs={{64,0},{128,64},{0,128},{65,1},{129,65},{1,129},{66,2},{130,66},{2... | collective-permute-start | bytes 393224 | tf_op jit(solution)/shard_map/ppermute | solution.py:169
  80.0 20.4 %all-to-all-start.4 = ((bf16[24,1,8,128]{3,2,1,0:T(8,128)(2,1)}), bf16[24,1,8,128]{3,2,1,0:T(8,128)(2,1)S(1)}, u32[]{:S(2)}, u32[]{:S(2)}) async-start(bf16[24,1,8,128]{3,2,1,0:T(8,128)(2,1)} %broadcast_in_dim.6), calls=%async_computation.4 | async-start | bytes 98304 | tf_op jit(solution)/shard_map/all_to_all | solution.py:165
  100.3 9.7 %all-to-all-start.3 = ((bf16[8,96,128]{2,1,0:T(8,128)(2,1)}), bf16[8,96,128]{2,1,0:T(8,128)(2,1)S(1)}, u32[]{:S(2)}, u32[]{:S(2)}) async-start(bf16[8,96,128]{2,1,0:T(8,128)(2,1)} %merge.1), calls=%async_computation.3 | async-start | bytes 393216 | tf_op jit(solution)/shard_map/all_to_all | solution.py:165
  110.7 24.2 %all-to-all-start.5 = ((bf16[32,4,1,8,128]{4,3,1,2,0:T(8,128)(2,1)}), bf16[32,4,1,8,128]{4,3,1,2,0:T(8,128)(2,1)S(1)}, u32[]{:S(2)}, u32[]{:S(2)}) async-start(bf16[32,4,1,8,128]{4,3,1,2,0:T(8,128)(2,1)} %broadcast_in_dim.7), calls=%async_computation.5 | async-start | bytes 524288 | tf_op jit(solution)/shard_map/all_to_all | solution.py:165

commit v5 on v3

--- a/solution.py
+++ b/solution.py
@@ -60,21 +60,18 @@
             out_ref[n, h, :, LANES:] = g_ref[h]
 
 
-def attend_kernel(
-    rows, z_ref, kv0_ref, kv1_ref, kv2_ref, qg_ref, w_ref, d0_ref, d1_ref, d2_ref, dq_ref, dw_ref, kx, kv, dkt, dvt
-):
-    group, ports, _ = kv0_ref.shape
+def attend_kernel(rows, kv_ref, qg_ref, w_ref, out_ref, dw_ref, kx, kv, dkt, dvt):
+    parts, group, ports, _ = kv_ref.shape
     own = group * ports
-    total = 3 * own
+    total = parts * own
     lane = lax.broadcasted_iota(jnp.int32, (own, LANES), 1)
     row = lax.broadcasted_iota(jnp.int32, (own, LANES), 0)
-    for r, ref in enumerate((kv0_ref, kv1_ref, kv2_ref)):
-        z = lax.rem(z_ref[0] + r, 3)
-        part = ref[...].reshape(own, LANES)
-        pair = lax.shift_right_logical(row, 7)
-        block = (pair * 3 + z) * 4 + lax.bitwise_and(lax.shift_right_logical(row, 5), 3)
-        hot = jnp.where(lane - HEAD_DIM == block, 1.0, 0.0)
-        sl = slice(r * own, (r + 1) * own)
+    pair = lax.shift_right_logical(row, 7)
+    inner = lax.bitwise_and(lax.shift_right_logical(row, 5), 3)
+    for z in range(parts):
+        part = kv_ref[z].reshape(own, LANES)
+        hot = jnp.where(lane - HEAD_DIM == (pair * parts + z) * 4 + inner, 1.0, 0.0)
+        sl = slice(z * own, (z + 1) * own)
         kv[sl, :] = part
         kx[sl, :] = jnp.where(lane < HEAD_DIM, part.astype(F32), hot).astype(BF16)
     w_n = jnp.concatenate([jnp.zeros_like(w_ref), w_ref[...]], axis=0)
@@ -112,37 +109,37 @@
         half = ports // 2
         for i in range(per):
             a, c = dq[i * ports : i * ports + half], dq[i * ports + half : (i + 1) * ports]
-            dq_ref[b * per + i] = jnp.where(low_half(half), a, swap(c)).astype(BF16)
+            both = jnp.where(low_half(half), a, swap(c)).astype(BF16)
+            for z in range(parts):
+                out_ref[(b * per + i) // 2, z, i % 2, ports : ports + half, :] = both
     dw = dw[HEAD_DIM:].astype(BF16)
     wide = dw.shape[1] // LANES
     for r in range(HEAD_DIM // 8):
         for c in range(wide):
             dw_ref[r * wide + c] = dw[r * 8 : (r + 1) * 8, c * LANES : (c + 1) * LANES]
-    for r, ref in enumerate((d0_ref, d1_ref, d2_ref)):
-        sl = slice(r * own, (r + 1) * own)
-        both = jnp.concatenate([dkt[:, sl] * 0.125, dvt[:, sl]], axis=0).T
-        ref[...] = both.astype(ref.dtype).reshape(ref.shape)
-
-
-def merge_kernel(d0_ref, d1_ref, d2_ref, dq_ref, out_ref):
-    ports = d0_ref.shape[1]
-    summed = d0_ref[...] + d1_ref[...].astype(F32) + d2_ref[...].astype(F32)
-    out_ref[:, :ports, :] = summed.astype(BF16)
-    out_ref[:, ports:, :] = dq_ref[...]
-
-
-def unpack_kernel(t_ref, q_ref, k_ref, v_ref):
+    for z in range(parts):
+        sl = slice(z * own, (z + 1) * own)
+        both = jnp.concatenate([dkt[:, sl] * 0.125, dvt[:, sl]], axis=0).T.astype(BF16)
+        for i in range(group):
+            out_ref[i // 2, z, i % 2, :ports, :] = both[i * ports : (i + 1) * ports]
+            out_ref[i // 2, z, i % 2, ports + half :, :] = jnp.zeros((8, LANES), BF16)
+
+
+def unpack_kernel(z_ref, t_ref, q_ref, k_ref, v_ref):
     hours, ports, width = q_ref.shape
     low = low_half(ports)
     half = ports // 2
     lh = low_half(half)
+    z_own = z_ref[0]
     for h in range(hours):
         for t in range(width // LANES):
             sl = slice(t * LANES, (t + 1) * LANES)
-            c, d = (t_ref[n, h, :ports].astype(F32) for n in (2 * t, 2 * t + 1))
+            c, d = (
+                sum(t_ref[n, z, h, :ports].astype(F32) for z in range(t_ref.shape[1])) for n in (2 * t, 2 * t + 1)
+            )
             k_ref[h, :, sl] = jnp.where(low, c, swap(d)).astype(BF16)
             v_ref[h, :, sl] = jnp.where(low, swap(c), d).astype(BF16)
-            a, b = (t_ref[n, h, ports:].astype(F32) for n in (2 * t, 2 * t + 1))
+            a, b = (t_ref[n, z_own, h, ports : ports + half].astype(F32) for n in (2 * t, 2 * t + 1))
             q_ref[h, :half, sl] = jnp.where(lh, a, swap(b)).astype(BF16)
             q_ref[h, half:, sl] = jnp.where(lh, swap(a), b).astype(BF16)
 
@@ -163,10 +160,6 @@
 
 def exchange(a, axes):
     return lax.all_to_all(a, axes, 0, 0, tiled=True)
-
-
-def shift(a, by):
-    return lax.ppermute(a, "zh", [((i + by) % 3, i) for i in range(3)])
 
 
 def per_device(query_rows, key_rows, value_rows, out_grad, out_weight, adjacency):
@@ -184,43 +177,40 @@
     adj = jnp.pad(adjacency, ((0, 0), (HEAD_DIM, LANES - HEAD_DIM - adjacency.shape[1])))
     qg_send = call(pack_qg_kernel, shape(heads, hours, ports, LANES + model), q, g, adj, name="pack_qg")
     kv0, qg_send = lax.optimization_barrier((kv0, qg_send))
-    kv1, kv2 = shift(kv0, 1), shift(kv0, 2)
+    kv_all = lax.all_gather(kv0, "zh")
     qg_got = exchange(qg_send.reshape(group, ports, LANES + model), ("x", "c"))
     w_n = lax.dynamic_slice_in_dim(out_weight, lax.axis_index("x") * HEAD_DIM, HEAD_DIM, 0)
     tiles = HEAD_DIM * model // (8 * LANES)
+    chunk = ports + ports // 2 + 8
     vec, acc = pltpu.VMEM((total, LANES), BF16), pltpu.VMEM((HEAD_DIM, total), F32)
-    block = shape(group, ports, LANES)
-    vmem = pl.BlockSpec(memory_space=pltpu.VMEM)
-    d0, d1, d2, dq, dw = pl.pallas_call(
+    back, dw = call(
         functools.partial(attend_kernel, 256),
-        out_shape=(
-            jax.ShapeDtypeStruct(block.shape, F32),
-            block,
-            block,
-            shape(group, ports // 2, LANES),
-            shape(tiles, 8, LANES),
-        ),
-        in_specs=[pl.BlockSpec(memory_space=pltpu.SMEM)] + [vmem] * 5,
-        out_specs=(vmem,) * 5,
-        scratch_shapes=[vec, vec, acc, acc],
-        compiler_params=pltpu.CompilerParams(vmem_limit_bytes=40 * 1024 * 1024),
+        (shape(heads, parts, hours, chunk, LANES), shape(tiles, 8, LANES)),
+        kv_all,
+        qg_got,
+        w_n,
+        scratch=[vec, vec, acc, acc],
         name="attend",
-    )(lax.axis_index("zh").reshape(1), kv0, kv1, kv2, qg_got, w_n)
-    d1, d2 = shift(d1, 2), shift(d2, 1)
+    )
     dw = exchange(dw, TM_AXES)
-    dw = jnp.sum(dw.reshape(tm_count, -1, 8, LANES).astype(F32), axis=0).astype(BF16)
-    dw = exchange(jnp.broadcast_to(dw, (port_count, *dw.shape)), PORT_AXES)
-    back = call(merge_kernel, shape(group, ports + ports // 2, LANES), d0, d1, d2, dq, name="merge")
-    back = exchange(back, ("x", "c"))
-    dw = dw.reshape(heads, parts, hours, -1, 8, LANES).astype(F32)
+    dw = jnp.sum(dw.astype(F32), axis=0).astype(BF16)
+    back = back.reshape(port_count, chunk, LANES)
+    back = back.at[:, chunk - 8 :, :].set(jnp.broadcast_to(dw, (port_count, 8, LANES)))
+    back = exchange(back, PORT_AXES).reshape(heads, parts, hours, chunk, LANES)
+    dw = back[:, :, :, chunk - 8 :, :].astype(F32)
     dw = (jnp.sum(dw, axis=(1, 2)) * (1.0 / (hours * tm_count))).astype(BF16)
     dw = exchange(jnp.broadcast_to(dw, (tm_count, *dw.shape)), TM_AXES)
-    dw = dw.transpose(1, 0, 2, 3, 4).reshape(heads, HEAD_DIM // 8, model // LANES, 8, LANES)
+    dw = dw.transpose(1, 0, 2, 3).reshape(heads, HEAD_DIM // 8, model // LANES, 8, LANES)
     dw = dw.transpose(0, 1, 3, 2, 4).reshape(width, model).astype(F32)
-    grads = shape(hours, ports, width)
-    grads = call(
-        unpack_kernel, (grads,) * 3, back.reshape(heads, hours, ports + ports // 2, LANES), name="unpack"
-    )
+    vmem = pl.BlockSpec(memory_space=pltpu.VMEM)
+    grads = pl.pallas_call(
+        unpack_kernel,
+        out_shape=(shape(hours, ports, width),) * 3,
+        in_specs=[pl.BlockSpec(memory_space=pltpu.SMEM), vmem],
+        out_specs=(vmem,) * 3,
+        compiler_params=pltpu.CompilerParams(vmem_limit_bytes=40 * 1024 * 1024),
+        name="unpack",
+    )(lax.axis_index("zh").reshape(1), back)
     return *(a.transpose(1, 0, 2) for a in grads), dw
 
 

time: 137 us -> 125 us (0.912)
  blocking collectives: 20.9 us -> 77.2 us
  waiting for transfers between devices: 46.2 us -> 11.4 us
  starting transfers between devices: 55 us -> 22.1 us
    all_to_all x1 -> x2, blocking collectives: 20.9 us -> 58.7 us  [exchange(): return lax.all_to_all(a, axes, 0, 0, tiled=True)]
    ppermute x4 -> x0, waiting for transfers between devices: 28.7 us -> none  [shift(): return lax.ppermute(a, 'zh', [((i + by) % 3, i) for i in range(3)])]
    all_gather x0 -> x1, blocking collectives: none -> 18.5 us  [per_device(): kv_all = lax.all_gather(kv0, 'zh')]
    ppermute x4 -> x0, starting transfers between devices: 18.4 us -> none  [shift(): return lax.ppermute(a, 'zh', [((i + by) % 3, i) for i in range(3)])]
    all_to_all x5 -> x3, starting transfers between devices: 36.7 us -> 22.1 us  [exchange(): return lax.all_to_all(a, axes, 0, 0, tiled=True)]
    all_to_all x5 -> x3, waiting for transfers between devices: 17.5 us -> 11.4 us  [exchange(): return lax.all_to_all(a, axes, 0, 0, tiled=True)]
    pallas_call x1, Pallas kernels: 3.83 us -> 0.13 us  [per_device(): pl.pallas_call(unpack_kernel, out_shape=(shape(hours, ports, width),) * 3...]
    pallas_call x4 -> x3, Pallas kernels: 2.54 us -> 5.48 us  [call(): pl.pallas_call(kernel, out_shape=outs, scratch_shapes=scratch, compiler_p...]
  transfers between devices with their start and end apart: 9 -> 3, of which waited for: 7 -> 2; matrix products, arithmetic and copies ran while one was open for 2% -> 2% of each run, Pallas kernels for 1% -> 1%
where the time goes in v5:
time: 125 us; the launch traced here: 123 us
  blocking collectives  77.2 us (62%)
  starting transfers between devices  22.1 us (18%)
  waiting for transfers between devices  11.4 us (9%)
  local copies, waits for them, and re-layouts  6.31 us (5%)
  Pallas kernels  5.61 us (4%)
    all_to_all x2, blocking collectives, exchange(): return lax.all_to_all(a, axes, 0, 0, tiled=True)  58.7 us
    all_to_all x3, starting transfers between devices, exchange(): return lax.all_to_all(a, axes, 0, 0, tiled=True)  22.1 us
    all_gather x1, blocking collectives, per_device(): kv_all = lax.all_gather(kv0, 'zh')  18.5 us
    all_to_all x3, waiting for transfers between devices, exchange(): return lax.all_to_all(a, axes, 0, 0, tiled=True)  11.4 us
    pallas_call x3, Pallas kernels, call(): pl.pallas_call(kernel, out_shape=outs, scratch_shapes=scratch, compiler_p...  5.48 us
    unnamed x13, local copies, waits for them, and re-layouts  3.68 us
  transfers between devices with their start and end apart: 3, of which 2 were waited for; matrix products, arithmetic and copies ran while one was open for 2% of the time, Pallas kernels for 1%

profile of v5, /device:TPU:1, one launch (start us, length us, event | category | flops | bytes accessed | tf_op | source)
XLA Modules:
  0.0 123.4 jit_solution(2992268241936135171)
XLA Ops:
  0.6 0.0 copy-start
  0.6 0.9 copy_bitcast_fusion.2
  1.6 0.8 pack_kv.1
  2.3 0.0 copy-start.2
  2.3 13.9 %all-to-all-start = ((bf16[8,64,128]{2,1,0:T(8,128)(2,1)}), bf16[8,64,128]{2,1,0:T(8,128)(2,1)S(1)}, u32[]{:S(2)}, u32[]{:S(2)}) async-start(bf16[8,64,128]{2,1,0:T(8,128)(2,1)} %bitcast.3), calls=%async_computation | async-start | bytes 262144 | tf_op jit(solution)/shard_map/all_to_all | solution.py:162
  16.3 0.0 copy-done.2
  16.3 0.0 copy-start.1
  16.3 0.9 copy-done.1
  17.2 0.0 copy-start.3
  17.2 0.7 copy-done.3
  17.9 0.1 pad.6.adj_ref
  17.9 0.9 pack_qg.1
  18.9 2.7 %all-to-all-done = bf16[8,64,128]{2,1,0:T(8,128)(2,1)S(1)} async-done(((bf16[8,64,128]{2,1,0:T(8,128)(2,1)}), bf16[8,64,128]{2,1,0:T(8,128)(2,1)S(1)}, u32[]{:S(2)}, u32[]{:S(2)}) %all-to-all-start) | async-done | bytes 131104 | tf_op jit(solution)/shard_map/all_to_all | solution.py:162
  21.6 4.3 %all-to-all-start.1 = ((bf16[8,64,640]{2,1,0:T(8,128)(2,1)}), bf16[8,64,640]{2,1,0:T(8,128)(2,1)S(1)}, u32[]{:S(2)}, u32[]{:S(2)}) async-start(bf16[8,64,640]{2,1,0:T(8,128)(2,1)} %bitcast.7), calls=%async_computation.1 | async-start | bytes 1310720 | tf_op jit(solution)/shard_map/all_to_all | solution.py:162
  25.9 0.0 copy-done
  25.9 18.5 %all-gather = bf16[24,64,128]{2,1,0:T(8,128)(2,1)S(1)} all-gather(bf16[8,64,128]{2,1,0:T(8,128)(2,1)S(1)} %all-to-all-done), channel_id=2, replica_groups=mesh['x'=4,'zh'=3,'c'=2,'y'=8,'zl'=4] {'zh'}, dimensions={0}, use_global_device_ids=true | all-gather | bytes 524288 | tf_op jit(solution)/shard_map/all_gather | solution.py:180
  44.4 0.0 all-to-all-done.1.qg_ref
  44.4 3.8 %attend.1 = (bf16[4,3,2,104,128]{4,3,2,1,0:T(8,128)(2,1)S(1)}, bf16[32,8,128]{2,1,0:T(8,128)(2,1)S(1)}) custom-call(bf16[3,8,64,128]{3,2,1,0:T(8,128)(2,1)S(1)} %bitcast.27, bf16[8,64,640]{2,1,0:T(8,128)(2,1)S(1)} %all-to-all-done.1.qg_ref, bf16[64,512]{1,0:T(8,128)(2,1)S(1)} %constant_dynamic-slice_fusion.w_ref), custom_call_target="tpu_custom_call" | custom-call | tf_op jit(solution)/shard_map/attend/pallas_call | solution.py:148
  48.2 23.0 %all_to_all.25 = bf16[32,8,128]{2,1,0:T(8,128)(2,1)S(1)} all-to-all(bf16[32,8,128]{2,1,0:T(8,128)(2,1)S(1)} %get-tuple-element.26), channel_id=1, replica_groups=mesh['x'=4,'zh'=3,'c'=2,'y'=8,'zl'=4] {'y','zl'}, dimensions={0} | all-to-all | bytes 131072 | tf_op jit(solution)/shard_map/all_to_all | solution.py:162
  71.2 35.7 %all_to_all.26 = bf16[24,104,128]{2,1,0:T(8,128)(2,1)S(1)} all-to-all(bf16[24,104,128]{2,1,0:T(8,128)(2,1)S(1)} %broadcast_dynamic-update-slice_fusion), channel_id=1, replica_groups=mesh['x'=4,'zh'=3,'c'=2,'y'=8,'zl'=4] {'x','zh','c'}, dimensions={0} | all-to-all | bytes 1277952 | tf_op jit(solution)/shard_map/all_to_all | solution.py:162
  106.9 0.7 broadcast_in_dim.4
  107.7 3.9 %all-to-all-start.4 = ((bf16[32,4,8,128]{3,2,1,0:T(8,128)(2,1)}), bf16[32,4,8,128]{3,2,1,0:T(8,128)(2,1)S(1)}, u32[]{:S(2)}, u32[]{:S(2)}) async-start(bf16[32,4,8,128]{3,2,1,0:T(8,128)(2,1)} %broadcast_in_dim.4), calls=%async_computation.4 | async-start | bytes 524288 | tf_op jit(solution)/shard_map/all_to_all | solution.py:162
  111.5 0.1 unpack.1
  111.7 0.7 copy.22
  112.4 0.7 copy.23
  113.1 0.7 copy.24
  113.8 8.7 %all-to-all-done.4 = bf16[32,4,8,128]{3,2,1,0:T(8,128)(2,1)S(1)} async-done(((bf16[32,4,8,128]{3,2,1,0:T(8,128)(2,1)}), bf16[32,4,8,128]{3,2,1,0:T(8,128)(2,1)S(1)}, u32[]{:S(2)}, u32[]{:S(2)}) %all-to-all-start.4) | async-done | bytes 262176 | tf_op jit(solution)/shard_map/all_to_all | solution.py:162
  122.6 0.9 copy.21
  (8 shorter events, 0.2 us)
Async XLA Ops:
  0.6 25.2 %copy-start = (bf16[256,512]{1,0:T(8,128)(2,1)S(1)}, bf16[256,512]{1,0:T(8,128)(2,1)}, u32[]{:S(2)}) copy-start(bf16[256,512]{1,0:T(8,128)(2,1)} %param.12) | copy-start | bytes 786436
  2.3 13.9 %copy-start.2 = (bf16[64,2,256]{2,1,0:T(2,128)(2,1)S(1)}, bf16[64,2,256]{2,1,0:T(2,128)(2,1)}, u32[]{:S(2)}) copy-start(bf16[64,2,256]{2,1,0:T(2,128)(2,1)} %param.8) | copy-start | bytes 196612
  2.3 19.2 %all-to-all-start = ((bf16[8,64,128]{2,1,0:T(8,128)(2,1)}), bf16[8,64,128]{2,1,0:T(8,128)(2,1)S(1)}, u32[]{:S(2)}, u32[]{:S(2)}) async-start(bf16[8,64,128]{2,1,0:T(8,128)(2,1)} %bitcast.3), calls=%async_computation | async-start | bytes 262144 | tf_op jit(solution)/shard_map/all_to_all | solution.py:162
  16.3 0.9 copy-start.1
  17.2 0.7 copy-start.3
  21.6 22.8 %all-to-all-start.1 = ((bf16[8,64,640]{2,1,0:T(8,128)(2,1)}), bf16[8,64,640]{2,1,0:T(8,128)(2,1)S(1)}, u32[]{:S(2)}, u32[]{:S(2)}) async-start(bf16[8,64,640]{2,1,0:T(8,128)(2,1)} %bitcast.7), calls=%async_computation.1 | async-start | bytes 1310720 | tf_op jit(solution)/shard_map/all_to_all | solution.py:162
  107.7 14.8 %all-to-all-start.4 = ((bf16[32,4,8,128]{3,2,1,0:T(8,128)(2,1)}), bf16[32,4,8,128]{3,2,1,0:T(8,128)(2,1)S(1)}, u32[]{:S(2)}, u32[]{:S(2)}) async-start(bf16[32,4,8,128]{3,2,1,0:T(8,128)(2,1)} %broadcast_in_dim.4), calls=%async_computation.4 | async-start | bytes 524288 | tf_op jit(solution)/shard_map/all_to_all | solution.py:162

commit v6 on v5

v6 whole, which is shorter than its diff:
```python
import jax
import jax.numpy as jnp
from jax import lax
from jax.experimental import pallas as pl
from jax.experimental.pallas import tpu as pltpu
from jax.sharding import Mesh, PartitionSpec as P

HEAD_DIM = 64
BLK = 32
LANES = 128
LOG2E = 1.4426950408889634
BIG = 1e30
F32, BF16 = jnp.float32, jnp.bfloat16

PORT_AXES = ("x", "zh", "c")
TM_AXES = ("y", "zl")
NT = (((1,), (1,)), ((), ()))
NN = (((1,), (0,)), ((), ()))
TN = (((0,), (0,)), ((), ()))


def dot(a, b, dims):
    return lax.dot_general(a, b, dims, preferred_element_type=F32)


def low_half(rows):
    return lax.broadcasted_iota(jnp.int32, (rows, LANES), 1) < HEAD_DIM


def swap(a):
    return jnp.concatenate([a[:, HEAD_DIM:], a[:, :HEAD_DIM]], axis=1)


def pack_kv_kernel(k_ref, v_ref, out_ref):
    hours, ports, width = k_ref.shape
    low = low_half(ports)
    for h in range(hours):
        for t in range(width // LANES):
            cols = slice(t * LANES, (t + 1) * LANES)
            k, v = k_ref[h, :, cols].astype(F32), v_ref[h, :, cols].astype(F32)
            even = jnp.where(low, k, swap(v)).astype(BF16)
            odd = jnp.where(low, swap(k), v).astype(BF16)
            for z in range(out_ref.shape[1]):
                out_ref[2 * t, z, h] = even
                out_ref[2 * t + 1, z, h] = odd


def pack_qg_kernel(q_ref, g_ref, adj_ref, out_ref):
    hours, ports, width = q_ref.shape
    low = low_half(ports)
    bias = (adj_ref[...].astype(F32) - 1.0) * BIG
    bias = jnp.concatenate(
        [jnp.broadcast_to(bias[b : b + 1, :], (BLK, LANES)) for b in range(ports // BLK)], axis=0
    )
    for h in range(hours):
        for t in range(width // LANES):
            q = q_ref[h, :, t * LANES : (t + 1) * LANES].astype(F32)
            at = 2 * t * LANES
            out_ref[h, :, at : at + LANES] = jnp.where(low, q, bias).astype(BF16)
            out_ref[h, :, at + LANES : at + 2 * LANES] = jnp.where(low, swap(q), bias).astype(BF16)
        out_ref[h, :, 2 * width :] = g_ref[h]


def route_kernel(at_ref, qg_ref, *out_refs):
    heads = len(out_refs)
    hour = at_ref[1]
    for s, out_ref in enumerate(out_refs):
        n = lax.rem(at_ref[0] + s, heads)
        for c in range(qg_ref.shape[0]):
            out_ref[c, :, :LANES] = qg_ref[c, hour, :, pl.ds(pl.multiple_of(n * LANES, LANES), LANES)]
            out_ref[c, :, LANES:] = qg_ref[c, hour, :, heads * LANES :]


def attend_kernel(kv_ref, p0_ref, p1_ref, p2_ref, p3_ref, w_ref, out_ref, dq_ref, dw_ref, kx, kv, dkt, dvt):
    sources, ports, _ = kv_ref.shape
    total = sources * ports
    parts = (p0_ref, p1_ref, p2_ref, p3_ref)
    own = len(parts) * 2 * ports
    rows = 4 * ports
    part = kv_ref[...].reshape(total, LANES)
    lane = lax.broadcasted_iota(jnp.int32, (total, LANES), 1)
    block = lax.shift_right_logical(lax.broadcasted_iota(jnp.int32, (total, LANES), 0), 5)
    hot = jnp.where(lane - HEAD_DIM == block, 1.0, 0.0)
    kv[...] = part
    kx[...] = jnp.where(lane < HEAD_DIM, part.astype(F32), hot).astype(BF16)
    w_n = jnp.concatenate([jnp.zeros_like(w_ref), w_ref[...]], axis=0)
    scale2 = 0.125 * LOG2E
    low = low_half(rows)
    per = rows // ports
    dw = None
    for b in range(own // rows):
        mine = jnp.concatenate([parts[2 * b][...], parts[2 * b + 1][...]], axis=0)
        qx = mine[:, :, :LANES].reshape(rows, LANES)
        g = mine[:, :, LANES:].reshape(rows, -1)
        d = dot(g, w_n, NT).astype(BF16)
        s = dot(qx, kx[...], NT)
        top = jnp.max(s, axis=1, keepdims=True)
        e = jnp.exp2((s - top) * scale2)
        p = e * (1.0 / jnp.sum(e, axis=1, keepdims=True))
        p_low = p.astype(BF16)
        att = dot(p_low, kv[...], NN).astype(BF16)
        part = dot(att, g, TN)
        dw = part if dw is None else dw + part
        d32 = d.astype(F32)
        term = jnp.sum(d32 * att.astype(F32), axis=1, keepdims=True)
        dp = dot(d, kv[...], NT)
        ds = (p * (dp - term)).astype(BF16)
        dq = dot(ds, kv[...], NN) * 0.125
        qdt = jnp.where(low, qx.astype(F32), d32).T.astype(BF16)
        dk_part = dot(qdt[:HEAD_DIM], ds, NN)
        dv_part = dot(qdt[HEAD_DIM:], p_low, NN)
        if b:
            dkt[...] += dk_part
            dvt[...] += dv_part
        else:
            dkt[...] = dk_part
            dvt[...] = dv_part
        half = ports // 2
        for i in range(per):
            a, c = dq[i * ports : i * ports + half], dq[i * ports + half : (i + 1) * ports]
            dq_ref[i % 2, (b * per + i) // 2] = jnp.where(low_half(half), a, swap(c)).astype(BF16)
    dw = dw[HEAD_DIM:].astype(BF16)
    wide = dw.shape[1] // LANES
    for r in range(HEAD_DIM // 8):
        for c in range(wide):
            dw_ref[r * wide + c] = dw[r * 8 : (r + 1) * 8, c * LANES : (c + 1) * LANES]
    both = jnp.concatenate([dkt[...] * 0.125, dvt[...]], axis=0).T.astype(BF16)
    for i in range(sources):
        out_ref[i, :ports, :] = both[i * ports : (i + 1) * ports]
        out_ref[i, ports:, :] = jnp.zeros((8, LANES), BF16)


def unpack_kernel(x_ref, t_ref, d0_ref, d1_ref, d2_ref, d3_ref, q_ref, k_ref, v_ref, dq):
    hours, ports, width = q_ref.shape
    low = low_half(ports)
    half = ports // 2
    lh = low_half(half)
    for s, ref in enumerate((d0_ref, d1_ref, d2_ref, d3_ref)):
        dq[lax.rem(x_ref[0] + s, 4)] = ref[...]
    for h in range(hours):
        for t in range(width // LANES):
            sl = slice(t * LANES, (t + 1) * LANES)
            c, d = (
                sum(t_ref[n, z, h, :ports].astype(F32) for z in range(t_ref.shape[1])) for n in (2 * t, 2 * t + 1)
            )
            k_ref[h, :, sl] = jnp.where(low, c, swap(d)).astype(BF16)
            v_ref[h, :, sl] = jnp.where(low, swap(c), d).astype(BF16)
            a, b = (dq[n, h].astype(F32) for n in (2 * t, 2 * t + 1))
            q_ref[h, :half, sl] = jnp.where(lh, a, swap(b)).astype(BF16)
            q_ref[h, half:, sl] = jnp.where(lh, swap(a), b).astype(BF16)


def call(kernel, outs, *args, scratch=(), scalars=0, name):
    smem, vmem = pl.BlockSpec(memory_space=pltpu.SMEM), pl.BlockSpec(memory_space=pltpu.VMEM)
    return pl.pallas_call(
        kernel,
        out_shape=outs,
        in_specs=[smem] * scalars + [vmem] * (len(args) - scalars),
        out_specs=jax.tree.map(lambda _: vmem, outs),
        scratch_shapes=scratch,
        compiler_params=pltpu.CompilerParams(vmem_limit_bytes=40 * 1024 * 1024),
        name=name,
    )(*args)


def shape(*dims):
    return jax.ShapeDtypeStruct(dims, BF16)


def exchange(a, axes):
    return lax.all_to_all(a, axes, 0, 0, tiled=True)


def along_x(a, by):
    heads = lax.axis_size("x")
    return lax.ppermute(a, "x", [(i, (i + by) % heads) for i in range(heads)])


def per_device(query_rows, key_rows, value_rows, out_grad, out_weight, adjacency):
    parts = lax.axis_size("zh")
    heads, hours = lax.axis_size("x"), lax.axis_size("c")
    port_count = lax.axis_size(PORT_AXES)
    tm_count = lax.axis_size(TM_AXES)
    ports, _, width = query_rows.shape
    model = out_grad.shape[2]
    total = port_count * ports
    x, core = lax.axis_index("x"), lax.axis_index("c")
    q, k, v, g = (a.transpose(1, 0, 2) for a in (query_rows, key_rows, value_rows, out_grad))
    kv_send = call(pack_kv_kernel, shape(heads, parts, hours, ports, LANES), k, v, name="pack_kv")
    kv_got = exchange(kv_send.reshape(port_count, ports, LANES), PORT_AXES)
    adj = jnp.pad(adjacency, ((0, 0), (HEAD_DIM, LANES - HEAD_DIM - adjacency.shape[1])))
    qg = call(pack_qg_kernel, shape(hours, ports, heads * LANES + model), q, g, adj, name="pack_qg")
    qg = lax.all_gather(qg, "c")
    routed = call(
        route_kernel,
        (shape(hours, ports, LANES + model),) * heads,
        jnp.stack([x, core]),
        qg,
        scalars=1,
        name="route",
    )
    routed = [a if s == 0 else along_x(a, s) for s, a in enumerate(routed)]
    w_n = lax.dynamic_slice_in_dim(out_weight, x * HEAD_DIM, HEAD_DIM, 0)
    tiles = HEAD_DIM * model // (8 * LANES)
    chunk = ports + 8
    vec, acc = pltpu.VMEM((total, LANES), BF16), pltpu.VMEM((HEAD_DIM, total), F32)
    back, dq, dw = call(
        attend_kernel,
        (shape(port_count, chunk, LANES), shape(hours, heads, ports // 2, LANES), shape(tiles, 8, LANES)),
        kv_got,
        *routed,
        w_n,
        scratch=[vec, vec, acc, acc],
        name="attend",
    )
    dw = exchange(dw, TM_AXES)
    dw = jnp.sum(dw.astype(F32), axis=0).astype(BF16)
    dq = lax.dynamic_index_in_dim(lax.all_gather(dq, "c"), core, 1, keepdims=False)
    dq = [dq[:, s] if s == 0 else along_x(dq[:, s], heads - s) for s in range(heads)]
    back = back.at[:, chunk - 8 :, :].set(jnp.broadcast_to(dw, (port_count, 8, LANES)))
    back, dq = lax.optimization_barrier((exchange(back, PORT_AXES), dq))
    back = back.reshape(heads, parts, hours, chunk, LANES)
    dw = back[:, :, :, chunk - 8 :, :].astype(F32)
    dw = (jnp.sum(dw, axis=(1, 2)) * (1.0 / (hours * tm_count))).astype(BF16)
    dw = exchange(jnp.broadcast_to(dw, (tm_count, *dw.shape)), TM_AXES)
    dw = dw.transpose(1, 0, 2, 3).reshape(heads, HEAD_DIM // 8, model // LANES, 8, LANES)
    dw = dw.transpose(0, 1, 3, 2, 4).reshape(width, model).astype(F32)
    grads = call(
        unpack_kernel,
        (shape(hours, ports, width),) * 3,
        x.reshape(1),
        back,
        *dq,
        scratch=[pltpu.VMEM((heads, hours, ports // 2, LANES), BF16)],
        scalars=1,
        name="unpack",
    )
    return *(a.transpose(1, 0, 2) for a in grads), dw


def solution(mesh):
    fine = Mesh(mesh.devices.reshape(4, 3, 2, 8, 4), PORT_AXES + TM_AXES)
    rows = P(PORT_AXES, TM_AXES, None)
    return jax.shard_map(
        per_device,
        mesh=fine,
        in_specs=(rows, rows, rows, rows, P(), P(PORT_AXES, None)),
        out_specs=(rows, rows, rows, P()),
        check_vma=False,
    )
```

time: 125 us -> 116 us (0.928)
  blocking collectives: 77.2 us -> 25.5 us
  starting transfers between devices: 22.1 us -> 53.8 us
  waiting for transfers between devices: 11.4 us -> 21.1 us
    all_to_all x2 -> x1, blocking collectives: 58.7 us -> 21.5 us  [exchange(): return lax.all_to_all(a, axes, 0, 0, tiled=True)]
    ppermute x0 -> x6, starting transfers between devices: none -> 21.4 us  [along_x(): return lax.ppermute(a, 'x', [(i, (i + by) % heads) for i in range(heads)])]
    all_gather x1 -> x2, blocking collectives: 18.5 us -> 4.07 us  [the longest x1 2.17 us: per_device(): qg = lax.all_gather(qg, 'c')]
    all_to_all x3, starting transfers between devices: 22.1 us -> 32.4 us  [exchange(): return lax.all_to_all(a, axes, 0, 0, tiled=True)]
    ppermute x0 -> x6, waiting for transfers between devices: none -> 5.84 us  [along_x(): return lax.ppermute(a, 'x', [(i, (i + by) % heads) for i in range(heads)])]
    all_to_all x3, waiting for transfers between devices: 11.4 us -> 15.3 us  [exchange(): return lax.all_to_all(a, axes, 0, 0, tiled=True)]
    pallas_call x4 -> x5, Pallas kernels: 5.61 us -> 6.15 us  [call(): pl.pallas_call(kernel, out_shape=outs, in_specs=[smem] * scalars + [vmem]...]
  transfers between devices with their start and end apart: 3 -> 9, of which waited for: 2 -> 4; matrix products, arithmetic and copies ran while one was open for 2% -> 2% of each run, Pallas kernels for 1% -> 1%
where the time goes in v6:
time: 116 us; the launch traced here: 115 us
  starting transfers between devices  53.8 us (46%)
  blocking collectives  25.5 us (22%)
  waiting for transfers between devices  21.1 us (18%)
  local copies, waits for them, and re-layouts  6.91 us (6%)
  Pallas kernels  6.15 us (5%)
    all_to_all x3, starting transfers between devices, exchange(): return lax.all_to_all(a, axes, 0, 0, tiled=True)  32.4 us
    all_to_all x1, blocking collectives, exchange(): return lax.all_to_all(a, axes, 0, 0, tiled=True)  21.5 us
    ppermute x6, starting transfers between devices, along_x(): return lax.ppermute(a, 'x', [(i, (i + by) % heads) for i in range(heads)])  21.4 us
    all_to_all x3, waiting for transfers between devices, exchange(): return lax.all_to_all(a, axes, 0, 0, tiled=True)  15.3 us
    pallas_call x5, Pallas kernels, call(): pl.pallas_call(kernel, out_shape=outs, in_specs=[smem] * scalars + [vmem]...  6.15 us
    ppermute x6, waiting for transfers between devices, along_x(): return lax.ppermute(a, 'x', [(i, (i + by) % heads) for i in range(heads)])  5.84 us
    unnamed x13, local copies, waits for them, and re-layouts  3.65 us
  transfers between devices with their start and end apart: 9, of which 4 were waited for; matrix products, arithmetic and copies ran while one was open for 2% of the time, Pallas kernels for 1%

profile of v6, /device:TPU:1, one launch (start us, length us, event | category | flops | bytes accessed | tf_op | source)
XLA Modules:
  0.0 114.5 jit_solution(18331368522403825939)
XLA Ops:
  0.6 0.0 copy-start
  0.6 0.9 copy_bitcast_fusion.3
  1.6 0.9 pack_kv.1
  2.4 0.0 copy-start.2
  2.4 18.1 %all-to-all-start = ((bf16[24,64,128]{2,1,0:T(8,128)(2,1)}), bf16[24,64,128]{2,1,0:T(8,128)(2,1)S(1)}, u32[]{:S(2)}, u32[]{:S(2)}) async-start(bf16[24,64,128]{2,1,0:T(8,128)(2,1)} %bitcast.3), calls=%async_computation | async-start | bytes 786432 | tf_op jit(solution)/shard_map/all_to_all | solution.py:171
  20.5 0.0 copy-start.1
  20.5 0.0 copy-done.2
  20.6 0.9 copy-done.1
  21.4 0.0 copy-start.3
  21.5 0.7 copy-done.3
  22.1 0.1 pad.6.adj_ref
  22.2 0.1 pack_qg.1
  22.3 0.1 pad_add_fusion.at_ref
  22.4 2.2 %all-gather = bf16[4,64,1024]{2,1,0:T(8,128)(2,1)S(1)} all-gather(bf16[2,64,1024]{2,1,0:T(8,128)(2,1)S(1)} %pack_qg.1), channel_id=2, replica_groups=mesh['x'=4,'zh'=3,'c'=2,'y'=8,'zl'=4] {'c'}, dimensions={0}, use_global_device_ids=true | all-gather | bytes 786432 | tf_op jit(solution)/shard_map/all_gather | solution.py:193
  24.5 0.6 route.1
  25.1 3.3 %collective-permute-start = (bf16[2,64,640]{2,1,0:T(8,128)(2,1)S(1)}, bf16[2,64,640]{2,1,0:T(8,128)(2,1)S(1)}, u32[]{:S(2)}, u32[]{:S(2)}) collective-permute-start(bf16[2,64,640]{2,1,0:T(8,128)(2,1)S(1)} %get-tuple-element.32), channel_id=1, source_target_pairs={{0,192},{192,384},{384,576},{576,0},{1,193},{193,385},{385,577},{5... | collective-permute-start | bytes 491528 | tf_op jit(solution)/shard_map/ppermute | solution.py:176
  28.4 4.3 %collective-permute-start.1 = (bf16[2,64,640]{2,1,0:T(8,128)(2,1)S(1)}, bf16[2,64,640]{2,1,0:T(8,128)(2,1)S(1)}, u32[]{:S(2)}, u32[]{:S(2)}) collective-permute-start(bf16[2,64,640]{2,1,0:T(8,128)(2,1)S(1)} %get-tuple-element.33), channel_id=1, source_target_pairs={{0,384},{192,576},{384,0},{576,192},{1,385},{193,577},{385,1},{577... | collective-permute-start | bytes 491528 | tf_op jit(solution)/shard_map/ppermute | solution.py:176
  32.8 3.1 %collective-permute-start.2 = (bf16[2,64,640]{2,1,0:T(8,128)(2,1)S(1)}, bf16[2,64,640]{2,1,0:T(8,128)(2,1)S(1)}, u32[]{:S(2)}, u32[]{:S(2)}) collective-permute-start(bf16[2,64,640]{2,1,0:T(8,128)(2,1)S(1)} %get-tuple-element.34), channel_id=1, source_target_pairs={{0,576},{192,0},{384,192},{576,384},{1,577},{193,1},{385,193},{577... | collective-permute-start | bytes 491528 | tf_op jit(solution)/shard_map/ppermute | solution.py:176
  35.9 0.0 copy-done
  35.9 0.0 collective-permute-done.p1_ref
  35.9 4.2 %collective-permute-done.1.p2_ref = bf16[2,64,640]{2,1,0:T(8,128)(2,1)S(1)} collective-permute-done((bf16[2,64,640]{2,1,0:T(8,128)(2,1)S(1)}, bf16[2,64,640]{2,1,0:T(8,128)(2,1)S(1)}, u32[]{:S(2)}, u32[]{:S(2)}) %collective-permute-start.1) | collective-permute-done | bytes 163872 | tf_op jit(solution)/shard_map/ppermute | solution.py:176
  40.1 0.0 collective-permute-done.2.p3_ref
  40.1 0.0 all-to-all-done.kv_ref
  40.1 4.5 %attend.1 = (bf16[24,72,128]{2,1,0:T(8,128)(2,1)}, bf16[2,4,32,128]{3,2,1,0:T(8,128)(2,1)S(1)}, bf16[32,8,128]{2,1,0:T(8,128)(2,1)S(1)}) custom-call(bf16[24,64,128]{2,1,0:T(8,128)(2,1)S(1)} %all-to-all-done.kv_ref, bf16[2,64,640]{2,1,0:T(8,128)(2,1)S(1)} %get-tuple-element.31.p0_ref, bf16[2,64,640]{2,1,0:T(8,128)(2,1)S(1)} %collective-permute-done.p1_ref, ...), custom_call_target="tpu_custom_call" | custom-call | tf_op jit(solution)/shard_map/attend/pallas_call | solution.py:155
  44.5 21.5 %all_to_all.20 = bf16[32,8,128]{2,1,0:T(8,128)(2,1)S(1)} all-to-all(bf16[32,8,128]{2,1,0:T(8,128)(2,1)S(1)} %get-tuple-element.36), channel_id=1, replica_groups=mesh['x'=4,'zh'=3,'c'=2,'y'=8,'zl'=4] {'y','zl'}, dimensions={0} | all-to-all | bytes 131072 | tf_op jit(solution)/shard_map/all_to_all | solution.py:171
  66.1 0.6 broadcast_dynamic-update-slice_fusion
  66.7 10.4 %all-to-all-start.2 = ((bf16[24,72,128]{2,1,0:T(8,128)(2,1)}), bf16[24,72,128]{2,1,0:T(8,128)(2,1)S(1)}, u32[]{:S(2)}, u32[]{:S(2)}) async-start(bf16[24,72,128]{2,1,0:T(8,128)(2,1)} %broadcast_dynamic-update-slice_fusion), calls=%async_computation.2 | async-start | bytes 884736 | tf_op jit(solution)/shard_map/all_to_all | solution.py:171
  77.1 1.9 %all-gather.1 = bf16[4,4,32,128]{3,2,1,0:T(8,128)(2,1)S(1)} all-gather(bf16[2,4,32,128]{3,2,1,0:T(8,128)(2,1)S(1)} %get-tuple-element.37), channel_id=3, replica_groups=mesh['x'=4,'zh'=3,'c'=2,'y'=8,'zl'=4] {'c'}, dimensions={0}, use_global_device_ids=true | all-gather | bytes 196608 | tf_op jit(solution)/shard_map/all_gather | solution.py:218
  79.0 3.3 %collective-permute-start.5 = (bf16[2,32,128]{2,1,0:T(8,128)(2,1)S(1)}, bf16[2,32,128]{2,1,0:T(8,128)(2,1)S(1)}, u32[]{:S(2)}, u32[]{:S(2)}) collective-permute-start(bf16[2,32,128]{2,1,0:T(8,128)(2,1)S(1)} %get-tuple-element.54), channel_id=1, source_target_pairs={{0,192},{192,384},{384,576},{576,0},{1,193},{193,385},{385,577},{5... | collective-permute-start | bytes 49160 | tf_op jit(solution)/shard_map/ppermute | solution.py:176
  82.3 4.3 %collective-permute-start.4 = (bf16[2,32,128]{2,1,0:T(8,128)(2,1)S(1)}, bf16[2,32,128]{2,1,0:T(8,128)(2,1)S(1)}, u32[]{:S(2)}, u32[]{:S(2)}) collective-permute-start(bf16[2,32,128]{2,1,0:T(8,128)(2,1)S(1)} %get-tuple-element.55), channel_id=1, source_target_pairs={{0,384},{192,576},{384,0},{576,192},{1,385},{193,577},{385,1},{577... | collective-permute-start | bytes 49160 | tf_op jit(solution)/shard_map/ppermute | solution.py:176
  86.7 3.1 %collective-permute-start.3 = (bf16[2,32,128]{2,1,0:T(8,128)(2,1)S(1)}, bf16[2,32,128]{2,1,0:T(8,128)(2,1)S(1)}, u32[]{:S(2)}, u32[]{:S(2)}) collective-permute-start(bf16[2,32,128]{2,1,0:T(8,128)(2,1)S(1)} %get-tuple-element.56), channel_id=1, source_target_pairs={{0,576},{192,0},{384,192},{576,384},{1,577},{193,1},{385,193},{577... | collective-permute-start | bytes 49160 | tf_op jit(solution)/shard_map/ppermute | solution.py:176
  89.8 0.0 collective-permute-done.5.d3_ref
  89.8 0.0 collective-permute-done.4.d2_ref
  89.8 1.7 %collective-permute-done.3.d1_ref = bf16[2,32,128]{2,1,0:T(8,128)(2,1)S(1)} collective-permute-done((bf16[2,32,128]{2,1,0:T(8,128)(2,1)S(1)}, bf16[2,32,128]{2,1,0:T(8,128)(2,1)S(1)}, u32[]{:S(2)}, u32[]{:S(2)}) %collective-permute-start.3) | collective-permute-done | bytes 16416 | tf_op jit(solution)/shard_map/ppermute | solution.py:176
  91.4 6.5 %all-to-all-done.2 = bf16[24,72,128]{2,1,0:T(8,128)(2,1)S(1)} async-done(((bf16[24,72,128]{2,1,0:T(8,128)(2,1)}), bf16[24,72,128]{2,1,0:T(8,128)(2,1)S(1)}, u32[]{:S(2)}, u32[]{:S(2)}) %all-to-all-start.2) | async-done | bytes 442400 | tf_op jit(solution)/shard_map/all_to_all | solution.py:171
  97.9 0.7 broadcast_in_dim.4
  98.7 3.9 %all-to-all-start.3 = ((bf16[32,4,8,128]{3,2,1,0:T(8,128)(2,1)}), bf16[32,4,8,128]{3,2,1,0:T(8,128)(2,1)S(1)}, u32[]{:S(2)}, u32[]{:S(2)}) async-start(bf16[32,4,8,128]{3,2,1,0:T(8,128)(2,1)} %broadcast_in_dim.4), calls=%async_computation.3 | async-start | bytes 524288 | tf_op jit(solution)/shard_map/all_to_all | solution.py:171
  102.5 0.1 unpack.1
  102.7 0.7 copy.24
  103.4 0.7 copy.25
  104.1 0.7 copy.26
  104.8 8.8 %all-to-all-done.3 = bf16[32,4,8,128]{3,2,1,0:T(8,128)(2,1)S(1)} async-done(((bf16[32,4,8,128]{3,2,1,0:T(8,128)(2,1)}), bf16[32,4,8,128]{3,2,1,0:T(8,128)(2,1)S(1)}, u32[]{:S(2)}, u32[]{:S(2)}) %all-to-all-start.3) | async-done | bytes 262176 | tf_op jit(solution)/shard_map/all_to_all | solution.py:171
  113.7 0.9 copy.23
  (9 shorter events, 0.2 us)
Async XLA Ops:
  0.6 35.2 %copy-start = (bf16[256,512]{1,0:T(8,128)(2,1)S(1)}, bf16[256,512]{1,0:T(8,128)(2,1)}, u32[]{:S(2)}) copy-start(bf16[256,512]{1,0:T(8,128)(2,1)} %param.12) | copy-start | bytes 786436
  2.4 18.1 %copy-start.2 = (bf16[64,2,256]{2,1,0:T(2,128)(2,1)S(1)}, bf16[64,2,256]{2,1,0:T(2,128)(2,1)}, u32[]{:S(2)}) copy-start(bf16[64,2,256]{2,1,0:T(2,128)(2,1)} %param.8) | copy-start | bytes 196612
  2.4 37.6 %all-to-all-start = ((bf16[24,64,128]{2,1,0:T(8,128)(2,1)}), bf16[24,64,128]{2,1,0:T(8,128)(2,1)S(1)}, u32[]{:S(2)}, u32[]{:S(2)}) async-start(bf16[24,64,128]{2,1,0:T(8,128)(2,1)} %bitcast.3), calls=%async_computation | async-start | bytes 786432 | tf_op jit(solution)/shard_map/all_to_all | solution.py:171
  20.5 0.9 copy-start.1
  21.4 0.7 copy-start.3
  25.1 10.8 %collective-permute-start = (bf16[2,64,640]{2,1,0:T(8,128)(2,1)S(1)}, bf16[2,64,640]{2,1,0:T(8,128)(2,1)S(1)}, u32[]{:S(2)}, u32[]{:S(2)}) collective-permute-start(bf16[2,64,640]{2,1,0:T(8,128)(2,1)S(1)} %get-tuple-element.32), channel_id=1, source_target_pairs={{0,192},{192,384},{384,576},{576,0},{1,193},{193,385},{385,577},{5... | collective-permute-start | bytes 491528 | tf_op jit(solution)/shard_map/ppermute | solution.py:176
  28.4 11.6 %collective-permute-start.1 = (bf16[2,64,640]{2,1,0:T(8,128)(2,1)S(1)}, bf16[2,64,640]{2,1,0:T(8,128)(2,1)S(1)}, u32[]{:S(2)}, u32[]{:S(2)}) collective-permute-start(bf16[2,64,640]{2,1,0:T(8,128)(2,1)S(1)} %get-tuple-element.33), channel_id=1, source_target_pairs={{0,384},{192,576},{384,0},{576,192},{1,385},{193,577},{385,1},{577... | collective-permute-start | bytes 491528 | tf_op jit(solution)/shard_map/ppermute | solution.py:176
  32.8 7.3 %collective-permute-start.2 = (bf16[2,64,640]{2,1,0:T(8,128)(2,1)S(1)}, bf16[2,64,640]{2,1,0:T(8,128)(2,1)S(1)}, u32[]{:S(2)}, u32[]{:S(2)}) collective-permute-start(bf16[2,64,640]{2,1,0:T(8,128)(2,1)S(1)} %get-tuple-element.34), channel_id=1, source_target_pairs={{0,576},{192,0},{384,192},{576,384},{1,577},{193,1},{385,193},{577... | collective-permute-start | bytes 491528 | tf_op jit(solution)/shard_map/ppermute | solution.py:176
  66.7 31.2 %all-to-all-start.2 = ((bf16[24,72,128]{2,1,0:T(8,128)(2,1)}), bf16[24,72,128]{2,1,0:T(8,128)(2,1)S(1)}, u32[]{:S(2)}, u32[]{:S(2)}) async-start(bf16[24,72,128]{2,1,0:T(8,128)(2,1)} %broadcast_dynamic-update-slice_fusion), calls=%async_computation.2 | async-start | bytes 884736 | tf_op jit(solution)/shard_map/all_to_all | solution.py:171
  79.0 10.7 %collective-permute-start.5 = (bf16[2,32,128]{2,1,0:T(8,128)(2,1)S(1)}, bf16[2,32,128]{2,1,0:T(8,128)(2,1)S(1)}, u32[]{:S(2)}, u32[]{:S(2)}) collective-permute-start(bf16[2,32,128]{2,1,0:T(8,128)(2,1)S(1)} %get-tuple-element.54), channel_id=1, source_target_pairs={{0,192},{192,384},{384,576},{576,0},{1,193},{193,385},{385,577},{5... | collective-permute-start | bytes 49160 | tf_op jit(solution)/shard_map/ppermute | solution.py:176
  82.3 7.4 %collective-permute-start.4 = (bf16[2,32,128]{2,1,0:T(8,128)(2,1)S(1)}, bf16[2,32,128]{2,1,0:T(8,128)(2,1)S(1)}, u32[]{:S(2)}, u32[]{:S(2)}) collective-permute-start(bf16[2,32,128]{2,1,0:T(8,128)(2,1)S(1)} %get-tuple-element.55), channel_id=1, source_target_pairs={{0,384},{192,576},{384,0},{576,192},{1,385},{193,577},{385,1},{577... | collective-permute-start | bytes 49160 | tf_op jit(solution)/shard_map/ppermute | solution.py:176
  86.7 4.8 %collective-permute-start.3 = (bf16[2,32,128]{2,1,0:T(8,128)(2,1)S(1)}, bf16[2,32,128]{2,1,0:T(8,128)(2,1)S(1)}, u32[]{:S(2)}, u32[]{:S(2)}) collective-permute-start(bf16[2,32,128]{2,1,0:T(8,128)(2,1)S(1)} %get-tuple-element.56), channel_id=1, source_target_pairs={{0,576},{192,0},{384,192},{576,384},{1,577},{193,1},{385,193},{577... | collective-permute-start | bytes 49160 | tf_op jit(solution)/shard_map/ppermute | solution.py:176
  98.7 14.9 %all-to-all-start.3 = ((bf16[32,4,8,128]{3,2,1,0:T(8,128)(2,1)}), bf16[32,4,8,128]{3,2,1,0:T(8,128)(2,1)S(1)}, u32[]{:S(2)}, u32[]{:S(2)}) async-start(bf16[32,4,8,128]{3,2,1,0:T(8,128)(2,1)} %broadcast_in_dim.4), calls=%async_computation.3 | async-start | bytes 524288 | tf_op jit(solution)/shard_map/all_to_all | solution.py:171

commit v7 on v6

--- a/solution.py
+++ b/solution.py
@@ -125,27 +125,35 @@
         for c in range(wide):
             dw_ref[r * wide + c] = dw[r * 8 : (r + 1) * 8, c * LANES : (c + 1) * LANES]
     both = jnp.concatenate([dkt[...] * 0.125, dvt[...]], axis=0).T.astype(BF16)
-    for i in range(sources):
-        out_ref[i, :ports, :] = both[i * ports : (i + 1) * ports]
-        out_ref[i, ports:, :] = jnp.zeros((8, LANES), BF16)
-
-
-def unpack_kernel(x_ref, t_ref, d0_ref, d1_ref, d2_ref, d3_ref, q_ref, k_ref, v_ref, dq):
+    thirds, pair = out_ref.shape[0], 2 * ports
+    for i in range(sources // 2):
+        at = (i // thirds) * pair
+        out_ref[i % thirds, at : at + pair, :] = both[i * pair : (i + 1) * pair]
+
+
+def merge_kernel(x_ref, kv_ref, dq_ref, out_ref):
+    heads, cores, ports, _ = kv_ref.shape
+    for s in range(heads):
+        to = lax.rem(x_ref[0] + heads - s, heads)
+        for c in range(cores):
+            out_ref[s, c, :ports, :] = kv_ref[to, c]
+            out_ref[s, c, ports:, :] = dq_ref[c, s]
+
+
+def unpack_kernel(x_ref, d0_ref, d1_ref, d2_ref, d3_ref, q_ref, k_ref, v_ref, all_ref):
     hours, ports, width = q_ref.shape
     low = low_half(ports)
     half = ports // 2
     lh = low_half(half)
     for s, ref in enumerate((d0_ref, d1_ref, d2_ref, d3_ref)):
-        dq[lax.rem(x_ref[0] + s, 4)] = ref[...]
+        all_ref[lax.rem(x_ref[0] + s, 4)] = ref[...]
     for h in range(hours):
         for t in range(width // LANES):
             sl = slice(t * LANES, (t + 1) * LANES)
-            c, d = (
-                sum(t_ref[n, z, h, :ports].astype(F32) for z in range(t_ref.shape[1])) for n in (2 * t, 2 * t + 1)
-            )
+            c, d = (all_ref[n, h, :ports].astype(F32) for n in (2 * t, 2 * t + 1))
             k_ref[h, :, sl] = jnp.where(low, c, swap(d)).astype(BF16)
             v_ref[h, :, sl] = jnp.where(low, swap(c), d).astype(BF16)
-            a, b = (dq[n, h].astype(F32) for n in (2 * t, 2 * t + 1))
+            a, b = (all_ref[n, h, ports:].astype(F32) for n in (2 * t, 2 * t + 1))
             q_ref[h, :half, sl] = jnp.where(lh, a, swap(b)).astype(BF16)
             q_ref[h, half:, sl] = jnp.where(lh, swap(a), b).astype(BF16)
 
@@ -202,11 +210,11 @@
     routed = [a if s == 0 else along_x(a, s) for s, a in enumerate(routed)]
     w_n = lax.dynamic_slice_in_dim(out_weight, x * HEAD_DIM, HEAD_DIM, 0)
     tiles = HEAD_DIM * model // (8 * LANES)
-    chunk = ports + 8
+    rows = ports + ports // 2
     vec, acc = pltpu.VMEM((total, LANES), BF16), pltpu.VMEM((HEAD_DIM, total), F32)
-    back, dq, dw = call(
+    dkv, dq, dw = call(
         attend_kernel,
-        (shape(port_count, chunk, LANES), shape(hours, heads, ports // 2, LANES), shape(tiles, 8, LANES)),
+        (shape(parts, total // parts, LANES), shape(hours, heads, ports // 2, LANES), shape(tiles, 8, LANES)),
         kv_got,
         *routed,
         w_n,
@@ -215,23 +223,31 @@
     )
     dw = exchange(dw, TM_AXES)
     dw = jnp.sum(dw.astype(F32), axis=0).astype(BF16)
-    dq = lax.dynamic_index_in_dim(lax.all_gather(dq, "c"), core, 1, keepdims=False)
-    dq = [dq[:, s] if s == 0 else along_x(dq[:, s], heads - s) for s in range(heads)]
-    back = back.at[:, chunk - 8 :, :].set(jnp.broadcast_to(dw, (port_count, 8, LANES)))
-    back, dq = lax.optimization_barrier((exchange(back, PORT_AXES), dq))
-    back = back.reshape(heads, parts, hours, chunk, LANES)
-    dw = back[:, :, :, chunk - 8 :, :].astype(F32)
+    dkv = lax.psum_scatter(dkv.reshape(total, LANES), "zh", scatter_dimension=0, tiled=True)
+    dw = exchange(jnp.broadcast_to(dw, (port_count, 8, LANES)), PORT_AXES)
+    dw, dq = lax.optimization_barrier((dw, dq))
+    dw = dw.reshape(heads, parts, hours, 8, LANES).astype(F32)
     dw = (jnp.sum(dw, axis=(1, 2)) * (1.0 / (hours * tm_count))).astype(BF16)
     dw = exchange(jnp.broadcast_to(dw, (tm_count, *dw.shape)), TM_AXES)
     dw = dw.transpose(1, 0, 2, 3).reshape(heads, HEAD_DIM // 8, model // LANES, 8, LANES)
     dw = dw.transpose(0, 1, 3, 2, 4).reshape(width, model).astype(F32)
+    both = call(
+        merge_kernel,
+        shape(heads, hours, rows, LANES),
+        x.reshape(1),
+        dkv.reshape(heads, hours, ports, LANES),
+        dq,
+        scalars=1,
+        name="merge",
+    )
+    both = lax.dynamic_index_in_dim(lax.all_gather(both, "c"), core, 2, keepdims=False)
+    both = [both[:, s] if s == 0 else along_x(both[:, s], heads - s) for s in range(heads)]
     grads = call(
         unpack_kernel,
         (shape(hours, ports, width),) * 3,
         x.reshape(1),
-        back,
-        *dq,
-        scratch=[pltpu.VMEM((heads, hours, ports // 2, LANES), BF16)],
+        *both,
+        scratch=[pltpu.VMEM((heads, hours, rows, LANES), BF16)],
         scalars=1,
         name="unpack",
     )

time: 116 us -> 134 us (1.16)
  the two profiles are of different devices: /device:TPU:1 before, /device:TPU:104 now
where the time goes in v7:
time: 134 us
  starting transfers between devices  59.5 us (44%)
  waiting for transfers between devices  23.3 us (17%)
  blocking collectives  23 us (17%)
  between operations  14.2 us (11%)
  local copies, waits for them, and re-layouts  7.16 us (5%)
  Pallas kernels  6.14 us (5%)
    all_to_all x3, starting transfers between devices, exchange(): return lax.all_to_all(a, axes, 0, 0, tiled=True)  36.1 us
    ppermute x6, starting transfers between devices, along_x(): return lax.ppermute(a, 'x', [(i, (i + by) % heads) for i in range(heads)])  23.4 us
    all_to_all x1, blocking collectives, exchange(): return lax.all_to_all(a, axes, 0, 0, tiled=True)  18.8 us
    ppermute x6, waiting for transfers between devices, along_x(): return lax.ppermute(a, 'x', [(i, (i + by) % heads) for i in range(heads)])  9.25 us
    reduce_scatter x1, waiting for transfers between devices, per_device(): lax.psum_scatter(dkv.reshape(total, LANES), 'zh', scatter_dimension=0, ti...  8.78 us
    pallas_call x6, Pallas kernels, call(): pl.pallas_call(kernel, out_shape=outs, in_specs=[smem] * scalars + [vmem]...  6.14 us
    all_to_all x3, waiting for transfers between devices, exchange(): return lax.all_to_all(a, axes, 0, 0, tiled=True)  4.54 us
    unnamed x15, local copies, waits for them, and re-layouts  4.51 us
  transfers between devices with their start and end apart: 10, of which 5 were waited for; matrix products, arithmetic and copies ran while one was open for 2% of the time, Pallas kernels for 1%

profile of v7, /device:TPU:104, one launch (start us, length us, event | category | flops | bytes accessed | tf_op | source)
XLA Modules:
  0.0 133.6 jit_solution(17103515147624966990)
XLA Ops:
  7.2 0.0 copy-start
  7.2 0.9 copy_bitcast_fusion.3
  8.1 0.9 pack_kv.1
  9.0 0.0 copy-start.2
  9.0 15.9 %all-to-all-start = ((bf16[24,64,128]{2,1,0:T(8,128)(2,1)}), bf16[24,64,128]{2,1,0:T(8,128)(2,1)S(1)}, u32[]{:S(2)}, u32[]{:S(2)}) async-start(bf16[24,64,128]{2,1,0:T(8,128)(2,1)} %bitcast.3), calls=%async_computation | async-start | bytes 786432 | tf_op jit(solution)/shard_map/all_to_all | solution.py:179
  24.8 0.0 copy-done.2
  24.9 0.0 copy-start.3
  24.9 0.8 copy-done.3
  25.7 0.0 copy-start.4
  25.7 0.7 copy-done.4
  26.4 0.1 pad.4.adj_ref
  26.5 0.1 pack_qg.1
  26.5 0.1 pad_add_fusion.at_ref
  26.6 2.2 %all-gather = bf16[4,64,1024]{2,1,0:T(8,128)(2,1)S(1)} all-gather(bf16[2,64,1024]{2,1,0:T(8,128)(2,1)S(1)} %pack_qg.1), channel_id=2, replica_groups=mesh['x'=4,'zh'=3,'c'=2,'y'=8,'zl'=4] {'c'}, dimensions={0}, use_global_device_ids=true | all-gather | bytes 786432 | tf_op jit(solution)/shard_map/all_gather | solution.py:201
  28.8 0.6 route.1
  29.4 3.8 %collective-permute-start = (bf16[2,64,640]{2,1,0:T(8,128)(2,1)S(1)}, bf16[2,64,640]{2,1,0:T(8,128)(2,1)S(1)}, u32[]{:S(2)}, u32[]{:S(2)}) collective-permute-start(bf16[2,64,640]{2,1,0:T(8,128)(2,1)S(1)} %get-tuple-element.17), channel_id=1, source_target_pairs={{0,192},{192,384},{384,576},{576,0},{1,193},{193,385},{385,577},{5... | collective-permute-start | bytes 491528 | tf_op jit(solution)/shard_map/ppermute | solution.py:184
  33.2 4.6 %collective-permute-start.1 = (bf16[2,64,640]{2,1,0:T(8,128)(2,1)S(1)}, bf16[2,64,640]{2,1,0:T(8,128)(2,1)S(1)}, u32[]{:S(2)}, u32[]{:S(2)}) collective-permute-start(bf16[2,64,640]{2,1,0:T(8,128)(2,1)S(1)} %get-tuple-element.18), channel_id=1, source_target_pairs={{0,384},{192,576},{384,0},{576,192},{1,385},{193,577},{385,1},{577... | collective-permute-start | bytes 491528 | tf_op jit(solution)/shard_map/ppermute | solution.py:184
  37.8 3.4 %collective-permute-start.2 = (bf16[2,64,640]{2,1,0:T(8,128)(2,1)S(1)}, bf16[2,64,640]{2,1,0:T(8,128)(2,1)S(1)}, u32[]{:S(2)}, u32[]{:S(2)}) collective-permute-start(bf16[2,64,640]{2,1,0:T(8,128)(2,1)S(1)} %get-tuple-element.19), channel_id=1, source_target_pairs={{0,576},{192,0},{384,192},{576,384},{1,577},{193,1},{385,193},{577... | collective-permute-start | bytes 491528 | tf_op jit(solution)/shard_map/ppermute | solution.py:184
  41.1 0.0 copy-done
  41.2 0.0 collective-permute-done.p1_ref
  41.2 4.8 %collective-permute-done.1.p2_ref = bf16[2,64,640]{2,1,0:T(8,128)(2,1)S(1)} collective-permute-done((bf16[2,64,640]{2,1,0:T(8,128)(2,1)S(1)}, bf16[2,64,640]{2,1,0:T(8,128)(2,1)S(1)}, u32[]{:S(2)}, u32[]{:S(2)}) %collective-permute-start.1) | collective-permute-done | bytes 163872 | tf_op jit(solution)/shard_map/ppermute | solution.py:184
  46.0 0.0 collective-permute-done.2.p3_ref
  46.0 0.0 all-to-all-done.kv_ref
  46.0 4.4 %attend.1 = (bf16[3,512,128]{2,1,0:T(8,128)(2,1)}, bf16[2,4,32,128]{3,2,1,0:T(8,128)(2,1)S(1)}, bf16[32,8,128]{2,1,0:T(8,128)(2,1)}) custom-call(bf16[24,64,128]{2,1,0:T(8,128)(2,1)S(1)} %all-to-all-done.kv_ref, bf16[2,64,640]{2,1,0:T(8,128)(2,1)S(1)} %get-tuple-element.16.p0_ref, bf16[2,64,640]{2,1,0:T(8,128)(2,1)S(1)} %collective-permute-done.p1_ref, ...), custom_call_target="tpu_custom_call" | custom-call | tf_op jit(solution)/shard_map/attend/pallas_call | solution.py:163
  50.4 11.2 %all-to-all-start.1 = ((bf16[32,8,128]{2,1,0:T(8,128)(2,1)}), bf16[32,8,128]{2,1,0:T(8,128)(2,1)S(1)}, u32[]{:S(2)}, u32[]{:S(2)}) async-start(bf16[32,8,128]{2,1,0:T(8,128)(2,1)} %get-tuple-element.21), calls=%async_computation.2 | async-start | bytes 131072 | tf_op jit(solution)/shard_map/all_to_all | solution.py:179
  61.6 0.0 reduce-scatter.2.cloned.1.call-start
  61.7 0.7 reduce-scatter.2.cloned.1.call-update
  62.4 4.5 %all-to-all-done.1 = bf16[32,8,128]{2,1,0:T(8,128)(2,1)S(1)} async-done(((bf16[32,8,128]{2,1,0:T(8,128)(2,1)}), bf16[32,8,128]{2,1,0:T(8,128)(2,1)S(1)}, u32[]{:S(2)}, u32[]{:S(2)}) %all-to-all-start.1) | async-done | bytes 65568 | tf_op jit(solution)/shard_map/all_to_all | solution.py:179
  67.0 18.8 %all_to_all.20 = bf16[24,8,128]{2,1,0:T(8,128)(2,1)S(1)} all-to-all(bf16[24,8,128]{2,1,0:T(8,128)(2,1)S(1)} %broadcast_in_dim.6), channel_id=1, replica_groups=mesh['x'=4,'zh'=3,'c'=2,'y'=8,'zl'=4] {'x','zh','c'}, dimensions={0} | all-to-all | bytes 98304 | tf_op jit(solution)/shard_map/all_to_all | solution.py:179
  85.8 0.7 broadcast_in_dim.7
  86.5 9.1 %all-to-all-start.3 = ((bf16[32,4,8,128]{3,2,1,0:T(8,128)(2,1)}), bf16[32,4,8,128]{3,2,1,0:T(8,128)(2,1)S(1)}, u32[]{:S(2)}, u32[]{:S(2)}) async-start(bf16[32,4,8,128]{3,2,1,0:T(8,128)(2,1)} %broadcast_in_dim.7), calls=%async_computation.4 | async-start | bytes 524288 | tf_op jit(solution)/shard_map/all_to_all | solution.py:179
  95.6 8.8 %reduce-scatter.2.cloned.1.call-done = bf16[512,128]{1,0:T(8,128)(2,1)} async-done(((bf16[1536,128]{1,0:T(8,128)(2,1)}), bf16[512,128]{1,0:T(8,128)(2,1)}) %reduce-scatter.2.cloned.1.call-update) | async-done | bytes 131088 | tf_op jit(solution)/shard_map/reduce_scatter | solution.py:226
  104.4 0.0 copy-start.1
  104.4 0.9 copy-done.1
  105.3 2.1 %all-gather.1 = bf16[8,2,96,128]{3,2,1,0:T(8,128)(2,1)S(1)} all-gather(bf16[4,2,96,128]{3,2,1,0:T(8,128)(2,1)S(1)} %merge.1), channel_id=3, replica_groups=mesh['x'=4,'zh'=3,'c'=2,'y'=8,'zl'=4] {'c'}, dimensions={0}, use_global_device_ids=true | all-gather | bytes 589824 | tf_op jit(solution)/shard_map/all_gather | solution.py:243
  107.4 6.2 %collective-permute-start.3 = (bf16[2,96,128]{2,1,0:T(8,128)(2,1)S(1)}, bf16[2,96,128]{2,1,0:T(8,128)(2,1)S(1)}, u32[]{:S(2)}, u32[]{:S(2)}) collective-permute-start(bf16[2,96,128]{2,1,0:T(8,128)(2,1)S(1)} %get-tuple-element.42), channel_id=1, source_target_pairs={{0,576},{192,0},{384,192},{576,384},{1,577},{193,1},{385,193},{577... | collective-permute-start | bytes 147464 | tf_op jit(solution)/shard_map/ppermute | solution.py:184
  113.6 2.7 %collective-permute-start.4 = (bf16[2,96,128]{2,1,0:T(8,128)(2,1)S(1)}, bf16[2,96,128]{2,1,0:T(8,128)(2,1)S(1)}, u32[]{:S(2)}, u32[]{:S(2)}) collective-permute-start(bf16[2,96,128]{2,1,0:T(8,128)(2,1)S(1)} %get-tuple-element.41), channel_id=1, source_target_pairs={{0,384},{192,576},{384,0},{576,192},{1,385},{193,577},{385,1},{577... | collective-permute-start | bytes 147464 | tf_op jit(solution)/shard_map/ppermute | solution.py:184
  116.3 2.7 %collective-permute-start.5 = (bf16[2,96,128]{2,1,0:T(8,128)(2,1)S(1)}, bf16[2,96,128]{2,1,0:T(8,128)(2,1)S(1)}, u32[]{:S(2)}, u32[]{:S(2)}) collective-permute-start(bf16[2,96,128]{2,1,0:T(8,128)(2,1)S(1)} %get-tuple-element.40), channel_id=1, source_target_pairs={{0,192},{192,384},{384,576},{576,0},{1,193},{193,385},{385,577},{5... | collective-permute-start | bytes 147464 | tf_op jit(solution)/shard_map/ppermute | solution.py:184
  119.1 0.0 collective-permute-done.3.d1_ref
  119.1 2.0 %collective-permute-done.4.d2_ref = bf16[2,96,128]{2,1,0:T(8,128)(2,1)S(1)} collective-permute-done((bf16[2,96,128]{2,1,0:T(8,128)(2,1)S(1)}, bf16[2,96,128]{2,1,0:T(8,128)(2,1)S(1)}, u32[]{:S(2)}, u32[]{:S(2)}) %collective-permute-start.4) | collective-permute-done | bytes 49184 | tf_op jit(solution)/shard_map/ppermute | solution.py:184
  121.1 2.4 %collective-permute-done.5.d3_ref = bf16[2,96,128]{2,1,0:T(8,128)(2,1)S(1)} collective-permute-done((bf16[2,96,128]{2,1,0:T(8,128)(2,1)S(1)}, bf16[2,96,128]{2,1,0:T(8,128)(2,1)S(1)}, u32[]{:S(2)}, u32[]{:S(2)}) %collective-permute-start.5) | collective-permute-done | bytes 49184 | tf_op jit(solution)/shard_map/ppermute | solution.py:184
  123.5 0.1 unpack.1
  123.7 0.7 copy.33
  124.4 0.7 copy.34
  125.1 0.7 copy.35
  125.8 0.0 all-to-all-done.3
  125.8 0.1 convert_element_type.38
  125.8 0.9 copy.32
  (10 shorter events, 0.1 us)
Async XLA Ops:
  7.2 34.0 %copy-start = (bf16[256,512]{1,0:T(8,128)(2,1)S(1)}, bf16[256,512]{1,0:T(8,128)(2,1)}, u32[]{:S(2)}) copy-start(bf16[256,512]{1,0:T(8,128)(2,1)} %param.10) | copy-start | bytes 786436
  9.0 15.9 %copy-start.2 = (bf16[64,2,512]{2,1,0:T(2,128)(2,1)S(1)}, bf16[64,2,512]{2,1,0:T(2,128)(2,1)}, u32[]{:S(2)}) copy-start(bf16[64,2,512]{2,1,0:T(2,128)(2,1)} %param.9) | copy-start | bytes 393220
  9.0 37.0 %all-to-all-start = ((bf16[24,64,128]{2,1,0:T(8,128)(2,1)}), bf16[24,64,128]{2,1,0:T(8,128)(2,1)S(1)}, u32[]{:S(2)}, u32[]{:S(2)}) async-start(bf16[24,64,128]{2,1,0:T(8,128)(2,1)} %bitcast.3), calls=%async_computation | async-start | bytes 786432 | tf_op jit(solution)/shard_map/all_to_all | solution.py:179
  24.9 0.8 copy-start.3
  25.7 0.7 copy-start.4
  29.4 11.8 %collective-permute-start = (bf16[2,64,640]{2,1,0:T(8,128)(2,1)S(1)}, bf16[2,64,640]{2,1,0:T(8,128)(2,1)S(1)}, u32[]{:S(2)}, u32[]{:S(2)}) collective-permute-start(bf16[2,64,640]{2,1,0:T(8,128)(2,1)S(1)} %get-tuple-element.17), channel_id=1, source_target_pairs={{0,192},{192,384},{384,576},{576,0},{1,193},{193,385},{385,577},{5... | collective-permute-start | bytes 491528 | tf_op jit(solution)/shard_map/ppermute | solution.py:184
  33.2 12.8 %collective-permute-start.1 = (bf16[2,64,640]{2,1,0:T(8,128)(2,1)S(1)}, bf16[2,64,640]{2,1,0:T(8,128)(2,1)S(1)}, u32[]{:S(2)}, u32[]{:S(2)}) collective-permute-start(bf16[2,64,640]{2,1,0:T(8,128)(2,1)S(1)} %get-tuple-element.18), channel_id=1, source_target_pairs={{0,384},{192,576},{384,0},{576,192},{1,385},{193,577},{385,1},{577... | collective-permute-start | bytes 491528 | tf_op jit(solution)/shard_map/ppermute | solution.py:184
  37.8 8.2 %collective-permute-start.2 = (bf16[2,64,640]{2,1,0:T(8,128)(2,1)S(1)}, bf16[2,64,640]{2,1,0:T(8,128)(2,1)S(1)}, u32[]{:S(2)}, u32[]{:S(2)}) collective-permute-start(bf16[2,64,640]{2,1,0:T(8,128)(2,1)S(1)} %get-tuple-element.19), channel_id=1, source_target_pairs={{0,576},{192,0},{384,192},{576,384},{1,577},{193,1},{385,193},{577... | collective-permute-start | bytes 491528 | tf_op jit(solution)/shard_map/ppermute | solution.py:184
  50.4 16.5 %all-to-all-start.1 = ((bf16[32,8,128]{2,1,0:T(8,128)(2,1)}), bf16[32,8,128]{2,1,0:T(8,128)(2,1)S(1)}, u32[]{:S(2)}, u32[]{:S(2)}) async-start(bf16[32,8,128]{2,1,0:T(8,128)(2,1)} %get-tuple-element.21), calls=%async_computation.2 | async-start | bytes 131072 | tf_op jit(solution)/shard_map/all_to_all | solution.py:179
  61.6 42.7 %reduce-scatter.2.cloned.1.call-start = ((), (), s32[]{:S(2)}) async-start(), calls=%async_computation.5 | async-start | bytes 524288 | tf_op jit(solution)/shard_map/reduce_scatter | solution.py:226
  86.5 39.3 %all-to-all-start.3 = ((bf16[32,4,8,128]{3,2,1,0:T(8,128)(2,1)}), bf16[32,4,8,128]{3,2,1,0:T(8,128)(2,1)S(1)}, u32[]{:S(2)}, u32[]{:S(2)}) async-start(bf16[32,4,8,128]{3,2,1,0:T(8,128)(2,1)} %broadcast_in_dim.7), calls=%async_computation.4 | async-start | bytes 524288 | tf_op jit(solution)/shard_map/all_to_all | solution.py:179
  104.4 0.9 copy-start.1
  107.4 11.7 %collective-permute-start.3 = (bf16[2,96,128]{2,1,0:T(8,128)(2,1)S(1)}, bf16[2,96,128]{2,1,0:T(8,128)(2,1)S(1)}, u32[]{:S(2)}, u32[]{:S(2)}) collective-permute-start(bf16[2,96,128]{2,1,0:T(8,128)(2,1)S(1)} %get-tuple-element.42), channel_id=1, source_target_pairs={{0,576},{192,0},{384,192},{576,384},{1,577},{193,1},{385,193},{577... | collective-permute-start | bytes 147464 | tf_op jit(solution)/shard_map/ppermute | solution.py:184
  113.6 7.5 %collective-permute-start.4 = (bf16[2,96,128]{2,1,0:T(8,128)(2,1)S(1)}, bf16[2,96,128]{2,1,0:T(8,128)(2,1)S(1)}, u32[]{:S(2)}, u32[]{:S(2)}) collective-permute-start(bf16[2,96,128]{2,1,0:T(8,128)(2,1)S(1)} %get-tuple-element.41), channel_id=1, source_target_pairs={{0,384},{192,576},{384,0},{576,192},{1,385},{193,577},{385,1},{577... | collective-permute-start | bytes 147464 | tf_op jit(solution)/shard_map/ppermute | solution.py:184
  116.3 7.2 %collective-permute-start.5 = (bf16[2,96,128]{2,1,0:T(8,128)(2,1)S(1)}, bf16[2,96,128]{2,1,0:T(8,128)(2,1)S(1)}, u32[]{:S(2)}, u32[]{:S(2)}) collective-permute-start(bf16[2,96,128]{2,1,0:T(8,128)(2,1)S(1)} %get-tuple-element.40), channel_id=1, source_target_pairs={{0,192},{192,384},{384,576},{576,0},{1,193},{193,385},{385,577},{5... | collective-permute-start | bytes 147464 | tf_op jit(solution)/shard_map/ppermute | solution.py:184
Sparse Core Ops, SparseCore 0:
  66.2 38.1 reduce-scatter.1

commit v8 on v6

--- a/solution.py
+++ b/solution.py
@@ -1,3 +1,5 @@
+import functools
+
 import jax
 import jax.numpy as jnp
 from jax import lax
@@ -32,12 +34,13 @@
 
 
 def pack_kv_kernel(k_ref, v_ref, out_ref):
-    hours, ports, width = k_ref.shape
+    ports, hours, width = k_ref.shape
     low = low_half(ports)
+    k_all, v_all = k_ref[...].astype(F32), v_ref[...].astype(F32)
     for h in range(hours):
         for t in range(width // LANES):
             cols = slice(t * LANES, (t + 1) * LANES)
-            k, v = k_ref[h, :, cols].astype(F32), v_ref[h, :, cols].astype(F32)
+            k, v = k_all[:, h, cols], v_all[:, h, cols]
             even = jnp.where(low, k, swap(v)).astype(BF16)
             odd = jnp.where(low, swap(k), v).astype(BF16)
             for z in range(out_ref.shape[1]):
@@ -65,7 +68,7 @@
     heads = len(out_refs)
     hour = at_ref[1]
     for s, out_ref in enumerate(out_refs):
-        n = lax.rem(at_ref[0] + s, heads)
+        n = lax.bitwise_xor(at_ref[0], s)
         for c in range(qg_ref.shape[0]):
             out_ref[c, :, :LANES] = qg_ref[c, hour, :, pl.ds(pl.multiple_of(n * LANES, LANES), LANES)]
             out_ref[c, :, LANES:] = qg_ref[c, hour, :, heads * LANES :]
@@ -136,7 +139,7 @@
     half = ports // 2
     lh = low_half(half)
     for s, ref in enumerate((d0_ref, d1_ref, d2_ref, d3_ref)):
-        dq[lax.rem(x_ref[0] + s, 4)] = ref[...]
+        dq[lax.bitwise_xor(x_ref[0], s)] = ref[...]
     for h in range(hours):
         for t in range(width // LANES):
             sl = slice(t * LANES, (t + 1) * LANES)
@@ -150,6 +153,25 @@
             q_ref[h, half:, sl] = jnp.where(lh, swap(a), b).astype(BF16)
 
 
+def spread_kernel(scale, t_ref, out_ref):
+    heads, parts, hours, rows, _ = t_ref.shape
+    for n in range(heads):
+        tile = sum(t_ref[n, z, h, rows - 8 :].astype(F32) for z in range(parts) for h in range(hours))
+        tile = (tile * scale).astype(BF16)
+        for t in range(out_ref.shape[0]):
+            out_ref[t, n] = tile
+
+
+def lay_kernel(t_ref, out_ref):
+    tiles, heads, _, _ = t_ref.shape
+    wide = out_ref.shape[1] // LANES
+    deep = tiles // wide * 8
+    for n in range(heads):
+        for t in range(tiles):
+            r, c = n * deep + t // wide * 8, t % wide * LANES
+            out_ref[r : r + 8, c : c + LANES] = t_ref[t, n].astype(F32)
+
+
 def call(kernel, outs, *args, scratch=(), scalars=0, name):
     smem, vmem = pl.BlockSpec(memory_space=pltpu.SMEM), pl.BlockSpec(memory_space=pltpu.VMEM)
     return pl.pallas_call(
@@ -172,8 +194,7 @@
 
 
 def along_x(a, by):
-    heads = lax.axis_size("x")
-    return lax.ppermute(a, "x", [(i, (i + by) % heads) for i in range(heads)])
+    return lax.ppermute(a, "x", [(i, i ^ by) for i in range(lax.axis_size("x"))])
 
 
 def per_device(query_rows, key_rows, value_rows, out_grad, out_weight, adjacency):
@@ -185,8 +206,8 @@
     model = out_grad.shape[2]
     total = port_count * ports
     x, core = lax.axis_index("x"), lax.axis_index("c")
-    q, k, v, g = (a.transpose(1, 0, 2) for a in (query_rows, key_rows, value_rows, out_grad))
-    kv_send = call(pack_kv_kernel, shape(heads, parts, hours, ports, LANES), k, v, name="pack_kv")
+    q, g = (a.transpose(1, 0, 2) for a in (query_rows, out_grad))
+    kv_send = call(pack_kv_kernel, shape(heads, parts, hours, ports, LANES), key_rows, value_rows, name="pack_kv")
     kv_got = exchange(kv_send.reshape(port_count, ports, LANES), PORT_AXES)
     adj = jnp.pad(adjacency, ((0, 0), (HEAD_DIM, LANES - HEAD_DIM - adjacency.shape[1])))
     qg = call(pack_qg_kernel, shape(hours, ports, heads * LANES + model), q, g, adj, name="pack_qg")
@@ -216,15 +237,18 @@
     dw = exchange(dw, TM_AXES)
     dw = jnp.sum(dw.astype(F32), axis=0).astype(BF16)
     dq = lax.dynamic_index_in_dim(lax.all_gather(dq, "c"), core, 1, keepdims=False)
-    dq = [dq[:, s] if s == 0 else along_x(dq[:, s], heads - s) for s in range(heads)]
+    dq = [dq[:, s] if s == 0 else along_x(dq[:, s], s) for s in range(heads)]
     back = back.at[:, chunk - 8 :, :].set(jnp.broadcast_to(dw, (port_count, 8, LANES)))
     back, dq = lax.optimization_barrier((exchange(back, PORT_AXES), dq))
     back = back.reshape(heads, parts, hours, chunk, LANES)
-    dw = back[:, :, :, chunk - 8 :, :].astype(F32)
-    dw = (jnp.sum(dw, axis=(1, 2)) * (1.0 / (hours * tm_count))).astype(BF16)
-    dw = exchange(jnp.broadcast_to(dw, (tm_count, *dw.shape)), TM_AXES)
-    dw = dw.transpose(1, 0, 2, 3).reshape(heads, HEAD_DIM // 8, model // LANES, 8, LANES)
-    dw = dw.transpose(0, 1, 3, 2, 4).reshape(width, model).astype(F32)
+    dw = call(
+        functools.partial(spread_kernel, 1.0 / (hours * tm_count)),
+        shape(tm_count, heads, 8, LANES),
+        back,
+        name="spread",
+    )
+    dw = exchange(dw, TM_AXES)
+    dw = call(lay_kernel, jax.ShapeDtypeStruct((width, model), F32), dw, name="lay")
     grads = call(
         unpack_kernel,
         (shape(hours, ports, width),) * 3,

time: 116 us -> 117 us (level)
  waiting for transfers between devices: 21.1 us -> 27.7 us
  starting transfers between devices: 53.8 us -> 48.7 us
  Pallas kernels: 6.15 us -> 7.96 us
    ppermute x6, waiting for transfers between devices: 5.84 us -> 11.8 us  [along_x(): lax.ppermute(a, 'x', [(i, i ^ by) for i in range(lax.axis_size('x'))])]
    ppermute x6, starting transfers between devices: 21.4 us -> 18.6 us  [along_x(): lax.ppermute(a, 'x', [(i, i ^ by) for i in range(lax.axis_size('x'))])]
    all_to_all x3, starting transfers between devices: 32.4 us -> 30.2 us  [exchange(): return lax.all_to_all(a, axes, 0, 0, tiled=True)]
    pallas_call x5 -> x7, Pallas kernels: 6.15 us -> 7.96 us  [call(): pl.pallas_call(kernel, out_shape=outs, in_specs=[smem] * scalars + [vmem]...]
    unnamed x13 -> x17, local copies, waits for them, and re-layouts: 3.65 us -> 5.37 us
  transfers between devices with their start and end apart: 9 -> 9, of which waited for: 4 -> 6; matrix products, arithmetic and copies ran while one was open for 2% -> 2% of each run, Pallas kernels for 1% -> 1%
where the time goes in v8:
time: 117 us; the launch traced here: 116 us
  starting transfers between devices  48.7 us (42%)
  waiting for transfers between devices  27.7 us (24%)
  blocking collectives  24.5 us (21%)
  Pallas kernels  7.96 us (7%)
  local copies, waits for them, and re-layouts  6.1 us (5%)
    all_to_all x3, starting transfers between devices, exchange(): return lax.all_to_all(a, axes, 0, 0, tiled=True)  30.2 us
    all_to_all x1, blocking collectives, exchange(): return lax.all_to_all(a, axes, 0, 0, tiled=True)  20.5 us
    ppermute x6, starting transfers between devices, along_x(): lax.ppermute(a, 'x', [(i, i ^ by) for i in range(lax.axis_size('x'))])  18.6 us
    all_to_all x3, waiting for transfers between devices, exchange(): return lax.all_to_all(a, axes, 0, 0, tiled=True)  15.9 us
    ppermute x6, waiting for transfers between devices, along_x(): lax.ppermute(a, 'x', [(i, i ^ by) for i in range(lax.axis_size('x'))])  11.8 us
    pallas_call x7, Pallas kernels, call(): pl.pallas_call(kernel, out_shape=outs, in_specs=[smem] * scalars + [vmem]...  7.96 us
    unnamed x17, local copies, waits for them, and re-layouts  5.37 us
  transfers between devices with their start and end apart: 9, of which 6 were waited for; matrix products, arithmetic and copies ran while one was open for 2% of the time, Pallas kernels for 1%

profile of v8, /device:TPU:1, one launch (start us, length us, event | category | flops | bytes accessed | tf_op | source)
XLA Modules:
  0.0 116.0 jit_solution(6500451282971633578)
XLA Ops:
  0.6 0.0 copy-start
  0.6 0.0 copy-start.1
  0.7 0.9 copy-done.1
  1.5 0.0 copy-start.2
  1.5 0.8 copy-done.2
  2.4 1.1 pack_kv.1
  3.5 0.0 copy-start.4
  3.5 18.1 %all-to-all-start = ((bf16[24,64,128]{2,1,0:T(8,128)(2,1)}), bf16[24,64,128]{2,1,0:T(8,128)(2,1)S(1)}, u32[]{:S(2)}, u32[]{:S(2)}) async-start(bf16[24,64,128]{2,1,0:T(8,128)(2,1)} %bitcast.1), calls=%async_computation | async-start | bytes 786432 | tf_op jit(solution)/shard_map/all_to_all | solution.py:193
  21.6 0.0 copy-start.3
  21.6 0.0 copy-done.4
  21.6 0.9 copy-done.3
  22.5 0.0 copy-start.5
  22.5 0.7 copy-done.5
  23.2 0.1 pad.6.adj_ref
  23.2 0.1 pack_qg.1
  23.3 0.1 pad_add_fusion.at_ref
  23.4 2.2 %all-gather = bf16[4,64,1024]{2,1,0:T(8,128)(2,1)S(1)} all-gather(bf16[2,64,1024]{2,1,0:T(8,128)(2,1)S(1)} %pack_qg.1), channel_id=2, replica_groups=mesh['x'=4,'zh'=3,'c'=2,'y'=8,'zl'=4] {'c'}, dimensions={0}, use_global_device_ids=true | all-gather | bytes 786432 | tf_op jit(solution)/shard_map/all_gather | solution.py:214
  25.6 0.6 route.1
  26.2 3.3 %collective-permute-start = (bf16[2,64,640]{2,1,0:T(8,128)(2,1)S(1)}, bf16[2,64,640]{2,1,0:T(8,128)(2,1)S(1)}, u32[]{:S(2)}, u32[]{:S(2)}) collective-permute-start(bf16[2,64,640]{2,1,0:T(8,128)(2,1)S(1)} %get-tuple-element.32), channel_id=1, source_target_pairs={{0,192},{192,0},{384,576},{576,384},{1,193},{193,1},{385,577},{577... | collective-permute-start | bytes 491528 | tf_op jit(solution)/shard_map/ppermute | solution.py:197
  29.5 4.3 %collective-permute-start.1 = (bf16[2,64,640]{2,1,0:T(8,128)(2,1)S(1)}, bf16[2,64,640]{2,1,0:T(8,128)(2,1)S(1)}, u32[]{:S(2)}, u32[]{:S(2)}) collective-permute-start(bf16[2,64,640]{2,1,0:T(8,128)(2,1)S(1)} %get-tuple-element.33), channel_id=1, source_target_pairs={{0,384},{192,576},{384,0},{576,192},{1,385},{193,577},{385,1},{577... | collective-permute-start | bytes 491528 | tf_op jit(solution)/shard_map/ppermute | solution.py:197
  33.8 2.0 %collective-permute-start.2 = (bf16[2,64,640]{2,1,0:T(8,128)(2,1)S(1)}, bf16[2,64,640]{2,1,0:T(8,128)(2,1)S(1)}, u32[]{:S(2)}, u32[]{:S(2)}) collective-permute-start(bf16[2,64,640]{2,1,0:T(8,128)(2,1)S(1)} %get-tuple-element.34), channel_id=1, source_target_pairs={{0,576},{192,384},{384,192},{576,0},{1,577},{193,385},{385,193},{5... | collective-permute-start | bytes 491528 | tf_op jit(solution)/shard_map/ppermute | solution.py:197
  35.8 0.0 copy-done
  35.8 0.0 collective-permute-done.p1_ref
  35.8 5.3 %collective-permute-done.1.p2_ref = bf16[2,64,640]{2,1,0:T(8,128)(2,1)S(1)} collective-permute-done((bf16[2,64,640]{2,1,0:T(8,128)(2,1)S(1)}, bf16[2,64,640]{2,1,0:T(8,128)(2,1)S(1)}, u32[]{:S(2)}, u32[]{:S(2)}) %collective-permute-start.1) | collective-permute-done | bytes 163872 | tf_op jit(solution)/shard_map/ppermute | solution.py:197
  41.1 3.8 %collective-permute-done.2.p3_ref = bf16[2,64,640]{2,1,0:T(8,128)(2,1)S(1)} collective-permute-done((bf16[2,64,640]{2,1,0:T(8,128)(2,1)S(1)}, bf16[2,64,640]{2,1,0:T(8,128)(2,1)S(1)}, u32[]{:S(2)}, u32[]{:S(2)}) %collective-permute-start.2) | collective-permute-done | bytes 163872 | tf_op jit(solution)/shard_map/ppermute | solution.py:197
  44.9 0.0 all-to-all-done.kv_ref
  44.9 4.5 %attend.1 = (bf16[24,72,128]{2,1,0:T(8,128)(2,1)}, bf16[2,4,32,128]{3,2,1,0:T(8,128)(2,1)S(1)}, bf16[32,8,128]{2,1,0:T(8,128)(2,1)S(1)}) custom-call(bf16[24,64,128]{2,1,0:T(8,128)(2,1)S(1)} %all-to-all-done.kv_ref, bf16[2,64,640]{2,1,0:T(8,128)(2,1)S(1)} %get-tuple-element.31.p0_ref, bf16[2,64,640]{2,1,0:T(8,128)(2,1)S(1)} %collective-permute-done.p1_ref, ...), custom_call_target="tpu_custom_call" | custom-call | tf_op jit(solution)/shard_map/attend/pallas_call | solution.py:177
  49.3 20.5 %all_to_all.20 = bf16[32,8,128]{2,1,0:T(8,128)(2,1)S(1)} all-to-all(bf16[32,8,128]{2,1,0:T(8,128)(2,1)S(1)} %get-tuple-element.36), channel_id=1, replica_groups=mesh['x'=4,'zh'=3,'c'=2,'y'=8,'zl'=4] {'y','zl'}, dimensions={0} | all-to-all | bytes 131072 | tf_op jit(solution)/shard_map/all_to_all | solution.py:193
  69.9 0.6 broadcast_dynamic-update-slice_fusion
  70.5 8.2 %all-to-all-start.2 = ((bf16[24,72,128]{2,1,0:T(8,128)(2,1)}), bf16[24,72,128]{2,1,0:T(8,128)(2,1)S(1)}, u32[]{:S(2)}, u32[]{:S(2)}) async-start(bf16[24,72,128]{2,1,0:T(8,128)(2,1)} %broadcast_dynamic-update-slice_fusion), calls=%async_computation.2 | async-start | bytes 884736 | tf_op jit(solution)/shard_map/all_to_all | solution.py:193
  78.7 1.9 %all-gather.1 = bf16[4,4,32,128]{3,2,1,0:T(8,128)(2,1)S(1)} all-gather(bf16[2,4,32,128]{3,2,1,0:T(8,128)(2,1)S(1)} %get-tuple-element.37), channel_id=3, replica_groups=mesh['x'=4,'zh'=3,'c'=2,'y'=8,'zl'=4] {'c'}, dimensions={0}, use_global_device_ids=true | all-gather | bytes 196608 | tf_op jit(solution)/shard_map/all_gather | solution.py:239
  80.6 4.5 %collective-permute-start.5 = (bf16[2,32,128]{2,1,0:T(8,128)(2,1)S(1)}, bf16[2,32,128]{2,1,0:T(8,128)(2,1)S(1)}, u32[]{:S(2)}, u32[]{:S(2)}) collective-permute-start(bf16[2,32,128]{2,1,0:T(8,128)(2,1)S(1)} %get-tuple-element.54), channel_id=1, source_target_pairs={{0,576},{192,384},{384,192},{576,0},{1,577},{193,385},{385,193},{5... | collective-permute-start | bytes 49160 | tf_op jit(solution)/shard_map/ppermute | solution.py:197
  85.2 2.5 %collective-permute-start.4 = (bf16[2,32,128]{2,1,0:T(8,128)(2,1)S(1)}, bf16[2,32,128]{2,1,0:T(8,128)(2,1)S(1)}, u32[]{:S(2)}, u32[]{:S(2)}) collective-permute-start(bf16[2,32,128]{2,1,0:T(8,128)(2,1)S(1)} %get-tuple-element.55), channel_id=1, source_target_pairs={{0,384},{192,576},{384,0},{576,192},{1,385},{193,577},{385,1},{577... | collective-permute-start | bytes 49160 | tf_op jit(solution)/shard_map/ppermute | solution.py:197
  87.6 2.0 %collective-permute-start.3 = (bf16[2,32,128]{2,1,0:T(8,128)(2,1)S(1)}, bf16[2,32,128]{2,1,0:T(8,128)(2,1)S(1)}, u32[]{:S(2)}, u32[]{:S(2)}) collective-permute-start(bf16[2,32,128]{2,1,0:T(8,128)(2,1)S(1)} %get-tuple-element.56), channel_id=1, source_target_pairs={{0,192},{192,0},{384,576},{576,384},{1,193},{193,1},{385,577},{577... | collective-permute-start | bytes 49160 | tf_op jit(solution)/shard_map/ppermute | solution.py:197
  89.6 0.0 collective-permute-done.5.d3_ref
  89.6 2.4 %collective-permute-done.4.d2_ref = bf16[2,32,128]{2,1,0:T(8,128)(2,1)S(1)} collective-permute-done((bf16[2,32,128]{2,1,0:T(8,128)(2,1)S(1)}, bf16[2,32,128]{2,1,0:T(8,128)(2,1)S(1)}, u32[]{:S(2)}, u32[]{:S(2)}) %collective-permute-start.4) | collective-permute-done | bytes 16416 | tf_op jit(solution)/shard_map/ppermute | solution.py:197
  92.0 0.4 collective-permute-done.3.d1_ref
  92.4 7.1 %all-to-all-done.2 = bf16[24,72,128]{2,1,0:T(8,128)(2,1)S(1)} async-done(((bf16[24,72,128]{2,1,0:T(8,128)(2,1)}), bf16[24,72,128]{2,1,0:T(8,128)(2,1)S(1)}, u32[]{:S(2)}, u32[]{:S(2)}) %all-to-all-start.2) | async-done | bytes 442400 | tf_op jit(solution)/shard_map/all_to_all | solution.py:193
  99.5 0.7 spread.1
  100.2 3.9 %all-to-all-start.3 = ((bf16[32,4,8,128]{3,2,1,0:T(8,128)(2,1)}), bf16[32,4,8,128]{3,2,1,0:T(8,128)(2,1)S(1)}, u32[]{:S(2)}, u32[]{:S(2)}) async-start(bf16[32,4,8,128]{3,2,1,0:T(8,128)(2,1)} %spread.1), calls=%async_computation.3 | async-start | bytes 524288 | tf_op jit(solution)/shard_map/all_to_all | solution.py:193
  104.1 0.1 unpack.1
  104.3 0.7 copy.19
  105.0 0.7 copy.20
  105.7 0.7 copy.21
  106.4 8.8 %all-to-all-done.3.t_ref = bf16[32,4,8,128]{3,2,1,0:T(8,128)(2,1)S(1)} async-done(((bf16[32,4,8,128]{3,2,1,0:T(8,128)(2,1)}), bf16[32,4,8,128]{3,2,1,0:T(8,128)(2,1)S(1)}, u32[]{:S(2)}, u32[]{:S(2)}) %all-to-all-start.3) | async-done | bytes 262176 | tf_op jit(solution)/shard_map/all_to_all | solution.py:193
  115.2 0.8 lay.1
  (6 shorter events, 0.1 us)
Async XLA Ops:
  0.6 35.2 %copy-start = (bf16[256,512]{1,0:T(8,128)(2,1)S(1)}, bf16[256,512]{1,0:T(8,128)(2,1)}, u32[]{:S(2)}) copy-start(bf16[256,512]{1,0:T(8,128)(2,1)} %param.12) | copy-start | bytes 786436
  0.6 0.9 copy-start.1
  1.5 0.8 copy-start.2
  3.5 18.1 %copy-start.4 = (bf16[64,2,256]{2,1,0:T(2,128)(2,1)S(1)}, bf16[64,2,256]{2,1,0:T(2,128)(2,1)}, u32[]{:S(2)}) copy-start(bf16[64,2,256]{2,1,0:T(2,128)(2,1)} %param.8) | copy-start | bytes 196612
  3.5 41.4 %all-to-all-start = ((bf16[24,64,128]{2,1,0:T(8,128)(2,1)}), bf16[24,64,128]{2,1,0:T(8,128)(2,1)S(1)}, u32[]{:S(2)}, u32[]{:S(2)}) async-start(bf16[24,64,128]{2,1,0:T(8,128)(2,1)} %bitcast.1), calls=%async_computation | async-start | bytes 786432 | tf_op jit(solution)/shard_map/all_to_all | solution.py:193
  21.6 0.9 copy-start.3
  22.5 0.7 copy-start.5
  26.2 9.6 %collective-permute-start = (bf16[2,64,640]{2,1,0:T(8,128)(2,1)S(1)}, bf16[2,64,640]{2,1,0:T(8,128)(2,1)S(1)}, u32[]{:S(2)}, u32[]{:S(2)}) collective-permute-start(bf16[2,64,640]{2,1,0:T(8,128)(2,1)S(1)} %get-tuple-element.32), channel_id=1, source_target_pairs={{0,192},{192,0},{384,576},{576,384},{1,193},{193,1},{385,577},{577... | collective-permute-start | bytes 491528 | tf_op jit(solution)/shard_map/ppermute | solution.py:197
  29.5 11.6 %collective-permute-start.1 = (bf16[2,64,640]{2,1,0:T(8,128)(2,1)S(1)}, bf16[2,64,640]{2,1,0:T(8,128)(2,1)S(1)}, u32[]{:S(2)}, u32[]{:S(2)}) collective-permute-start(bf16[2,64,640]{2,1,0:T(8,128)(2,1)S(1)} %get-tuple-element.33), channel_id=1, source_target_pairs={{0,384},{192,576},{384,0},{576,192},{1,385},{193,577},{385,1},{577... | collective-permute-start | bytes 491528 | tf_op jit(solution)/shard_map/ppermute | solution.py:197
  33.8 11.1 %collective-permute-start.2 = (bf16[2,64,640]{2,1,0:T(8,128)(2,1)S(1)}, bf16[2,64,640]{2,1,0:T(8,128)(2,1)S(1)}, u32[]{:S(2)}, u32[]{:S(2)}) collective-permute-start(bf16[2,64,640]{2,1,0:T(8,128)(2,1)S(1)} %get-tuple-element.34), channel_id=1, source_target_pairs={{0,576},{192,384},{384,192},{576,0},{1,577},{193,385},{385,193},{5... | collective-permute-start | bytes 491528 | tf_op jit(solution)/shard_map/ppermute | solution.py:197
  70.5 29.0 %all-to-all-start.2 = ((bf16[24,72,128]{2,1,0:T(8,128)(2,1)}), bf16[24,72,128]{2,1,0:T(8,128)(2,1)S(1)}, u32[]{:S(2)}, u32[]{:S(2)}) async-start(bf16[24,72,128]{2,1,0:T(8,128)(2,1)} %broadcast_dynamic-update-slice_fusion), calls=%async_computation.2 | async-start | bytes 884736 | tf_op jit(solution)/shard_map/all_to_all | solution.py:193
  80.6 9.0 %collective-permute-start.5 = (bf16[2,32,128]{2,1,0:T(8,128)(2,1)S(1)}, bf16[2,32,128]{2,1,0:T(8,128)(2,1)S(1)}, u32[]{:S(2)}, u32[]{:S(2)}) collective-permute-start(bf16[2,32,128]{2,1,0:T(8,128)(2,1)S(1)} %get-tuple-element.54), channel_id=1, source_target_pairs={{0,576},{192,384},{384,192},{576,0},{1,577},{193,385},{385,193},{5... | collective-permute-start | bytes 49160 | tf_op jit(solution)/shard_map/ppermute | solution.py:197
  85.2 6.8 %collective-permute-start.4 = (bf16[2,32,128]{2,1,0:T(8,128)(2,1)S(1)}, bf16[2,32,128]{2,1,0:T(8,128)(2,1)S(1)}, u32[]{:S(2)}, u32[]{:S(2)}) collective-permute-start(bf16[2,32,128]{2,1,0:T(8,128)(2,1)S(1)} %get-tuple-element.55), channel_id=1, source_target_pairs={{0,384},{192,576},{384,0},{576,192},{1,385},{193,577},{385,1},{577... | collective-permute-start | bytes 49160 | tf_op jit(solution)/shard_map/ppermute | solution.py:197
  87.6 4.8 %collective-permute-start.3 = (bf16[2,32,128]{2,1,0:T(8,128)(2,1)S(1)}, bf16[2,32,128]{2,1,0:T(8,128)(2,1)S(1)}, u32[]{:S(2)}, u32[]{:S(2)}) collective-permute-start(bf16[2,32,128]{2,1,0:T(8,128)(2,1)S(1)} %get-tuple-element.56), channel_id=1, source_target_pairs={{0,192},{192,0},{384,576},{576,384},{1,193},{193,1},{385,577},{577... | collective-permute-start | bytes 49160 | tf_op jit(solution)/shard_map/ppermute | solution.py:197
  100.2 14.9 %all-to-all-start.3 = ((bf16[32,4,8,128]{3,2,1,0:T(8,128)(2,1)}), bf16[32,4,8,128]{3,2,1,0:T(8,128)(2,1)S(1)}, u32[]{:S(2)}, u32[]{:S(2)}) async-start(bf16[32,4,8,128]{3,2,1,0:T(8,128)(2,1)} %spread.1), calls=%async_computation.3 | async-start | bytes 524288 | tf_op jit(solution)/shard_map/all_to_all | solution.py:193

commit v9 on v6

--- a/solution.py
+++ b/solution.py
@@ -71,7 +71,7 @@
             out_ref[c, :, LANES:] = qg_ref[c, hour, :, heads * LANES :]
 
 
-def attend_kernel(kv_ref, p0_ref, p1_ref, p2_ref, p3_ref, w_ref, out_ref, dq_ref, dw_ref, kx, kv, dkt, dvt):
+def attend_kernel(kv_ref, p0_ref, p2_ref, p1_ref, p3_ref, w_ref, out_ref, dq_ref, dw_ref, kx, kv, dkt, dvt):
     sources, ports, _ = kv_ref.shape
     total = sources * ports
     parts = (p0_ref, p1_ref, p2_ref, p3_ref)
@@ -208,7 +208,7 @@
         attend_kernel,
         (shape(port_count, chunk, LANES), shape(hours, heads, ports // 2, LANES), shape(tiles, 8, LANES)),
         kv_got,
-        *routed,
+        *(routed[s] for s in (0, 2, 1, 3)),
         w_n,
         scratch=[vec, vec, acc, acc],
         name="attend",

time: 116 us -> 115 us (level)
  waiting for transfers between devices: 21.1 us -> 19.7 us
    ppermute x6, waiting for transfers between devices: 5.84 us -> 4.37 us  [along_x(): return lax.ppermute(a, 'x', [(i, (i + by) % heads) for i in range(heads)])]
where the time goes in v9:
time: 115 us; the launch traced here: 114 us
  starting transfers between devices  54.6 us (47%)
  blocking collectives  25.4 us (22%)
  waiting for transfers between devices  19.7 us (17%)
  local copies, waits for them, and re-layouts  6.91 us (6%)
  Pallas kernels  6.14 us (5%)
    all_to_all x3, starting transfers between devices, exchange(): return lax.all_to_all(a, axes, 0, 0, tiled=True)  32.6 us
    ppermute x6, starting transfers between devices, along_x(): return lax.ppermute(a, 'x', [(i, (i + by) % heads) for i in range(heads)])  22 us
    all_to_all x1, blocking collectives, exchange(): return lax.all_to_all(a, axes, 0, 0, tiled=True)  21.3 us
    all_to_all x3, waiting for transfers between devices, exchange(): return lax.all_to_all(a, axes, 0, 0, tiled=True)  15.3 us
    pallas_call x5, Pallas kernels, call(): pl.pallas_call(kernel, out_shape=outs, in_specs=[smem] * scalars + [vmem]...  6.14 us
    ppermute x6, waiting for transfers between devices, along_x(): return lax.ppermute(a, 'x', [(i, (i + by) % heads) for i in range(heads)])  4.37 us
    unnamed x13, local copies, waits for them, and re-layouts  3.65 us
  transfers between devices with their start and end apart: 9, of which 4 were waited for; matrix products, arithmetic and copies ran while one was open for 2% of the time, Pallas kernels for 1%

profile of v9, /device:TPU:1, one launch (start us, length us, event | category | flops | bytes accessed | tf_op | source)
XLA Modules:
  0.0 113.8 jit_solution(13186320493485323383)
XLA Ops:
  0.6 0.0 copy-start
  0.6 0.9 copy_bitcast_fusion.3
  1.6 0.9 pack_kv.1
  2.4 0.0 copy-start.2
  2.4 18.1 %all-to-all-start = ((bf16[24,64,128]{2,1,0:T(8,128)(2,1)}), bf16[24,64,128]{2,1,0:T(8,128)(2,1)S(1)}, u32[]{:S(2)}, u32[]{:S(2)}) async-start(bf16[24,64,128]{2,1,0:T(8,128)(2,1)} %bitcast.3), calls=%async_computation | async-start | bytes 786432 | tf_op jit(solution)/shard_map/all_to_all | solution.py:171
  20.5 0.0 copy-start.1
  20.5 0.0 copy-done.2
  20.6 0.9 copy-done.1
  21.4 0.0 copy-start.3
  21.5 0.7 copy-done.3
  22.1 0.1 pad.6.adj_ref
  22.2 0.1 pack_qg.1
  22.3 0.1 pad_add_fusion.at_ref
  22.4 2.2 %all-gather = bf16[4,64,1024]{2,1,0:T(8,128)(2,1)S(1)} all-gather(bf16[2,64,1024]{2,1,0:T(8,128)(2,1)S(1)} %pack_qg.1), channel_id=2, replica_groups=mesh['x'=4,'zh'=3,'c'=2,'y'=8,'zl'=4] {'c'}, dimensions={0}, use_global_device_ids=true | all-gather | bytes 786432 | tf_op jit(solution)/shard_map/all_gather | solution.py:193
  24.5 0.6 route.1
  25.1 4.8 %collective-permute-start = (bf16[2,64,640]{2,1,0:T(8,128)(2,1)S(1)}, bf16[2,64,640]{2,1,0:T(8,128)(2,1)S(1)}, u32[]{:S(2)}, u32[]{:S(2)}) collective-permute-start(bf16[2,64,640]{2,1,0:T(8,128)(2,1)S(1)} %get-tuple-element.32), channel_id=1, source_target_pairs={{0,384},{192,576},{384,0},{576,192},{1,385},{193,577},{385,1},{577... | collective-permute-start | bytes 491528 | tf_op jit(solution)/shard_map/ppermute | solution.py:176
  30.0 2.2 %collective-permute-start.1 = (bf16[2,64,640]{2,1,0:T(8,128)(2,1)S(1)}, bf16[2,64,640]{2,1,0:T(8,128)(2,1)S(1)}, u32[]{:S(2)}, u32[]{:S(2)}) collective-permute-start(bf16[2,64,640]{2,1,0:T(8,128)(2,1)S(1)} %get-tuple-element.33), channel_id=1, source_target_pairs={{0,192},{192,384},{384,576},{576,0},{1,193},{193,385},{385,577},{5... | collective-permute-start | bytes 491528 | tf_op jit(solution)/shard_map/ppermute | solution.py:176
  32.2 4.3 %collective-permute-start.2 = (bf16[2,64,640]{2,1,0:T(8,128)(2,1)S(1)}, bf16[2,64,640]{2,1,0:T(8,128)(2,1)S(1)}, u32[]{:S(2)}, u32[]{:S(2)}) collective-permute-start(bf16[2,64,640]{2,1,0:T(8,128)(2,1)S(1)} %get-tuple-element.34), channel_id=1, source_target_pairs={{0,576},{192,0},{384,192},{576,384},{1,577},{193,1},{385,193},{577... | collective-permute-start | bytes 491528 | tf_op jit(solution)/shard_map/ppermute | solution.py:176
  36.5 0.0 copy-done
  36.5 0.0 collective-permute-done.p2_ref
  36.5 2.7 %collective-permute-done.1.p1_ref = bf16[2,64,640]{2,1,0:T(8,128)(2,1)S(1)} collective-permute-done((bf16[2,64,640]{2,1,0:T(8,128)(2,1)S(1)}, bf16[2,64,640]{2,1,0:T(8,128)(2,1)S(1)}, u32[]{:S(2)}, u32[]{:S(2)}) %collective-permute-start.1) | collective-permute-done | bytes 163872 | tf_op jit(solution)/shard_map/ppermute | solution.py:176
  39.2 0.0 collective-permute-done.2.p3_ref
  39.2 0.0 all-to-all-done.kv_ref
  39.2 4.5 %attend.1 = (bf16[24,72,128]{2,1,0:T(8,128)(2,1)}, bf16[2,4,32,128]{3,2,1,0:T(8,128)(2,1)S(1)}, bf16[32,8,128]{2,1,0:T(8,128)(2,1)S(1)}) custom-call(bf16[24,64,128]{2,1,0:T(8,128)(2,1)S(1)} %all-to-all-done.kv_ref, bf16[2,64,640]{2,1,0:T(8,128)(2,1)S(1)} %get-tuple-element.31.p0_ref, bf16[2,64,640]{2,1,0:T(8,128)(2,1)S(1)} %collective-permute-done.p2_ref, ...), custom_call_target="tpu_custom_call" | custom-call | tf_op jit(solution)/shard_map/attend/pallas_call | solution.py:155
  43.7 21.3 %all_to_all.20 = bf16[32,8,128]{2,1,0:T(8,128)(2,1)S(1)} all-to-all(bf16[32,8,128]{2,1,0:T(8,128)(2,1)S(1)} %get-tuple-element.36), channel_id=1, replica_groups=mesh['x'=4,'zh'=3,'c'=2,'y'=8,'zl'=4] {'y','zl'}, dimensions={0} | all-to-all | bytes 131072 | tf_op jit(solution)/shard_map/all_to_all | solution.py:171
  65.0 0.6 broadcast_dynamic-update-slice_fusion
  65.7 10.7 %all-to-all-start.2 = ((bf16[24,72,128]{2,1,0:T(8,128)(2,1)}), bf16[24,72,128]{2,1,0:T(8,128)(2,1)S(1)}, u32[]{:S(2)}, u32[]{:S(2)}) async-start(bf16[24,72,128]{2,1,0:T(8,128)(2,1)} %broadcast_dynamic-update-slice_fusion), calls=%async_computation.2 | async-start | bytes 884736 | tf_op jit(solution)/shard_map/all_to_all | solution.py:171
  76.4 1.9 %all-gather.1 = bf16[4,4,32,128]{3,2,1,0:T(8,128)(2,1)S(1)} all-gather(bf16[2,4,32,128]{3,2,1,0:T(8,128)(2,1)S(1)} %get-tuple-element.37), channel_id=3, replica_groups=mesh['x'=4,'zh'=3,'c'=2,'y'=8,'zl'=4] {'c'}, dimensions={0}, use_global_device_ids=true | all-gather | bytes 196608 | tf_op jit(solution)/shard_map/all_gather | solution.py:218
  78.3 3.3 %collective-permute-start.5 = (bf16[2,32,128]{2,1,0:T(8,128)(2,1)S(1)}, bf16[2,32,128]{2,1,0:T(8,128)(2,1)S(1)}, u32[]{:S(2)}, u32[]{:S(2)}) collective-permute-start(bf16[2,32,128]{2,1,0:T(8,128)(2,1)S(1)} %get-tuple-element.54), channel_id=1, source_target_pairs={{0,192},{192,384},{384,576},{576,0},{1,193},{193,385},{385,577},{5... | collective-permute-start | bytes 49160 | tf_op jit(solution)/shard_map/ppermute | solution.py:176
  81.6 4.3 %collective-permute-start.4 = (bf16[2,32,128]{2,1,0:T(8,128)(2,1)S(1)}, bf16[2,32,128]{2,1,0:T(8,128)(2,1)S(1)}, u32[]{:S(2)}, u32[]{:S(2)}) collective-permute-start(bf16[2,32,128]{2,1,0:T(8,128)(2,1)S(1)} %get-tuple-element.55), channel_id=1, source_target_pairs={{0,384},{192,576},{384,0},{576,192},{1,385},{193,577},{385,1},{577... | collective-permute-start | bytes 49160 | tf_op jit(solution)/shard_map/ppermute | solution.py:176
  85.9 3.1 %collective-permute-start.3 = (bf16[2,32,128]{2,1,0:T(8,128)(2,1)S(1)}, bf16[2,32,128]{2,1,0:T(8,128)(2,1)S(1)}, u32[]{:S(2)}, u32[]{:S(2)}) collective-permute-start(bf16[2,32,128]{2,1,0:T(8,128)(2,1)S(1)} %get-tuple-element.56), channel_id=1, source_target_pairs={{0,576},{192,0},{384,192},{576,384},{1,577},{193,1},{385,193},{577... | collective-permute-start | bytes 49160 | tf_op jit(solution)/shard_map/ppermute | solution.py:176
  89.0 0.0 collective-permute-done.5.d3_ref
  89.0 0.0 collective-permute-done.4.d2_ref
  89.0 1.7 %collective-permute-done.3.d1_ref = bf16[2,32,128]{2,1,0:T(8,128)(2,1)S(1)} collective-permute-done((bf16[2,32,128]{2,1,0:T(8,128)(2,1)S(1)}, bf16[2,32,128]{2,1,0:T(8,128)(2,1)S(1)}, u32[]{:S(2)}, u32[]{:S(2)}) %collective-permute-start.3) | collective-permute-done | bytes 16416 | tf_op jit(solution)/shard_map/ppermute | solution.py:176
  90.7 6.5 %all-to-all-done.2 = bf16[24,72,128]{2,1,0:T(8,128)(2,1)S(1)} async-done(((bf16[24,72,128]{2,1,0:T(8,128)(2,1)}), bf16[24,72,128]{2,1,0:T(8,128)(2,1)S(1)}, u32[]{:S(2)}, u32[]{:S(2)}) %all-to-all-start.2) | async-done | bytes 442400 | tf_op jit(solution)/shard_map/all_to_all | solution.py:171
  97.2 0.7 broadcast_in_dim.4
  97.9 3.9 %all-to-all-start.3 = ((bf16[32,4,8,128]{3,2,1,0:T(8,128)(2,1)}), bf16[32,4,8,128]{3,2,1,0:T(8,128)(2,1)S(1)}, u32[]{:S(2)}, u32[]{:S(2)}) async-start(bf16[32,4,8,128]{3,2,1,0:T(8,128)(2,1)} %broadcast_in_dim.4), calls=%async_computation.3 | async-start | bytes 524288 | tf_op jit(solution)/shard_map/all_to_all | solution.py:171
  101.8 0.1 unpack.1
  101.9 0.7 copy.24
  102.6 0.7 copy.25
  103.3 0.7 copy.26
  104.0 8.8 %all-to-all-done.3 = bf16[32,4,8,128]{3,2,1,0:T(8,128)(2,1)S(1)} async-done(((bf16[32,4,8,128]{3,2,1,0:T(8,128)(2,1)}), bf16[32,4,8,128]{3,2,1,0:T(8,128)(2,1)S(1)}, u32[]{:S(2)}, u32[]{:S(2)}) %all-to-all-start.3) | async-done | bytes 262176 | tf_op jit(solution)/shard_map/all_to_all | solution.py:171
  112.9 0.9 copy.23
  (9 shorter events, 0.2 us)
Async XLA Ops:
  0.6 35.8 %copy-start = (bf16[256,512]{1,0:T(8,128)(2,1)S(1)}, bf16[256,512]{1,0:T(8,128)(2,1)}, u32[]{:S(2)}) copy-start(bf16[256,512]{1,0:T(8,128)(2,1)} %param.12) | copy-start | bytes 786436
  2.4 18.1 %copy-start.2 = (bf16[64,2,256]{2,1,0:T(2,128)(2,1)S(1)}, bf16[64,2,256]{2,1,0:T(2,128)(2,1)}, u32[]{:S(2)}) copy-start(bf16[64,2,256]{2,1,0:T(2,128)(2,1)} %param.8) | copy-start | bytes 196612
  2.4 36.8 %all-to-all-start = ((bf16[24,64,128]{2,1,0:T(8,128)(2,1)}), bf16[24,64,128]{2,1,0:T(8,128)(2,1)S(1)}, u32[]{:S(2)}, u32[]{:S(2)}) async-start(bf16[24,64,128]{2,1,0:T(8,128)(2,1)} %bitcast.3), calls=%async_computation | async-start | bytes 786432 | tf_op jit(solution)/shard_map/all_to_all | solution.py:171
  20.5 0.9 copy-start.1
  21.4 0.7 copy-start.3
  25.1 11.4 %collective-permute-start = (bf16[2,64,640]{2,1,0:T(8,128)(2,1)S(1)}, bf16[2,64,640]{2,1,0:T(8,128)(2,1)S(1)}, u32[]{:S(2)}, u32[]{:S(2)}) collective-permute-start(bf16[2,64,640]{2,1,0:T(8,128)(2,1)S(1)} %get-tuple-element.32), channel_id=1, source_target_pairs={{0,384},{192,576},{384,0},{576,192},{1,385},{193,577},{385,1},{577... | collective-permute-start | bytes 491528 | tf_op jit(solution)/shard_map/ppermute | solution.py:176
  30.0 9.2 %collective-permute-start.1 = (bf16[2,64,640]{2,1,0:T(8,128)(2,1)S(1)}, bf16[2,64,640]{2,1,0:T(8,128)(2,1)S(1)}, u32[]{:S(2)}, u32[]{:S(2)}) collective-permute-start(bf16[2,64,640]{2,1,0:T(8,128)(2,1)S(1)} %get-tuple-element.33), channel_id=1, source_target_pairs={{0,192},{192,384},{384,576},{576,0},{1,193},{193,385},{385,577},{5... | collective-permute-start | bytes 491528 | tf_op jit(solution)/shard_map/ppermute | solution.py:176
  32.2 7.0 %collective-permute-start.2 = (bf16[2,64,640]{2,1,0:T(8,128)(2,1)S(1)}, bf16[2,64,640]{2,1,0:T(8,128)(2,1)S(1)}, u32[]{:S(2)}, u32[]{:S(2)}) collective-permute-start(bf16[2,64,640]{2,1,0:T(8,128)(2,1)S(1)} %get-tuple-element.34), channel_id=1, source_target_pairs={{0,576},{192,0},{384,192},{576,384},{1,577},{193,1},{385,193},{577... | collective-permute-start | bytes 491528 | tf_op jit(solution)/shard_map/ppermute | solution.py:176
  65.7 31.5 %all-to-all-start.2 = ((bf16[24,72,128]{2,1,0:T(8,128)(2,1)}), bf16[24,72,128]{2,1,0:T(8,128)(2,1)S(1)}, u32[]{:S(2)}, u32[]{:S(2)}) async-start(bf16[24,72,128]{2,1,0:T(8,128)(2,1)} %broadcast_dynamic-update-slice_fusion), calls=%async_computation.2 | async-start | bytes 884736 | tf_op jit(solution)/shard_map/all_to_all | solution.py:171
  78.3 10.7 %collective-permute-start.5 = (bf16[2,32,128]{2,1,0:T(8,128)(2,1)S(1)}, bf16[2,32,128]{2,1,0:T(8,128)(2,1)S(1)}, u32[]{:S(2)}, u32[]{:S(2)}) collective-permute-start(bf16[2,32,128]{2,1,0:T(8,128)(2,1)S(1)} %get-tuple-element.54), channel_id=1, source_target_pairs={{0,192},{192,384},{384,576},{576,0},{1,193},{193,385},{385,577},{5... | collective-permute-start | bytes 49160 | tf_op jit(solution)/shard_map/ppermute | solution.py:176
  81.6 7.4 %collective-permute-start.4 = (bf16[2,32,128]{2,1,0:T(8,128)(2,1)S(1)}, bf16[2,32,128]{2,1,0:T(8,128)(2,1)S(1)}, u32[]{:S(2)}, u32[]{:S(2)}) collective-permute-start(bf16[2,32,128]{2,1,0:T(8,128)(2,1)S(1)} %get-tuple-element.55), channel_id=1, source_target_pairs={{0,384},{192,576},{384,0},{576,192},{1,385},{193,577},{385,1},{577... | collective-permute-start | bytes 49160 | tf_op jit(solution)/shard_map/ppermute | solution.py:176
  85.9 4.8 %collective-permute-start.3 = (bf16[2,32,128]{2,1,0:T(8,128)(2,1)S(1)}, bf16[2,32,128]{2,1,0:T(8,128)(2,1)S(1)}, u32[]{:S(2)}, u32[]{:S(2)}) collective-permute-start(bf16[2,32,128]{2,1,0:T(8,128)(2,1)S(1)} %get-tuple-element.56), channel_id=1, source_target_pairs={{0,576},{192,0},{384,192},{576,384},{1,577},{193,1},{385,193},{577... | collective-permute-start | bytes 49160 | tf_op jit(solution)/shard_map/ppermute | solution.py:176
  97.9 14.9 %all-to-all-start.3 = ((bf16[32,4,8,128]{3,2,1,0:T(8,128)(2,1)}), bf16[32,4,8,128]{3,2,1,0:T(8,128)(2,1)S(1)}, u32[]{:S(2)}, u32[]{:S(2)}) async-start(bf16[32,4,8,128]{3,2,1,0:T(8,128)(2,1)} %broadcast_in_dim.4), calls=%async_computation.3 | async-start | bytes 524288 | tf_op jit(solution)/shard_map/all_to_all | solution.py:171

commit v10 on v9

--- a/solution.py
+++ b/solution.py
@@ -71,7 +71,41 @@
             out_ref[c, :, LANES:] = qg_ref[c, hour, :, heads * LANES :]
 
 
-def attend_kernel(kv_ref, p0_ref, p2_ref, p1_ref, p3_ref, w_ref, out_ref, dq_ref, dw_ref, kx, kv, dkt, dvt):
+def softmax_rows(qx, kx):
+    s = dot(qx, kx, NT)
+    top = jnp.max(s, axis=1, keepdims=True)
+    e = jnp.exp2((s - top) * (0.125 * LOG2E))
+    return e * (1.0 / jnp.sum(e, axis=1, keepdims=True))
+
+
+def weight_kernel(kv_ref, p0_ref, p2_ref, p1_ref, p3_ref, dw_ref, kx, kv):
+    sources, ports, _ = kv_ref.shape
+    total = sources * ports
+    parts = (p0_ref, p1_ref, p2_ref, p3_ref)
+    own = len(parts) * 2 * ports
+    rows = 4 * ports
+    part = kv_ref[...].reshape(total, LANES)
+    lane = lax.broadcasted_iota(jnp.int32, (total, LANES), 1)
+    block = lax.shift_right_logical(lax.broadcasted_iota(jnp.int32, (total, LANES), 0), 5)
+    hot = jnp.where(lane - HEAD_DIM == block, 1.0, 0.0)
+    kv[...] = part
+    kx[...] = jnp.where(lane < HEAD_DIM, part.astype(F32), hot).astype(BF16)
+    dw = None
+    for b in range(own // rows):
+        mine = jnp.concatenate([parts[2 * b][...], parts[2 * b + 1][...]], axis=0)
+        qx = mine[:, :, :LANES].reshape(rows, LANES)
+        g = mine[:, :, LANES:].reshape(rows, -1)
+        att = dot(softmax_rows(qx, kx[...]).astype(BF16), kv[...], NN).astype(BF16)
+        part = dot(att, g, TN)
+        dw = part if dw is None else dw + part
+    dw = dw[HEAD_DIM:].astype(BF16)
+    wide = dw.shape[1] // LANES
+    for r in range(HEAD_DIM // 8):
+        for c in range(wide):
+            dw_ref[r * wide + c] = dw[r * 8 : (r + 1) * 8, c * LANES : (c + 1) * LANES]
+
+
+def attend_kernel(kv_ref, p0_ref, p2_ref, p1_ref, p3_ref, w_ref, out_ref, dq_ref, kx, kv, dkt, dvt):
     sources, ports, _ = kv_ref.shape
     total = sources * ports
     parts = (p0_ref, p1_ref, p2_ref, p3_ref)
@@ -84,23 +118,16 @@
     kv[...] = part
     kx[...] = jnp.where(lane < HEAD_DIM, part.astype(F32), hot).astype(BF16)
     w_n = jnp.concatenate([jnp.zeros_like(w_ref), w_ref[...]], axis=0)
-    scale2 = 0.125 * LOG2E
     low = low_half(rows)
     per = rows // ports
-    dw = None
     for b in range(own // rows):
         mine = jnp.concatenate([parts[2 * b][...], parts[2 * b + 1][...]], axis=0)
         qx = mine[:, :, :LANES].reshape(rows, LANES)
         g = mine[:, :, LANES:].reshape(rows, -1)
         d = dot(g, w_n, NT).astype(BF16)
-        s = dot(qx, kx[...], NT)
-        top = jnp.max(s, axis=1, keepdims=True)
-        e = jnp.exp2((s - top) * scale2)
-        p = e * (1.0 / jnp.sum(e, axis=1, keepdims=True))
+        p = softmax_rows(qx, kx[...])
         p_low = p.astype(BF16)
         att = dot(p_low, kv[...], NN).astype(BF16)
-        part = dot(att, g, TN)
-        dw = part if dw is None else dw + part
         d32 = d.astype(F32)
         term = jnp.sum(d32 * att.astype(F32), axis=1, keepdims=True)
         dp = dot(d, kv[...], NT)
@@ -119,11 +146,6 @@
         for i in range(per):
             a, c = dq[i * ports : i * ports + half], dq[i * ports + half : (i + 1) * ports]
             dq_ref[i % 2, (b * per + i) // 2] = jnp.where(low_half(half), a, swap(c)).astype(BF16)
-    dw = dw[HEAD_DIM:].astype(BF16)
-    wide = dw.shape[1] // LANES
-    for r in range(HEAD_DIM // 8):
-        for c in range(wide):
-            dw_ref[r * wide + c] = dw[r * 8 : (r + 1) * 8, c * LANES : (c + 1) * LANES]
     both = jnp.concatenate([dkt[...] * 0.125, dvt[...]], axis=0).T.astype(BF16)
     for i in range(sources):
         out_ref[i, :ports, :] = both[i * ports : (i + 1) * ports]
@@ -204,11 +226,12 @@
     tiles = HEAD_DIM * model // (8 * LANES)
     chunk = ports + 8
     vec, acc = pltpu.VMEM((total, LANES), BF16), pltpu.VMEM((HEAD_DIM, total), F32)
-    back, dq, dw = call(
+    shared = (kv_got, *(routed[s] for s in (0, 2, 1, 3)))
+    dw = call(weight_kernel, shape(tiles, 8, LANES), *shared, scratch=[vec, vec], name="weight_rows")
+    back, dq = call(
         attend_kernel,
-        (shape(port_count, chunk, LANES), shape(hours, heads, ports // 2, LANES), shape(tiles, 8, LANES)),
-        kv_got,
-        *(routed[s] for s in (0, 2, 1, 3)),
+        (shape(port_count, chunk, LANES), shape(hours, heads, ports // 2, LANES)),
+        *shared,
         w_n,
         scratch=[vec, vec, acc, acc],
         name="attend",

time: 115 us -> 114 us (level)
  blocking collectives: 25.4 us -> 4.07 us
  starting transfers between devices: 54.6 us -> 65.6 us
  waiting for transfers between devices: 19.7 us -> 26 us
  Pallas kernels: 6.14 us -> 8.71 us
    all_to_all x1 -> x0, blocking collectives: 21.3 us -> none  [exchange(): return lax.all_to_all(a, axes, 0, 0, tiled=True)]
    all_to_all x3 -> x4, starting transfers between devices: 32.6 us -> 44.8 us  [exchange(): return lax.all_to_all(a, axes, 0, 0, tiled=True)]
    all_to_all x3 -> x4, waiting for transfers between devices: 15.3 us -> 19.8 us  [exchange(): return lax.all_to_all(a, axes, 0, 0, tiled=True)]
    pallas_call x5 -> x6, Pallas kernels: 6.14 us -> 8.71 us  [call(): pl.pallas_call(kernel, out_shape=outs, in_specs=[smem] * scalars + [vmem]...]
    ppermute x6, waiting for transfers between devices: 4.37 us -> 6.24 us  [along_x(): return lax.ppermute(a, 'x', [(i, (i + by) % heads) for i in range(heads)])]
    ppermute x6, starting transfers between devices: 22 us -> 20.8 us  [along_x(): return lax.ppermute(a, 'x', [(i, (i + by) % heads) for i in range(heads)])]
  transfers between devices with their start and end apart: 9 -> 10, of which waited for: 4 -> 6; matrix products, arithmetic and copies ran while one was open for 2% -> 2% of each run, Pallas kernels for 1% -> 4%
where the time goes in v10:
time: 114 us; the launch traced here: 112 us
  starting transfers between devices  65.6 us (58%)
  waiting for transfers between devices  26 us (23%)
  Pallas kernels  8.71 us (8%)
  local copies, waits for them, and re-layouts  6.86 us (6%)
  blocking collectives  4.07 us (4%)
    all_to_all x4, starting transfers between devices, exchange(): return lax.all_to_all(a, axes, 0, 0, tiled=True)  44.8 us
    ppermute x6, starting transfers between devices, along_x(): return lax.ppermute(a, 'x', [(i, (i + by) % heads) for i in range(heads)])  20.8 us
    all_to_all x4, waiting for transfers between devices, exchange(): return lax.all_to_all(a, axes, 0, 0, tiled=True)  19.8 us
    pallas_call x6, Pallas kernels, call(): pl.pallas_call(kernel, out_shape=outs, in_specs=[smem] * scalars + [vmem]...  8.71 us
    ppermute x6, waiting for transfers between devices, along_x(): return lax.ppermute(a, 'x', [(i, (i + by) % heads) for i in range(heads)])  6.24 us
    unnamed x13, local copies, waits for them, and re-layouts  3.61 us
  transfers between devices with their start and end apart: 10, of which 6 were waited for; matrix products, arithmetic and copies ran while one was open for 2% of the time, Pallas kernels for 4%

profile of v10, /device:TPU:1, one launch (start us, length us, event | category | flops | bytes accessed | tf_op | source)
XLA Modules:
  0.0 112.3 jit_solution(17230444262496819029)
XLA Ops:
  0.6 0.0 copy-start
  0.6 0.9 copy_bitcast_fusion.3
  1.6 0.9 pack_kv.1
  2.4 0.0 copy-start.1
  2.4 18.1 %all-to-all-start = ((bf16[24,64,128]{2,1,0:T(8,128)(2,1)}), bf16[24,64,128]{2,1,0:T(8,128)(2,1)S(1)}, u32[]{:S(2)}, u32[]{:S(2)}) async-start(bf16[24,64,128]{2,1,0:T(8,128)(2,1)} %bitcast.3), calls=%async_computation | async-start | bytes 786432 | tf_op jit(solution)/shard_map/all_to_all | solution.py:193
  20.5 0.0 copy-done.1
  20.5 0.0 copy-start.2
  20.6 0.8 copy-done.2
  21.4 0.0 copy-start.3
  21.4 0.7 copy-done.3
  22.1 0.1 pad.6.adj_ref
  22.1 0.1 pack_qg.1
  22.2 0.1 pad_add_fusion.at_ref
  22.3 2.2 %all-gather = bf16[4,64,1024]{2,1,0:T(8,128)(2,1)S(1)} all-gather(bf16[2,64,1024]{2,1,0:T(8,128)(2,1)S(1)} %pack_qg.1), channel_id=2, replica_groups=mesh['x'=4,'zh'=3,'c'=2,'y'=8,'zl'=4] {'c'}, dimensions={0}, use_global_device_ids=true | all-gather | bytes 786432 | tf_op jit(solution)/shard_map/all_gather | solution.py:215
  24.5 0.6 route.1
  25.1 4.8 %collective-permute-start = (bf16[2,64,640]{2,1,0:T(8,128)(2,1)S(1)}, bf16[2,64,640]{2,1,0:T(8,128)(2,1)S(1)}, u32[]{:S(2)}, u32[]{:S(2)}) collective-permute-start(bf16[2,64,640]{2,1,0:T(8,128)(2,1)S(1)} %get-tuple-element.31), channel_id=1, source_target_pairs={{0,384},{192,576},{384,0},{576,192},{1,385},{193,577},{385,1},{577... | collective-permute-start | bytes 491528 | tf_op jit(solution)/shard_map/ppermute | solution.py:198
  29.9 2.2 %collective-permute-start.1 = (bf16[2,64,640]{2,1,0:T(8,128)(2,1)S(1)}, bf16[2,64,640]{2,1,0:T(8,128)(2,1)S(1)}, u32[]{:S(2)}, u32[]{:S(2)}) collective-permute-start(bf16[2,64,640]{2,1,0:T(8,128)(2,1)S(1)} %get-tuple-element.32), channel_id=1, source_target_pairs={{0,192},{192,384},{384,576},{576,0},{1,193},{193,385},{385,577},{5... | collective-permute-start | bytes 491528 | tf_op jit(solution)/shard_map/ppermute | solution.py:198
  32.1 4.3 %collective-permute-start.2 = (bf16[2,64,640]{2,1,0:T(8,128)(2,1)S(1)}, bf16[2,64,640]{2,1,0:T(8,128)(2,1)S(1)}, u32[]{:S(2)}, u32[]{:S(2)}) collective-permute-start(bf16[2,64,640]{2,1,0:T(8,128)(2,1)S(1)} %get-tuple-element.33), channel_id=1, source_target_pairs={{0,576},{192,0},{384,192},{576,384},{1,577},{193,1},{385,193},{577... | collective-permute-start | bytes 491528 | tf_op jit(solution)/shard_map/ppermute | solution.py:198
  36.4 0.0 collective-permute-done.p2_ref
  36.4 2.7 %collective-permute-done.1.p1_ref = bf16[2,64,640]{2,1,0:T(8,128)(2,1)S(1)} collective-permute-done((bf16[2,64,640]{2,1,0:T(8,128)(2,1)S(1)}, bf16[2,64,640]{2,1,0:T(8,128)(2,1)S(1)}, u32[]{:S(2)}, u32[]{:S(2)}) %collective-permute-start.1) | collective-permute-done | bytes 163872 | tf_op jit(solution)/shard_map/ppermute | solution.py:198
  39.2 0.0 collective-permute-done.2.p3_ref
  39.2 0.0 all-to-all-done.kv_ref
  39.2 2.8 %weight_rows.1 = bf16[32,8,128]{2,1,0:T(8,128)(2,1)} custom-call(bf16[24,64,128]{2,1,0:T(8,128)(2,1)S(1)} %all-to-all-done.kv_ref, bf16[2,64,640]{2,1,0:T(8,128)(2,1)S(1)} %get-tuple-element.30.p0_ref, bf16[2,64,640]{2,1,0:T(8,128)(2,1)S(1)} %collective-permute-done.p2_ref, bf16[2,64,640]{2,1,0:T(8,128)(2,1)S(1)} %collective-permute-done.1.p1_ref, ...), custom_call_target="tpu_custom_call" | custom-call | tf_op jit(solution)/shard_map/weight_rows/pallas_call | solution.py:177
  42.0 12.1 %all-to-all-start.1 = ((bf16[32,8,128]{2,1,0:T(8,128)(2,1)}), bf16[32,8,128]{2,1,0:T(8,128)(2,1)S(1)}, u32[]{:S(2)}, u32[]{:S(2)}) async-start(bf16[32,8,128]{2,1,0:T(8,128)(2,1)} %weight_rows.1), calls=%async_computation.1 | async-start | bytes 131072 | tf_op jit(solution)/shard_map/all_to_all | solution.py:193
  54.1 0.0 copy-done
  54.2 4.2 %attend.1 = (bf16[24,72,128]{2,1,0:T(8,128)(2,1)}, bf16[2,4,32,128]{3,2,1,0:T(8,128)(2,1)S(1)}) custom-call(bf16[24,64,128]{2,1,0:T(8,128)(2,1)S(1)} %all-to-all-done.kv_ref, bf16[2,64,640]{2,1,0:T(8,128)(2,1)S(1)} %get-tuple-element.30.p0_ref, bf16[2,64,640]{2,1,0:T(8,128)(2,1)S(1)} %collective-permute-done.p2_ref, ...), custom_call_target="tpu_custom_call" | custom-call | tf_op jit(solution)/shard_map/attend/pallas_call | solution.py:177
  58.4 5.1 %all-to-all-done.1 = bf16[32,8,128]{2,1,0:T(8,128)(2,1)S(1)} async-done(((bf16[32,8,128]{2,1,0:T(8,128)(2,1)}), bf16[32,8,128]{2,1,0:T(8,128)(2,1)S(1)}, u32[]{:S(2)}, u32[]{:S(2)}) %all-to-all-start.1) | async-done | bytes 65568 | tf_op jit(solution)/shard_map/all_to_all | solution.py:193
  63.5 0.6 broadcast_dynamic-update-slice_fusion
  64.1 10.7 %all-to-all-start.2 = ((bf16[24,72,128]{2,1,0:T(8,128)(2,1)}), bf16[24,72,128]{2,1,0:T(8,128)(2,1)S(1)}, u32[]{:S(2)}, u32[]{:S(2)}) async-start(bf16[24,72,128]{2,1,0:T(8,128)(2,1)} %broadcast_dynamic-update-slice_fusion), calls=%async_computation.2 | async-start | bytes 884736 | tf_op jit(solution)/shard_map/all_to_all | solution.py:193
  74.9 1.9 %all-gather.1 = bf16[4,4,32,128]{3,2,1,0:T(8,128)(2,1)S(1)} all-gather(bf16[2,4,32,128]{3,2,1,0:T(8,128)(2,1)S(1)} %get-tuple-element.35), channel_id=3, replica_groups=mesh['x'=4,'zh'=3,'c'=2,'y'=8,'zl'=4] {'c'}, dimensions={0}, use_global_device_ids=true | all-gather | bytes 196608 | tf_op jit(solution)/shard_map/all_gather | solution.py:241
  76.8 4.5 %collective-permute-start.3 = (bf16[2,32,128]{2,1,0:T(8,128)(2,1)S(1)}, bf16[2,32,128]{2,1,0:T(8,128)(2,1)S(1)}, u32[]{:S(2)}, u32[]{:S(2)}) collective-permute-start(bf16[2,32,128]{2,1,0:T(8,128)(2,1)S(1)} %get-tuple-element.54), channel_id=1, source_target_pairs={{0,576},{192,0},{384,192},{576,384},{1,577},{193,1},{385,193},{577... | collective-permute-start | bytes 49160 | tf_op jit(solution)/shard_map/ppermute | solution.py:198
  81.3 2.5 %collective-permute-start.4 = (bf16[2,32,128]{2,1,0:T(8,128)(2,1)S(1)}, bf16[2,32,128]{2,1,0:T(8,128)(2,1)S(1)}, u32[]{:S(2)}, u32[]{:S(2)}) collective-permute-start(bf16[2,32,128]{2,1,0:T(8,128)(2,1)S(1)} %get-tuple-element.53), channel_id=1, source_target_pairs={{0,384},{192,576},{384,0},{576,192},{1,385},{193,577},{385,1},{577... | collective-permute-start | bytes 49160 | tf_op jit(solution)/shard_map/ppermute | solution.py:198
  83.8 2.5 %collective-permute-start.5 = (bf16[2,32,128]{2,1,0:T(8,128)(2,1)S(1)}, bf16[2,32,128]{2,1,0:T(8,128)(2,1)S(1)}, u32[]{:S(2)}, u32[]{:S(2)}) collective-permute-start(bf16[2,32,128]{2,1,0:T(8,128)(2,1)S(1)} %get-tuple-element.52), channel_id=1, source_target_pairs={{0,192},{192,384},{384,576},{576,0},{1,193},{193,385},{385,577},{5... | collective-permute-start | bytes 49160 | tf_op jit(solution)/shard_map/ppermute | solution.py:198
  86.3 0.0 collective-permute-done.3.d1_ref
  86.3 1.9 %collective-permute-done.4.d2_ref = bf16[2,32,128]{2,1,0:T(8,128)(2,1)S(1)} collective-permute-done((bf16[2,32,128]{2,1,0:T(8,128)(2,1)S(1)}, bf16[2,32,128]{2,1,0:T(8,128)(2,1)S(1)}, u32[]{:S(2)}, u32[]{:S(2)}) %collective-permute-start.4) | collective-permute-done | bytes 16416 | tf_op jit(solution)/shard_map/ppermute | solution.py:198
  88.2 1.6 %collective-permute-done.5.d3_ref = bf16[2,32,128]{2,1,0:T(8,128)(2,1)S(1)} collective-permute-done((bf16[2,32,128]{2,1,0:T(8,128)(2,1)S(1)}, bf16[2,32,128]{2,1,0:T(8,128)(2,1)S(1)}, u32[]{:S(2)}, u32[]{:S(2)}) %collective-permute-start.5) | collective-permute-done | bytes 16416 | tf_op jit(solution)/shard_map/ppermute | solution.py:198
  89.8 5.9 %all-to-all-done.2 = bf16[24,72,128]{2,1,0:T(8,128)(2,1)S(1)} async-done(((bf16[24,72,128]{2,1,0:T(8,128)(2,1)}), bf16[24,72,128]{2,1,0:T(8,128)(2,1)S(1)}, u32[]{:S(2)}, u32[]{:S(2)}) %all-to-all-start.2) | async-done | bytes 442400 | tf_op jit(solution)/shard_map/all_to_all | solution.py:193
  95.7 0.7 broadcast_in_dim.4
  96.4 3.9 %all-to-all-start.3 = ((bf16[32,4,8,128]{3,2,1,0:T(8,128)(2,1)}), bf16[32,4,8,128]{3,2,1,0:T(8,128)(2,1)S(1)}, u32[]{:S(2)}, u32[]{:S(2)}) async-start(bf16[32,4,8,128]{3,2,1,0:T(8,128)(2,1)} %broadcast_in_dim.4), calls=%async_computation.3 | async-start | bytes 524288 | tf_op jit(solution)/shard_map/all_to_all | solution.py:193
  100.3 0.1 unpack.1
  100.4 0.7 copy.24
  101.1 0.7 copy.25
  101.8 0.7 copy.26
  102.5 8.8 %all-to-all-done.3 = bf16[32,4,8,128]{3,2,1,0:T(8,128)(2,1)S(1)} async-done(((bf16[32,4,8,128]{3,2,1,0:T(8,128)(2,1)}), bf16[32,4,8,128]{3,2,1,0:T(8,128)(2,1)S(1)}, u32[]{:S(2)}, u32[]{:S(2)}) %all-to-all-start.3) | async-done | bytes 262176 | tf_op jit(solution)/shard_map/all_to_all | solution.py:193
  111.4 0.9 copy.23
  (9 shorter events, 0.2 us)
Async XLA Ops:
  0.6 53.5 %copy-start = (bf16[256,512]{1,0:T(8,128)(2,1)S(1)}, bf16[256,512]{1,0:T(8,128)(2,1)}, u32[]{:S(2)}) copy-start(bf16[256,512]{1,0:T(8,128)(2,1)} %param.12) | copy-start | bytes 786436
  2.4 18.1 %copy-start.1 = (bf16[64,2,512]{2,1,0:T(2,128)(2,1)S(1)}, bf16[64,2,512]{2,1,0:T(2,128)(2,1)}, u32[]{:S(2)}) copy-start(bf16[64,2,512]{2,1,0:T(2,128)(2,1)} %param.11) | copy-start | bytes 393220
  2.4 36.7 %all-to-all-start = ((bf16[24,64,128]{2,1,0:T(8,128)(2,1)}), bf16[24,64,128]{2,1,0:T(8,128)(2,1)S(1)}, u32[]{:S(2)}, u32[]{:S(2)}) async-start(bf16[24,64,128]{2,1,0:T(8,128)(2,1)} %bitcast.3), calls=%async_computation | async-start | bytes 786432 | tf_op jit(solution)/shard_map/all_to_all | solution.py:193
  20.5 0.8 copy-start.2
  21.4 0.7 copy-start.3
  25.1 11.3 %collective-permute-start = (bf16[2,64,640]{2,1,0:T(8,128)(2,1)S(1)}, bf16[2,64,640]{2,1,0:T(8,128)(2,1)S(1)}, u32[]{:S(2)}, u32[]{:S(2)}) collective-permute-start(bf16[2,64,640]{2,1,0:T(8,128)(2,1)S(1)} %get-tuple-element.31), channel_id=1, source_target_pairs={{0,384},{192,576},{384,0},{576,192},{1,385},{193,577},{385,1},{577... | collective-permute-start | bytes 491528 | tf_op jit(solution)/shard_map/ppermute | solution.py:198
  29.9 9.3 %collective-permute-start.1 = (bf16[2,64,640]{2,1,0:T(8,128)(2,1)S(1)}, bf16[2,64,640]{2,1,0:T(8,128)(2,1)S(1)}, u32[]{:S(2)}, u32[]{:S(2)}) collective-permute-start(bf16[2,64,640]{2,1,0:T(8,128)(2,1)S(1)} %get-tuple-element.32), channel_id=1, source_target_pairs={{0,192},{192,384},{384,576},{576,0},{1,193},{193,385},{385,577},{5... | collective-permute-start | bytes 491528 | tf_op jit(solution)/shard_map/ppermute | solution.py:198
  32.1 7.1 %collective-permute-start.2 = (bf16[2,64,640]{2,1,0:T(8,128)(2,1)S(1)}, bf16[2,64,640]{2,1,0:T(8,128)(2,1)S(1)}, u32[]{:S(2)}, u32[]{:S(2)}) collective-permute-start(bf16[2,64,640]{2,1,0:T(8,128)(2,1)S(1)} %get-tuple-element.33), channel_id=1, source_target_pairs={{0,576},{192,0},{384,192},{576,384},{1,577},{193,1},{385,193},{577... | collective-permute-start | bytes 491528 | tf_op jit(solution)/shard_map/ppermute | solution.py:198
  42.0 21.5 %all-to-all-start.1 = ((bf16[32,8,128]{2,1,0:T(8,128)(2,1)}), bf16[32,8,128]{2,1,0:T(8,128)(2,1)S(1)}, u32[]{:S(2)}, u32[]{:S(2)}) async-start(bf16[32,8,128]{2,1,0:T(8,128)(2,1)} %weight_rows.1), calls=%async_computation.1 | async-start | bytes 131072 | tf_op jit(solution)/shard_map/all_to_all | solution.py:193
  64.1 31.5 %all-to-all-start.2 = ((bf16[24,72,128]{2,1,0:T(8,128)(2,1)}), bf16[24,72,128]{2,1,0:T(8,128)(2,1)S(1)}, u32[]{:S(2)}, u32[]{:S(2)}) async-start(bf16[24,72,128]{2,1,0:T(8,128)(2,1)} %broadcast_dynamic-update-slice_fusion), calls=%async_computation.2 | async-start | bytes 884736 | tf_op jit(solution)/shard_map/all_to_all | solution.py:193
  76.8 9.5 %collective-permute-start.3 = (bf16[2,32,128]{2,1,0:T(8,128)(2,1)S(1)}, bf16[2,32,128]{2,1,0:T(8,128)(2,1)S(1)}, u32[]{:S(2)}, u32[]{:S(2)}) collective-permute-start(bf16[2,32,128]{2,1,0:T(8,128)(2,1)S(1)} %get-tuple-element.54), channel_id=1, source_target_pairs={{0,576},{192,0},{384,192},{576,384},{1,577},{193,1},{385,193},{577... | collective-permute-start | bytes 49160 | tf_op jit(solution)/shard_map/ppermute | solution.py:198
  81.3 6.8 %collective-permute-start.4 = (bf16[2,32,128]{2,1,0:T(8,128)(2,1)S(1)}, bf16[2,32,128]{2,1,0:T(8,128)(2,1)S(1)}, u32[]{:S(2)}, u32[]{:S(2)}) collective-permute-start(bf16[2,32,128]{2,1,0:T(8,128)(2,1)S(1)} %get-tuple-element.53), channel_id=1, source_target_pairs={{0,384},{192,576},{384,0},{576,192},{1,385},{193,577},{385,1},{577... | collective-permute-start | bytes 49160 | tf_op jit(solution)/shard_map/ppermute | solution.py:198
  83.8 6.0 %collective-permute-start.5 = (bf16[2,32,128]{2,1,0:T(8,128)(2,1)S(1)}, bf16[2,32,128]{2,1,0:T(8,128)(2,1)S(1)}, u32[]{:S(2)}, u32[]{:S(2)}) collective-permute-start(bf16[2,32,128]{2,1,0:T(8,128)(2,1)S(1)} %get-tuple-element.52), channel_id=1, source_target_pairs={{0,192},{192,384},{384,576},{576,0},{1,193},{193,385},{385,577},{5... | collective-permute-start | bytes 49160 | tf_op jit(solution)/shard_map/ppermute | solution.py:198
  96.4 14.9 %all-to-all-start.3 = ((bf16[32,4,8,128]{3,2,1,0:T(8,128)(2,1)}), bf16[32,4,8,128]{3,2,1,0:T(8,128)(2,1)S(1)}, u32[]{:S(2)}, u32[]{:S(2)}) async-start(bf16[32,4,8,128]{3,2,1,0:T(8,128)(2,1)} %broadcast_in_dim.4), calls=%async_computation.3 | async-start | bytes 524288 | tf_op jit(solution)/shard_map/all_to_all | solution.py:193

commit v11 on v10

--- a/solution.py
+++ b/solution.py
@@ -88,14 +88,18 @@
     lane = lax.broadcasted_iota(jnp.int32, (total, LANES), 1)
     block = lax.shift_right_logical(lax.broadcasted_iota(jnp.int32, (total, LANES), 0), 5)
     hot = jnp.where(lane - HEAD_DIM == block, 1.0, 0.0)
-    kv[...] = part
+    kv[...] = jnp.where(lane < HEAD_DIM, 1.0, part.astype(F32)).astype(BF16)
     kx[...] = jnp.where(lane < HEAD_DIM, part.astype(F32), hot).astype(BF16)
     dw = None
     for b in range(own // rows):
         mine = jnp.concatenate([parts[2 * b][...], parts[2 * b + 1][...]], axis=0)
         qx = mine[:, :, :LANES].reshape(rows, LANES)
         g = mine[:, :, LANES:].reshape(rows, -1)
-        att = dot(softmax_rows(qx, kx[...]).astype(BF16), kv[...], NN).astype(BF16)
+        s = dot(qx, kx[...], NT)
+        top = jnp.max(s, axis=1, keepdims=True)
+        e = jnp.exp2((s - top) * (0.125 * LOG2E)).astype(BF16)
+        att = dot(e, kv[...], NN)
+        att = (att * (1.0 / att[:, :1])).astype(BF16)
         part = dot(att, g, TN)
         dw = part if dw is None else dw + part
     dw = dw[HEAD_DIM:].astype(BF16)

time: 114 us -> 113 us (level)
  transfers between devices with their start and end apart: 10 -> 10, of which waited for: 6 -> 6; matrix products, arithmetic and copies ran while one was open for 2% -> 2% of each run, Pallas kernels for 4% -> 5%
where the time goes in v11:
time: 113 us; the launch traced here: 112 us
  starting transfers between devices  65.6 us (58%)
  waiting for transfers between devices  26 us (23%)
  Pallas kernels  8.3 us (7%)
  local copies, waits for them, and re-layouts  6.86 us (6%)
  blocking collectives  4.07 us (4%)
    all_to_all x4, starting transfers between devices, exchange(): return lax.all_to_all(a, axes, 0, 0, tiled=True)  44.8 us
    ppermute x6, starting transfers between devices, along_x(): return lax.ppermute(a, 'x', [(i, (i + by) % heads) for i in range(heads)])  20.8 us
    all_to_all x4, waiting for transfers between devices, exchange(): return lax.all_to_all(a, axes, 0, 0, tiled=True)  19.8 us
    pallas_call x6, Pallas kernels, call(): pl.pallas_call(kernel, out_shape=outs, in_specs=[smem] * scalars + [vmem]...  8.3 us
    ppermute x6, waiting for transfers between devices, along_x(): return lax.ppermute(a, 'x', [(i, (i + by) % heads) for i in range(heads)])  6.24 us
    unnamed x13, local copies, waits for them, and re-layouts  3.61 us
  transfers between devices with their start and end apart: 10, of which 6 were waited for; matrix products, arithmetic and copies ran while one was open for 2% of the time, Pallas kernels for 5%

profile of v11, /device:TPU:1, one launch (start us, length us, event | category | flops | bytes accessed | tf_op | source)
XLA Modules:
  0.0 111.9 jit_solution(7667778220200143864)
XLA Ops:
  0.6 0.0 copy-start
  0.6 0.9 copy_bitcast_fusion.3
  1.6 0.9 pack_kv.1
  2.4 0.0 copy-start.1
  2.4 18.1 %all-to-all-start = ((bf16[24,64,128]{2,1,0:T(8,128)(2,1)}), bf16[24,64,128]{2,1,0:T(8,128)(2,1)S(1)}, u32[]{:S(2)}, u32[]{:S(2)}) async-start(bf16[24,64,128]{2,1,0:T(8,128)(2,1)} %bitcast.3), calls=%async_computation | async-start | bytes 786432 | tf_op jit(solution)/shard_map/all_to_all | solution.py:197
  20.5 0.0 copy-done.1
  20.5 0.0 copy-start.2
  20.6 0.8 copy-done.2
  21.4 0.0 copy-start.3
  21.4 0.7 copy-done.3
  22.1 0.1 pad.6.adj_ref
  22.1 0.1 pack_qg.1
  22.2 0.1 pad_add_fusion.at_ref
  22.3 2.2 %all-gather = bf16[4,64,1024]{2,1,0:T(8,128)(2,1)S(1)} all-gather(bf16[2,64,1024]{2,1,0:T(8,128)(2,1)S(1)} %pack_qg.1), channel_id=2, replica_groups=mesh['x'=4,'zh'=3,'c'=2,'y'=8,'zl'=4] {'c'}, dimensions={0}, use_global_device_ids=true | all-gather | bytes 786432 | tf_op jit(solution)/shard_map/all_gather | solution.py:219
  24.5 0.6 route.1
  25.1 4.8 %collective-permute-start = (bf16[2,64,640]{2,1,0:T(8,128)(2,1)S(1)}, bf16[2,64,640]{2,1,0:T(8,128)(2,1)S(1)}, u32[]{:S(2)}, u32[]{:S(2)}) collective-permute-start(bf16[2,64,640]{2,1,0:T(8,128)(2,1)S(1)} %get-tuple-element.31), channel_id=1, source_target_pairs={{0,384},{192,576},{384,0},{576,192},{1,385},{193,577},{385,1},{577... | collective-permute-start | bytes 491528 | tf_op jit(solution)/shard_map/ppermute | solution.py:202
  29.9 2.2 %collective-permute-start.1 = (bf16[2,64,640]{2,1,0:T(8,128)(2,1)S(1)}, bf16[2,64,640]{2,1,0:T(8,128)(2,1)S(1)}, u32[]{:S(2)}, u32[]{:S(2)}) collective-permute-start(bf16[2,64,640]{2,1,0:T(8,128)(2,1)S(1)} %get-tuple-element.32), channel_id=1, source_target_pairs={{0,192},{192,384},{384,576},{576,0},{1,193},{193,385},{385,577},{5... | collective-permute-start | bytes 491528 | tf_op jit(solution)/shard_map/ppermute | solution.py:202
  32.1 4.3 %collective-permute-start.2 = (bf16[2,64,640]{2,1,0:T(8,128)(2,1)S(1)}, bf16[2,64,640]{2,1,0:T(8,128)(2,1)S(1)}, u32[]{:S(2)}, u32[]{:S(2)}) collective-permute-start(bf16[2,64,640]{2,1,0:T(8,128)(2,1)S(1)} %get-tuple-element.33), channel_id=1, source_target_pairs={{0,576},{192,0},{384,192},{576,384},{1,577},{193,1},{385,193},{577... | collective-permute-start | bytes 491528 | tf_op jit(solution)/shard_map/ppermute | solution.py:202
  36.4 0.0 collective-permute-done.p2_ref
  36.4 2.7 %collective-permute-done.1.p1_ref = bf16[2,64,640]{2,1,0:T(8,128)(2,1)S(1)} collective-permute-done((bf16[2,64,640]{2,1,0:T(8,128)(2,1)S(1)}, bf16[2,64,640]{2,1,0:T(8,128)(2,1)S(1)}, u32[]{:S(2)}, u32[]{:S(2)}) %collective-permute-start.1) | collective-permute-done | bytes 163872 | tf_op jit(solution)/shard_map/ppermute | solution.py:202
  39.2 0.0 collective-permute-done.2.p3_ref
  39.2 0.0 all-to-all-done.kv_ref
  39.2 2.4 %weight_rows.1 = bf16[32,8,128]{2,1,0:T(8,128)(2,1)} custom-call(bf16[24,64,128]{2,1,0:T(8,128)(2,1)S(1)} %all-to-all-done.kv_ref, bf16[2,64,640]{2,1,0:T(8,128)(2,1)S(1)} %get-tuple-element.30.p0_ref, bf16[2,64,640]{2,1,0:T(8,128)(2,1)S(1)} %collective-permute-done.p2_ref, bf16[2,64,640]{2,1,0:T(8,128)(2,1)S(1)} %collective-permute-done.1.p1_ref, ...), custom_call_target="tpu_custom_call" | custom-call | tf_op jit(solution)/shard_map/weight_rows/pallas_call | solution.py:181
  41.6 12.1 %all-to-all-start.1 = ((bf16[32,8,128]{2,1,0:T(8,128)(2,1)}), bf16[32,8,128]{2,1,0:T(8,128)(2,1)S(1)}, u32[]{:S(2)}, u32[]{:S(2)}) async-start(bf16[32,8,128]{2,1,0:T(8,128)(2,1)} %weight_rows.1), calls=%async_computation.1 | async-start | bytes 131072 | tf_op jit(solution)/shard_map/all_to_all | solution.py:197
  53.7 0.0 copy-done
  53.7 4.2 %attend.1 = (bf16[24,72,128]{2,1,0:T(8,128)(2,1)}, bf16[2,4,32,128]{3,2,1,0:T(8,128)(2,1)S(1)}) custom-call(bf16[24,64,128]{2,1,0:T(8,128)(2,1)S(1)} %all-to-all-done.kv_ref, bf16[2,64,640]{2,1,0:T(8,128)(2,1)S(1)} %get-tuple-element.30.p0_ref, bf16[2,64,640]{2,1,0:T(8,128)(2,1)S(1)} %collective-permute-done.p2_ref, ...), custom_call_target="tpu_custom_call" | custom-call | tf_op jit(solution)/shard_map/attend/pallas_call | solution.py:181
  58.0 5.1 %all-to-all-done.1 = bf16[32,8,128]{2,1,0:T(8,128)(2,1)S(1)} async-done(((bf16[32,8,128]{2,1,0:T(8,128)(2,1)}), bf16[32,8,128]{2,1,0:T(8,128)(2,1)S(1)}, u32[]{:S(2)}, u32[]{:S(2)}) %all-to-all-start.1) | async-done | bytes 65568 | tf_op jit(solution)/shard_map/all_to_all | solution.py:197
  63.1 0.6 broadcast_dynamic-update-slice_fusion
  63.7 10.7 %all-to-all-start.2 = ((bf16[24,72,128]{2,1,0:T(8,128)(2,1)}), bf16[24,72,128]{2,1,0:T(8,128)(2,1)S(1)}, u32[]{:S(2)}, u32[]{:S(2)}) async-start(bf16[24,72,128]{2,1,0:T(8,128)(2,1)} %broadcast_dynamic-update-slice_fusion), calls=%async_computation.2 | async-start | bytes 884736 | tf_op jit(solution)/shard_map/all_to_all | solution.py:197
  74.5 1.9 %all-gather.1 = bf16[4,4,32,128]{3,2,1,0:T(8,128)(2,1)S(1)} all-gather(bf16[2,4,32,128]{3,2,1,0:T(8,128)(2,1)S(1)} %get-tuple-element.35), channel_id=3, replica_groups=mesh['x'=4,'zh'=3,'c'=2,'y'=8,'zl'=4] {'c'}, dimensions={0}, use_global_device_ids=true | all-gather | bytes 196608 | tf_op jit(solution)/shard_map/all_gather | solution.py:245
  76.4 4.5 %collective-permute-start.3 = (bf16[2,32,128]{2,1,0:T(8,128)(2,1)S(1)}, bf16[2,32,128]{2,1,0:T(8,128)(2,1)S(1)}, u32[]{:S(2)}, u32[]{:S(2)}) collective-permute-start(bf16[2,32,128]{2,1,0:T(8,128)(2,1)S(1)} %get-tuple-element.54), channel_id=1, source_target_pairs={{0,576},{192,0},{384,192},{576,384},{1,577},{193,1},{385,193},{577... | collective-permute-start | bytes 49160 | tf_op jit(solution)/shard_map/ppermute | solution.py:202
  80.9 2.5 %collective-permute-start.4 = (bf16[2,32,128]{2,1,0:T(8,128)(2,1)S(1)}, bf16[2,32,128]{2,1,0:T(8,128)(2,1)S(1)}, u32[]{:S(2)}, u32[]{:S(2)}) collective-permute-start(bf16[2,32,128]{2,1,0:T(8,128)(2,1)S(1)} %get-tuple-element.53), channel_id=1, source_target_pairs={{0,384},{192,576},{384,0},{576,192},{1,385},{193,577},{385,1},{577... | collective-permute-start | bytes 49160 | tf_op jit(solution)/shard_map/ppermute | solution.py:202
  83.4 2.5 %collective-permute-start.5 = (bf16[2,32,128]{2,1,0:T(8,128)(2,1)S(1)}, bf16[2,32,128]{2,1,0:T(8,128)(2,1)S(1)}, u32[]{:S(2)}, u32[]{:S(2)}) collective-permute-start(bf16[2,32,128]{2,1,0:T(8,128)(2,1)S(1)} %get-tuple-element.52), channel_id=1, source_target_pairs={{0,192},{192,384},{384,576},{576,0},{1,193},{193,385},{385,577},{5... | collective-permute-start | bytes 49160 | tf_op jit(solution)/shard_map/ppermute | solution.py:202
  85.9 0.0 collective-permute-done.3.d1_ref
  85.9 1.9 %collective-permute-done.4.d2_ref = bf16[2,32,128]{2,1,0:T(8,128)(2,1)S(1)} collective-permute-done((bf16[2,32,128]{2,1,0:T(8,128)(2,1)S(1)}, bf16[2,32,128]{2,1,0:T(8,128)(2,1)S(1)}, u32[]{:S(2)}, u32[]{:S(2)}) %collective-permute-start.4) | collective-permute-done | bytes 16416 | tf_op jit(solution)/shard_map/ppermute | solution.py:202
  87.8 1.6 %collective-permute-done.5.d3_ref = bf16[2,32,128]{2,1,0:T(8,128)(2,1)S(1)} collective-permute-done((bf16[2,32,128]{2,1,0:T(8,128)(2,1)S(1)}, bf16[2,32,128]{2,1,0:T(8,128)(2,1)S(1)}, u32[]{:S(2)}, u32[]{:S(2)}) %collective-permute-start.5) | collective-permute-done | bytes 16416 | tf_op jit(solution)/shard_map/ppermute | solution.py:202
  89.4 5.9 %all-to-all-done.2 = bf16[24,72,128]{2,1,0:T(8,128)(2,1)S(1)} async-done(((bf16[24,72,128]{2,1,0:T(8,128)(2,1)}), bf16[24,72,128]{2,1,0:T(8,128)(2,1)S(1)}, u32[]{:S(2)}, u32[]{:S(2)}) %all-to-all-start.2) | async-done | bytes 442400 | tf_op jit(solution)/shard_map/all_to_all | solution.py:197
  95.3 0.7 broadcast_in_dim.4
  96.0 3.9 %all-to-all-start.3 = ((bf16[32,4,8,128]{3,2,1,0:T(8,128)(2,1)}), bf16[32,4,8,128]{3,2,1,0:T(8,128)(2,1)S(1)}, u32[]{:S(2)}, u32[]{:S(2)}) async-start(bf16[32,4,8,128]{3,2,1,0:T(8,128)(2,1)} %broadcast_in_dim.4), calls=%async_computation.3 | async-start | bytes 524288 | tf_op jit(solution)/shard_map/all_to_all | solution.py:197
  99.9 0.1 unpack.1
  100.0 0.7 copy.24
  100.7 0.7 copy.25
  101.4 0.7 copy.26
  102.1 8.8 %all-to-all-done.3 = bf16[32,4,8,128]{3,2,1,0:T(8,128)(2,1)S(1)} async-done(((bf16[32,4,8,128]{3,2,1,0:T(8,128)(2,1)}), bf16[32,4,8,128]{3,2,1,0:T(8,128)(2,1)S(1)}, u32[]{:S(2)}, u32[]{:S(2)}) %all-to-all-start.3) | async-done | bytes 262176 | tf_op jit(solution)/shard_map/all_to_all | solution.py:197
  111.0 0.9 copy.23
  (9 shorter events, 0.2 us)
Async XLA Ops:
  0.6 53.1 %copy-start = (bf16[256,512]{1,0:T(8,128)(2,1)S(1)}, bf16[256,512]{1,0:T(8,128)(2,1)}, u32[]{:S(2)}) copy-start(bf16[256,512]{1,0:T(8,128)(2,1)} %param.12) | copy-start | bytes 786436
  2.4 18.1 %copy-start.1 = (bf16[64,2,512]{2,1,0:T(2,128)(2,1)S(1)}, bf16[64,2,512]{2,1,0:T(2,128)(2,1)}, u32[]{:S(2)}) copy-start(bf16[64,2,512]{2,1,0:T(2,128)(2,1)} %param.11) | copy-start | bytes 393220
  2.4 36.7 %all-to-all-start = ((bf16[24,64,128]{2,1,0:T(8,128)(2,1)}), bf16[24,64,128]{2,1,0:T(8,128)(2,1)S(1)}, u32[]{:S(2)}, u32[]{:S(2)}) async-start(bf16[24,64,128]{2,1,0:T(8,128)(2,1)} %bitcast.3), calls=%async_computation | async-start | bytes 786432 | tf_op jit(solution)/shard_map/all_to_all | solution.py:197
  20.5 0.8 copy-start.2
  21.4 0.7 copy-start.3
  25.1 11.3 %collective-permute-start = (bf16[2,64,640]{2,1,0:T(8,128)(2,1)S(1)}, bf16[2,64,640]{2,1,0:T(8,128)(2,1)S(1)}, u32[]{:S(2)}, u32[]{:S(2)}) collective-permute-start(bf16[2,64,640]{2,1,0:T(8,128)(2,1)S(1)} %get-tuple-element.31), channel_id=1, source_target_pairs={{0,384},{192,576},{384,0},{576,192},{1,385},{193,577},{385,1},{577... | collective-permute-start | bytes 491528 | tf_op jit(solution)/shard_map/ppermute | solution.py:202
  29.9 9.3 %collective-permute-start.1 = (bf16[2,64,640]{2,1,0:T(8,128)(2,1)S(1)}, bf16[2,64,640]{2,1,0:T(8,128)(2,1)S(1)}, u32[]{:S(2)}, u32[]{:S(2)}) collective-permute-start(bf16[2,64,640]{2,1,0:T(8,128)(2,1)S(1)} %get-tuple-element.32), channel_id=1, source_target_pairs={{0,192},{192,384},{384,576},{576,0},{1,193},{193,385},{385,577},{5... | collective-permute-start | bytes 491528 | tf_op jit(solution)/shard_map/ppermute | solution.py:202
  32.1 7.1 %collective-permute-start.2 = (bf16[2,64,640]{2,1,0:T(8,128)(2,1)S(1)}, bf16[2,64,640]{2,1,0:T(8,128)(2,1)S(1)}, u32[]{:S(2)}, u32[]{:S(2)}) collective-permute-start(bf16[2,64,640]{2,1,0:T(8,128)(2,1)S(1)} %get-tuple-element.33), channel_id=1, source_target_pairs={{0,576},{192,0},{384,192},{576,384},{1,577},{193,1},{385,193},{577... | collective-permute-start | bytes 491528 | tf_op jit(solution)/shard_map/ppermute | solution.py:202
  41.6 21.5 %all-to-all-start.1 = ((bf16[32,8,128]{2,1,0:T(8,128)(2,1)}), bf16[32,8,128]{2,1,0:T(8,128)(2,1)S(1)}, u32[]{:S(2)}, u32[]{:S(2)}) async-start(bf16[32,8,128]{2,1,0:T(8,128)(2,1)} %weight_rows.1), calls=%async_computation.1 | async-start | bytes 131072 | tf_op jit(solution)/shard_map/all_to_all | solution.py:197
  63.7 31.5 %all-to-all-start.2 = ((bf16[24,72,128]{2,1,0:T(8,128)(2,1)}), bf16[24,72,128]{2,1,0:T(8,128)(2,1)S(1)}, u32[]{:S(2)}, u32[]{:S(2)}) async-start(bf16[24,72,128]{2,1,0:T(8,128)(2,1)} %broadcast_dynamic-update-slice_fusion), calls=%async_computation.2 | async-start | bytes 884736 | tf_op jit(solution)/shard_map/all_to_all | solution.py:197
  76.4 9.5 %collective-permute-start.3 = (bf16[2,32,128]{2,1,0:T(8,128)(2,1)S(1)}, bf16[2,32,128]{2,1,0:T(8,128)(2,1)S(1)}, u32[]{:S(2)}, u32[]{:S(2)}) collective-permute-start(bf16[2,32,128]{2,1,0:T(8,128)(2,1)S(1)} %get-tuple-element.54), channel_id=1, source_target_pairs={{0,576},{192,0},{384,192},{576,384},{1,577},{193,1},{385,193},{577... | collective-permute-start | bytes 49160 | tf_op jit(solution)/shard_map/ppermute | solution.py:202
  80.9 6.8 %collective-permute-start.4 = (bf16[2,32,128]{2,1,0:T(8,128)(2,1)S(1)}, bf16[2,32,128]{2,1,0:T(8,128)(2,1)S(1)}, u32[]{:S(2)}, u32[]{:S(2)}) collective-permute-start(bf16[2,32,128]{2,1,0:T(8,128)(2,1)S(1)} %get-tuple-element.53), channel_id=1, source_target_pairs={{0,384},{192,576},{384,0},{576,192},{1,385},{193,577},{385,1},{577... | collective-permute-start | bytes 49160 | tf_op jit(solution)/shard_map/ppermute | solution.py:202
  83.4 6.0 %collective-permute-start.5 = (bf16[2,32,128]{2,1,0:T(8,128)(2,1)S(1)}, bf16[2,32,128]{2,1,0:T(8,128)(2,1)S(1)}, u32[]{:S(2)}, u32[]{:S(2)}) collective-permute-start(bf16[2,32,128]{2,1,0:T(8,128)(2,1)S(1)} %get-tuple-element.52), channel_id=1, source_target_pairs={{0,192},{192,384},{384,576},{576,0},{1,193},{193,385},{385,577},{5... | collective-permute-start | bytes 49160 | tf_op jit(solution)/shard_map/ppermute | solution.py:202
  96.0 14.9 %all-to-all-start.3 = ((bf16[32,4,8,128]{3,2,1,0:T(8,128)(2,1)}), bf16[32,4,8,128]{3,2,1,0:T(8,128)(2,1)S(1)}, u32[]{:S(2)}, u32[]{:S(2)}) async-start(bf16[32,4,8,128]{3,2,1,0:T(8,128)(2,1)} %broadcast_in_dim.4), calls=%async_computation.3 | async-start | bytes 524288 | tf_op jit(solution)/shard_map/all_to_all | solution.py:197
